TPU v7x, 32 devices: a whole 2x2x4 slice. The times are simulated.
32 devices in a mesh: grp: 2 (over y), row: 4 (over z), col: 2 (over x), rep: 2 (over core).
Axes of the slice: x: 2, y: 2, z: 4, core: 2. Of those that a mesh axis runs over, the one named last changes fastest.
Arguments:
- h_strips: bfloat16 [64, 64, 1024], P(('grp', 'row')), parts along dimension 0, may hold values from -0.1875 to 0.1875
- h_slots: int32 [64, 16], P(('grp', 'row')), parts along dimension 0, may hold values from 0 to 23, all different within a row
- t_prev: float32 [4096, 2048], P(('grp', 'row'), ('col', 'rep')), parts along dimension 0, may hold values from -6 to 6
- t_now: float32 [4096, 2048], P(('grp', 'row'), ('col', 'rep')), parts along dimension 0, may hold values from -6 to 6
- t_mask: int32 [64, 32], P(('grp', 'row'), ('col', 'rep')), parts along dimension 0, may hold values 0 or 1
- coeffs: float32 [2], replicated, may hold values from 0.5 to 1.5
Outputs:
- t_mid: float32 [4096, 2048], P(('grp', 'row'), ('col', 'rep')), parts along dimension 0
- t_next: float32 [4096, 2048], P(('grp', 'row'), ('col', 'rep')), parts along dimension 0
- density: float32 [4096, 2048], P(('grp', 'row'), ('col', 'rep')), parts along dimension 0
There are 2 independent parts, one for each index of `grp`. A program takes and returns all parts, laid end to end along the dimension named above; an argument that names none is the same for every part. Nothing has to cross between parts.
Inputs may be any that keep to these rules, and one draw needn't show every extreme that they name: `h_slots`: in each block row the 16 values are distinct.
All inputs are finite; a program needn't handle non-finite values. No bound on the sum of `t_mask` on one device may be relied on, other than what follows from the above.
Results may differ from a plain program's by a relative error of at most 0.0037.
Values may be sent and summed in bfloat16 or wider, within the bound.
No kernel may reach another device: no remote copies, remote signals or barrier semaphores. Data moves between devices by JAX's collectives and lax.ppermute only.
A program may use at most 64 MiB of HBM per device.

v0:
```python
import functools

import jax
import jax.numpy as jnp
from jax import lax
from jax.experimental import pallas as pl
from jax.experimental.pallas import tpu as pltpu
from jax.sharding import PartitionSpec as P

LANES = 128
CHUNKS = 2
MIB = 1024 * 1024

SMEM = pl.BlockSpec(memory_space=pltpu.SMEM)
VMEM = pl.BlockSpec(memory_space=pltpu.VMEM)
ANY = pl.BlockSpec(memory_space=pl.ANY)
HBM = pl.BlockSpec(memory_space=pltpu.HBM)


def from_side(block, order, mixed):
    rows, reps = lax.axis_size("row"), lax.axis_size("rep")
    route = []
    for row in range(rows):
        for rep in range(reps):
            turn = 1 if order == (mixed and rep % 2) else -1
            source = (row - turn) % rows
            route.append((source * reps + rep, row * reps + rep))
    return lax.ppermute(block, ("row", "rep"), route)


def both_sides(block):
    return tuple(from_side(block, order, True) for order in (0, 1))


def side_columns(depth, order, mixed):
    if not mixed:
        return pl.ds(2 * depth * order, depth)
    odd = lax.axis_index("rep") % 2
    return pl.ds(pl.multiple_of(jnp.where(odd == order, 0, 2 * depth), LANES), depth)


def params(limit=32 * MIB):
    return pltpu.CompilerParams(vmem_limit_bytes=limit)


def cost(flops, moved):
    return pl.CostEstimate(flops=flops, transcendentals=0, bytes_accessed=moved)


def round_kernel(starts, now_ref, *out_refs):
    for start, out_ref in zip(starts, out_refs):
        out_ref[...] = now_ref[:, start:start + out_ref.shape[1]].astype(jnp.bfloat16)


def rounded(now, spans):
    rows = now.shape[0]
    size = rows * sum(width for _, width in spans)
    return list(pl.pallas_call(
        functools.partial(round_kernel, [start for start, _ in spans]),
        in_specs=[VMEM],
        out_specs=[VMEM] * len(spans),
        out_shape=[jax.ShapeDtypeStruct((rows, width), jnp.bfloat16) for _, width in spans],
        compiler_params=params(),
        cost_estimate=cost(size, 6 * size),
        name="round_part",
    )(now))


def band_kernel(slots_ref, strips_ref, out_ref):
    block_rows, block, slot_lanes = strips_ref.shape
    out_ref[...] = jnp.zeros_like(out_ref)
    half = lax.broadcasted_iota(jnp.int32, (block, LANES), 1) // block

    @pl.loop(0, block_rows)
    def _(row):
        at = pl.ds(pl.multiple_of(row * block, block), block)
        for pair in range(slot_lanes // LANES):
            straight = strips_ref[row, :, pair * LANES:(pair + 1) * LANES].astype(jnp.float32)
            swapped = jnp.concatenate([straight[:, block:], straight[:, :block]], axis=1)
            for side in range(2):
                target = slots_ref[row, 2 * pair + side]
                odd = target % 2
                value = jnp.where(odd == side, straight, swapped)
                value = jnp.where(half == odd, value, 0.0).astype(jnp.bfloat16)
                lanes = pl.ds(pl.multiple_of((target // 2) * LANES, LANES), LANES)
                out_ref[at, lanes] += value


def banded(h_slots, h_strips):
    block_rows, block, slot_lanes = h_strips.shape
    rows, columns = block_rows * block, 3 * block_rows * block
    return pl.pallas_call(
        band_kernel,
        in_specs=[SMEM, VMEM],
        out_specs=VMEM,
        out_shape=jax.ShapeDtypeStruct((rows, columns), jnp.bfloat16),
        compiler_params=params(),
        cost_estimate=cost(8 * rows * columns, 2 * rows * (columns + slot_lanes)),
        name="band",
    )(h_slots, h_strips)


def product(band_ref, here_ref, first_ref, second_ref=None, mixed=True):
    depth = here_ref.shape[0]
    total = jnp.dot(band_ref[:, depth:2 * depth], here_ref[...], preferred_element_type=jnp.float32)
    total += jnp.dot(band_ref[:, side_columns(depth, 0, mixed)], first_ref[...], preferred_element_type=jnp.float32)
    if second_ref is not None:
        total += jnp.dot(band_ref[:, side_columns(depth, 1, mixed)], second_ref[...], preferred_element_type=jnp.float32)
    return total


def kept(mask_ref, block_row, first, block, width):
    column = lax.broadcasted_iota(jnp.int32, (block, width), 1) // block
    row = jnp.zeros((block, width), jnp.int32)
    for c in range(width // block):
        row = jnp.where(column == c, mask_ref[block_row, first + c], row)
    return row != 0


def masked(start, mask_ref, term):
    rows, width = term.shape
    block = rows // mask_ref.shape[0]
    for i in range(rows // block):
        at = slice(i * block, (i + 1) * block)
        yield at, jnp.where(kept(mask_ref, i, start // block, block, width), term[at], 0.0)


def start_writes(jobs, sems, first):
    copies = []
    for held, out_ref, at, column in jobs:
        copies.append(pltpu.make_async_copy(
            held.at[at, :], out_ref.at[at, pl.ds(column, held.shape[1])], sems.at[first + len(copies)]))
        copies[-1].start()
    return copies


def mid_kernel(start, pieces, mask_ref, band_ref, here_ref, second_ref, first_ref, prev_ref, *rest):
    mid_ref, round_refs = rest[-len(pieces) - 1], rest[-len(pieces):]
    total = product(band_ref, here_ref, first_ref, second_ref)
    term = 2.0 * total - prev_ref[:, start:start + here_ref.shape[1]]
    for at, value in masked(start, mask_ref, term):
        mid_ref[at, :] = value
        low = value.astype(jnp.bfloat16)
        for (column, size), round_ref in zip(pieces, round_refs):
            round_ref[at, :] = low[:, column:column + size]


def mid_part(span, pieces, mask, band, here, first, second, prev, after):
    rows, width = here.shape
    return pl.pallas_call(
        functools.partial(mid_kernel, span[0], pieces),
        in_specs=[SMEM] + [VMEM] * 5 + [ANY] * len(after),
        out_specs=[VMEM] * (1 + len(pieces)),
        out_shape=[jax.ShapeDtypeStruct(here.shape, jnp.float32)]
        + [jax.ShapeDtypeStruct((rows, size), jnp.bfloat16) for _, size in pieces],
        compiler_params=params(),
        cost_estimate=cost(6 * rows * rows * width, 6 * rows * rows + 16 * rows * width),
        name="mid_part",
    )(mask, band, here, second, first, prev, *after)


def next_kernel(mask_ref, coeffs_ref, band_ref, here_ref, second_ref, first_ref, now_ref, mid_ref, other_mid_ref,
                t_mid_ref, next_ref, density_ref, token_ref, held_next, held_density, sems):
    rows, width = here_ref.shape
    block = rows // mask_ref.shape[0]
    everything = pl.ds(0, rows)
    token_ref[...] = jnp.zeros_like(token_ref)
    copies = start_writes(
        [(mid_ref, t_mid_ref, everything, 0), (other_mid_ref, t_mid_ref, everything, width)], sems, 0)
    term = 2.0 * product(band_ref, here_ref, first_ref, second_ref) - now_ref[:, :width]
    for at, value in masked(0, mask_ref, term):
        held_next[at, :] = value
        held_density[at, :] = coeffs_ref[0] * mid_ref[at, :] + coeffs_ref[1] * value
    copies += start_writes(
        [(held_next, next_ref, everything, 0), (held_density, density_ref, everything, 0)], sems, len(copies))
    for copy in copies:
        copy.wait()


def next_part(mask, coeffs, band, here, first, second, now, mids):
    rows, width = here.shape
    return pl.pallas_call(
        next_kernel,
        in_specs=[SMEM] * 2 + [VMEM] * 7,
        out_specs=[HBM] * 3 + [VMEM],
        out_shape=[jax.ShapeDtypeStruct(now.shape, jnp.float32)] * 3 + [jax.ShapeDtypeStruct((8, LANES), jnp.float32)],
        scratch_shapes=[pltpu.VMEM(here.shape, jnp.float32)] * 2 + [pltpu.SemaphoreType.DMA((4,))],
        compiler_params=params(),
        cost_estimate=cost(6 * rows * rows * width, 6 * rows * rows + 30 * rows * width),
        name="next_part",
    )(mask, coeffs, band, here, second, first, now, *mids)


def begun_kernel(start, band_ref, here_ref, first_ref, now_ref, *rest):
    sums_ref = rest[-1]
    sums_ref[...] = 2.0 * product(band_ref, here_ref, first_ref, mixed=False) - now_ref[:, start:start + here_ref.shape[1]]


def begun_part(span, band, here, first, now, after):
    rows, width = here.shape
    return pl.pallas_call(
        functools.partial(begun_kernel, span[0]),
        in_specs=[VMEM] * 4 + [ANY] * len(after),
        out_specs=VMEM,
        out_shape=jax.ShapeDtypeStruct(here.shape, jnp.float32),
        compiler_params=params(),
        cost_estimate=cost(4 * rows * rows * width, 4 * rows * rows + 12 * rows * width),
        name="begun_part",
    )(band, here, first, now, *after)


def last_kernel(begin, column, mask_ref, coeffs_ref, band_ref, second_ref, sums_ref, mid_ref, *rest):
    next_ref, density_ref, held_next, held_density, sems = rest[-5:]
    rows, width = second_ref.shape
    block = rows // mask_ref.shape[0]
    step = rows // CHUNKS
    inside = slice(column, column + width)
    copies = []
    for c in range(CHUNKS):
        total = jnp.dot(
            band_ref[c * step:(c + 1) * step, side_columns(rows, 1, False)], second_ref[...],
            preferred_element_type=jnp.float32)
        for i in range(step // block):
            at = slice(c * step + i * block, c * step + (i + 1) * block)
            keep = kept(mask_ref, c * (step // block) + i, (begin + column) // block, block, width)
            value = jnp.where(keep, 2.0 * total[i * block:(i + 1) * block] + sums_ref[at, inside], 0.0)
            held_next[at, :] = value
            held_density[at, :] = coeffs_ref[0] * mid_ref[at, inside] + coeffs_ref[1] * value
        done = pl.ds(c * step, step)
        copies += start_writes(
            [(held_next, next_ref, done, begin + column), (held_density, density_ref, done, begin + column)],
            sems, len(copies))
    for copy in copies:
        copy.wait()


def last_part(begin, column, mask, coeffs, band, second, sums, mid, outs):
    rows, width = second.shape
    return pl.pallas_call(
        functools.partial(last_kernel, begin, column),
        in_specs=[SMEM] * 2 + [VMEM] * 4 + [HBM] * 2,
        out_specs=[HBM] * 2,
        out_shape=[jax.ShapeDtypeStruct(out.shape, jnp.float32) for out in outs],
        scratch_shapes=[pltpu.VMEM((rows, width), jnp.float32)] * 2 + [pltpu.SemaphoreType.DMA((2 * CHUNKS,))],
        input_output_aliases={6: 0, 7: 1},
        compiler_params=params(),
        cost_estimate=cost(2 * rows * rows * width, 2 * rows * rows + 22 * rows * width),
        name="last_part",
    )(mask, coeffs, band, second, sums, mid, *outs)


def local(h_strips, h_slots, t_prev, t_now, t_mask, coeffs):
    width = t_now.shape[1] // 2
    low = t_now[:, :width].astype(jnp.bfloat16)
    low, t_now, t_prev, h_strips = lax.optimization_barrier((low, t_now, t_prev, h_strips))
    (high,) = rounded(t_now, [(width, width)])
    band = banded(h_slots, h_strips)
    low_sides, high_sides = both_sides(low), both_sides(high)
    mid_low, low_again = mid_part((0, width), [(0, width)], t_mask, band, low, *low_sides, t_prev, [])
    low_sides = both_sides(low_again)
    pieces = [(column, width // 2) for column in (0, width // 2)]
    mid_high, high_again, *cuts = mid_part(
        (width, width), [(0, width)] + pieces, t_mask, band, high, *high_sides, t_prev, [mid_low])
    first = from_side(high_again, 0, False)
    seconds = [from_side(cut, 1, False) for cut in cuts]
    t_mid, *outs, token = next_part(t_mask, coeffs, band, low_again, *low_sides, t_now, [mid_low, mid_high])
    sums = begun_part((width, width), band, high_again, first, t_now, [token])
    for (column, _), second in zip(pieces, seconds):
        outs = last_part(width, column, t_mask, coeffs, band, second, sums, mid_high, outs)
    return (t_mid, outs[0], outs[1])


def solution(mesh):
    panel = P(("grp", "row"), ("col", "rep"))
    return jax.shard_map(
        local,
        mesh=mesh,
        in_specs=(P(("grp", "row"), None, None), P(("grp", "row"), None), panel, panel, panel, P()),
        out_specs=(panel, panel, panel),
        check_vma=False,
    )
```

profile of v0, /device:TPU:0, one launch (start us, length us, event | category | flops | bytes accessed | tf_op | source)
XLA Modules:
  0.0 52.1 jit_solution(14328994962952473692)
XLA Ops:
  0.6 0.0 copy-start.6
  0.6 1.1 %slice.7.here_ref = bf16[512,256]{1,0:T(8,128)(2,1)S(1)} slice(f32[512,512]{1,0:T(8,128)} %now_ref.2), slice={[0:512], [0:256]} | slice | bytes 524288 | tf_op jit(solution)/shard_map/slice | solution.py:254
  1.7 3.1 %collective-permute-start.1 = (bf16[512,256]{1,0:T(8,128)(2,1)S(1)}, bf16[512,256]{1,0:T(8,128)(2,1)S(1)}, u32[]{:S(2)}, u32[]{:S(2)}) collective-permute-start(bf16[512,256]{1,0:T(8,128)(2,1)S(1)} %slice.7.here_ref), channel_id=1, source_target_pairs={{12,0},{5,1},{0,4},{9,5},{4,8},{13,9},{8,12},{1,13},{14,2},{7,3},{... | collective-permute-start | bytes 786440 | tf_op jit(solution)/shard_map/ppermute | solution.py:28
  4.8 2.1 %collective-permute-start = (bf16[512,256]{1,0:T(8,128)(2,1)S(1)}, bf16[512,256]{1,0:T(8,128)(2,1)S(1)}, u32[]{:S(2)}, u32[]{:S(2)}) collective-permute-start(bf16[512,256]{1,0:T(8,128)(2,1)S(1)} %slice.7.here_ref), channel_id=1, source_target_pairs={{4,0},{13,1},{8,4},{1,5},{12,8},{5,9},{0,12},{9,13},{6,2},{15,3},{... | collective-permute-start | bytes 786440 | tf_op jit(solution)/shard_map/ppermute | solution.py:28
  6.9 0.0 copy-start
  6.9 1.2 %copy-done = f32[512,512]{1,0:T(8,128)S(1)} copy-done((f32[512,512]{1,0:T(8,128)S(1)}, f32[512,512]{1,0:T(8,128)}, u32[]{:S(2)}) %copy-start) | copy-done | bytes 1048600
  8.1 0.0 copy-start.3
  8.2 0.0 copy-start.2
  8.2 0.0 copy-start.4
  8.2 0.1 collective-permute-start.5
  8.2 3.8 %collective-permute-start.4 = (bf16[512,256]{1,0:T(8,128)(2,1)S(1)}, bf16[512,256]{1,0:T(8,128)(2,1)S(1)}, u32[]{:S(2)}, u32[]{:S(2)}) collective-permute-start(bf16[512,256]{1,0:T(8,128)(2,1)S(1)} %round_part.1.here_ref), channel_id=1, source_target_pairs={{4,0},{13,1},{8,4},{1,5},{12,8},{5,9},{0,12},{9,13},{6,2},{15,3},{... | collective-permute-start | bytes 786440 | tf_op jit(solution)/shard_map/ppermute | solution.py:28
  12.1 0.0 copy-done.6
  12.1 0.0 copy-done.3
  12.1 2.2 %band.1.band_ref = bf16[512,1536]{1,0:T(8,128)(2,1)S(1)} custom-call(s32[8,16]{1,0:T(8,128)S(1)} %copy-done.6, bf16[8,64,1024]{2,1,0:T(8,128)(2,1)S(1)} %copy-done.3), custom_call_target="tpu_custom_call" | custom-call | flops 6291456 | bytes 2621440 | tf_op jit(solution)/shard_map/band/pallas_call | solution.py:92
  14.2 0.0 collective-permute-done.1.first_ref
  14.2 4.3 %collective-permute-done.second_ref = bf16[512,256]{1,0:T(8,128)(2,1)S(1)} collective-permute-done((bf16[512,256]{1,0:T(8,128)(2,1)S(1)}, bf16[512,256]{1,0:T(8,128)(2,1)S(1)}, u32[]{:S(2)}, u32[]{:S(2)}) %collective-permute-start) | collective-permute-done | bytes 262176 | tf_op jit(solution)/shard_map/ppermute | solution.py:28
  18.6 0.0 copy-done.2
  18.6 0.0 copy-done.4
  18.6 1.2 %mid_part.2 = (f32[512,256]{1,0:T(8,128)S(1)}, bf16[512,256]{1,0:T(8,128)(2,1)S(1)}) custom-call(s32[8,8]{1,0:T(8,128)S(1)} %copy-done.4, bf16[512,1536]{1,0:T(8,128)(2,1)S(1)} %band.1.band_ref, bf16[512,256]{1,0:T(8,128)(2,1)S(1)} %slice.7.here_ref, bf16[512,256]{1,0:T(8,128)(2,1)S(1)} %collective-permute-done.second_ref, ...), custom_call_target="tpu_custom_call" | custom-call | flops 402653184 | bytes 3670016 | tf_op jit(solution)/shard_map/mid_part/pallas_call | solution.py:150
  19.7 2.8 %collective-permute-start.3 = (bf16[512,256]{1,0:T(8,128)(2,1)S(1)}, bf16[512,256]{1,0:T(8,128)(2,1)S(1)}, u32[]{:S(2)}, u32[]{:S(2)}) collective-permute-start(bf16[512,256]{1,0:T(8,128)(2,1)S(1)} %get-tuple-element.24.here_ref), channel_id=1, source_target_pairs={{12,0},{5,1},{0,4},{9,5},{4,8},{13,9},{8,12},{1,13},{14,2},{7,3},{... | collective-permute-start | bytes 786440 | tf_op jit(solution)/shard_map/ppermute | solution.py:28
  22.5 1.1 %collective-permute-start.2 = (bf16[512,256]{1,0:T(8,128)(2,1)S(1)}, bf16[512,256]{1,0:T(8,128)(2,1)S(1)}, u32[]{:S(2)}, u32[]{:S(2)}) collective-permute-start(bf16[512,256]{1,0:T(8,128)(2,1)S(1)} %get-tuple-element.24.here_ref), channel_id=1, source_target_pairs={{4,0},{13,1},{8,4},{1,5},{12,8},{5,9},{0,12},{9,13},{6,2},{15,3},{... | collective-permute-start | bytes 786440 | tf_op jit(solution)/shard_map/ppermute | solution.py:28
  23.6 1.7 %collective-permute-done.5.first_ref = bf16[512,256]{1,0:T(8,128)(2,1)S(1)} collective-permute-done((bf16[512,256]{1,0:T(8,128)(2,1)S(1)}, bf16[512,256]{1,0:T(8,128)(2,1)S(1)}, u32[]{:S(2)}, u32[]{:S(2)}) %collective-permute-start.5) | collective-permute-done | bytes 262176 | tf_op jit(solution)/shard_map/ppermute | solution.py:28
  25.3 3.6 %collective-permute-done.4.second_ref = bf16[512,256]{1,0:T(8,128)(2,1)S(1)} collective-permute-done((bf16[512,256]{1,0:T(8,128)(2,1)S(1)}, bf16[512,256]{1,0:T(8,128)(2,1)S(1)}, u32[]{:S(2)}, u32[]{:S(2)}) %collective-permute-start.4) | collective-permute-done | bytes 262176 | tf_op jit(solution)/shard_map/ppermute | solution.py:28
  28.9 0.0 copy-start.1
  28.9 0.0 copy-start.5
  28.9 1.2 %mid_part.3 = (f32[512,256]{1,0:T(8,128)S(1)}, bf16[512,256]{1,0:T(8,128)(2,1)S(1)}, bf16[512,128]{1,0:T(8,128)(2,1)S(1)}, bf16[512,128]{1,0:T(8,128)(2,1)S(1)}) custom-call(s32[8,8]{1,0:T(8,128)S(1)} %copy-done.4, bf16[512,1536]{1,0:T(8,128)(2,1)S(1)} %band.1.band_ref, bf16[512,256]{1,0:T(8,128)(2,1)S(1)} %round_part.1.here_ref, ...), custom_call_target="tpu_custom_call" | custom-call | flops 402653184 | bytes 3670016 | tf_op jit(solution)/shard_map/mid_part/pallas_call | solution.py:150
  30.1 2.6 %collective-permute-start.7 = (bf16[512,256]{1,0:T(8,128)(2,1)S(1)}, bf16[512,256]{1,0:T(8,128)(2,1)S(1)}, u32[]{:S(2)}, u32[]{:S(2)}) collective-permute-start(bf16[512,256]{1,0:T(8,128)(2,1)S(1)} %get-tuple-element.30.here_ref), channel_id=1, source_target_pairs={{12,0},{13,1},{0,4},{1,5},{4,8},{5,9},{8,12},{9,13},{14,2},{15,3},... | collective-permute-start | bytes 786440 | tf_op jit(solution)/shard_map/ppermute | solution.py:28
  32.7 1.5 %collective-permute-start.8 = (bf16[512,128]{1,0:T(8,128)(2,1)S(1)}, bf16[512,128]{1,0:T(8,128)(2,1)S(1)}, u32[]{:S(2)}, u32[]{:S(2)}) collective-permute-start(bf16[512,128]{1,0:T(8,128)(2,1)S(1)} %get-tuple-element.32), channel_id=1, source_target_pairs={{4,0},{5,1},{8,4},{9,5},{12,8},{13,9},{0,12},{1,13},{6,2},{7,3},{1... | collective-permute-start | bytes 393224 | tf_op jit(solution)/shard_map/ppermute | solution.py:28
  34.2 2.0 %collective-permute-start.6 = (bf16[512,128]{1,0:T(8,128)(2,1)S(1)}, bf16[512,128]{1,0:T(8,128)(2,1)S(1)}, u32[]{:S(2)}, u32[]{:S(2)}) collective-permute-start(bf16[512,128]{1,0:T(8,128)(2,1)S(1)} %get-tuple-element.29), channel_id=1, source_target_pairs={{4,0},{5,1},{8,4},{9,5},{12,8},{13,9},{0,12},{1,13},{6,2},{7,3},{1... | collective-permute-start | bytes 393224 | tf_op jit(solution)/shard_map/ppermute | solution.py:28
  36.1 0.5 collective-permute-done.3.first_ref
  36.6 2.2 %collective-permute-done.2.second_ref = bf16[512,256]{1,0:T(8,128)(2,1)S(1)} collective-permute-done((bf16[512,256]{1,0:T(8,128)(2,1)S(1)}, bf16[512,256]{1,0:T(8,128)(2,1)S(1)}, u32[]{:S(2)}, u32[]{:S(2)}) %collective-permute-start.2) | collective-permute-done | bytes 262176 | tf_op jit(solution)/shard_map/ppermute | solution.py:28
  38.8 0.0 copy-done.1
  38.8 0.0 copy-done.5
  38.8 2.4 %next_part.1 = (f32[512,512]{1,0:T(8,128)}, f32[512,512]{1,0:T(8,128)}, f32[512,512]{1,0:T(8,128)}, f32[8,128]{1,0:T(8,128)S(1)}) custom-call(s32[8,8]{1,0:T(8,128)S(1)} %copy-done.4, f32[2]{0:T(128)S(1)} %copy-done.5, bf16[512,1536]{1,0:T(8,128)(2,1)S(1)} %band.1.band_ref, bf16[512,256]{1,0:T(8,128)(2,1)S(1)} %get-tuple-element.24.here_ref, ...), custom_call_target="tpu_custom_call" | custom-call | flops 402653184 | bytes 5505024 | tf_op jit(solution)/shard_map/next_part/pallas_call | solution.py:182
  41.3 6.5 %collective-permute-done.7.first_ref = bf16[512,256]{1,0:T(8,128)(2,1)S(1)} collective-permute-done((bf16[512,256]{1,0:T(8,128)(2,1)S(1)}, bf16[512,256]{1,0:T(8,128)(2,1)S(1)}, u32[]{:S(2)}, u32[]{:S(2)}) %collective-permute-start.7) | collective-permute-done | bytes 262176 | tf_op jit(solution)/shard_map/ppermute | solution.py:28
  47.7 0.4 begun_part.1.sums_ref
  48.2 0.0 collective-permute-done.8.second_ref
  48.2 1.6 %last_part.2 = (f32[512,512]{1,0:T(8,128)}, f32[512,512]{1,0:T(8,128)}) custom-call(s32[8,8]{1,0:T(8,128)S(1)} %copy-done.4, f32[2]{0:T(128)S(1)} %copy-done.5, bf16[512,1536]{1,0:T(8,128)(2,1)S(1)} %band.1.band_ref, bf16[512,128]{1,0:T(8,128)(2,1)S(1)} %collective-permute-done.8.second_ref, ...), custom_call_target="tpu_custom_call", output_to_operand_aliasing={{0}: (6, {}), {1}: (7, {})} | custom-call | flops 67108864 | bytes 1966080 | tf_op jit(solution)/shard_map/last_part/pallas_call | solution.py:239
  49.9 0.6 %collective-permute-done.6.second_ref = bf16[512,128]{1,0:T(8,128)(2,1)S(1)} collective-permute-done((bf16[512,128]{1,0:T(8,128)(2,1)S(1)}, bf16[512,128]{1,0:T(8,128)(2,1)S(1)}, u32[]{:S(2)}, u32[]{:S(2)}) %collective-permute-start.6) | collective-permute-done | bytes 131104 | tf_op jit(solution)/shard_map/ppermute | solution.py:28
  50.5 1.6 %last_part.3 = (f32[512,512]{1,0:T(8,128)}, f32[512,512]{1,0:T(8,128)}) custom-call(s32[8,8]{1,0:T(8,128)S(1)} %copy-done.4, f32[2]{0:T(128)S(1)} %copy-done.5, bf16[512,1536]{1,0:T(8,128)(2,1)S(1)} %band.1.band_ref, bf16[512,128]{1,0:T(8,128)(2,1)S(1)} %collective-permute-done.6.second_ref, ...), custom_call_target="tpu_custom_call", output_to_operand_aliasing={{0}: (6, {}), {1}: (7, {})} | custom-call | flops 67108864 | bytes 1966080 | tf_op jit(solution)/shard_map/last_part/pallas_call | solution.py:239
  (1 shorter events, 0.0 us)
Async XLA Ops:
  0.6 11.4 %copy-start.6 = (s32[8,16]{1,0:T(8,128)S(1)}, s32[8,16]{1,0:T(8,128)}, u32[]{:S(2)}) copy-start(s32[8,16]{1,0:T(8,128)} %slots_ref.1) | copy-start | bytes 1540
  1.7 12.5 %collective-permute-start.1 = (bf16[512,256]{1,0:T(8,128)(2,1)S(1)}, bf16[512,256]{1,0:T(8,128)(2,1)S(1)}, u32[]{:S(2)}, u32[]{:S(2)}) collective-permute-start(bf16[512,256]{1,0:T(8,128)(2,1)S(1)} %slice.7.here_ref), channel_id=1, source_target_pairs={{12,0},{5,1},{0,4},{9,5},{4,8},{13,9},{8,12},{1,13},{14,2},{7,3},{... | collective-permute-start | bytes 786440 | tf_op jit(solution)/shard_map/ppermute | solution.py:28
  4.8 13.8 %collective-permute-start = (bf16[512,256]{1,0:T(8,128)(2,1)S(1)}, bf16[512,256]{1,0:T(8,128)(2,1)S(1)}, u32[]{:S(2)}, u32[]{:S(2)}) collective-permute-start(bf16[512,256]{1,0:T(8,128)(2,1)S(1)} %slice.7.here_ref), channel_id=1, source_target_pairs={{4,0},{13,1},{8,4},{1,5},{12,8},{5,9},{0,12},{9,13},{6,2},{15,3},{... | collective-permute-start | bytes 786440 | tf_op jit(solution)/shard_map/ppermute | solution.py:28
  6.9 1.2 %copy-start = (f32[512,512]{1,0:T(8,128)S(1)}, f32[512,512]{1,0:T(8,128)}, u32[]{:S(2)}) copy-start(f32[512,512]{1,0:T(8,128)} %now_ref.2) | copy-start | bytes 3145732
  8.1 3.9 %copy-start.3 = (bf16[8,64,1024]{2,1,0:T(8,128)(2,1)S(1)}, bf16[8,64,1024]{2,1,0:T(8,128)(2,1)}, u32[]{:S(2)}) copy-start(bf16[8,64,1024]{2,1,0:T(8,128)(2,1)} %strips_ref) | copy-start | bytes 3145732
  8.2 10.4 %copy-start.2 = (f32[512,512]{1,0:T(8,128)S(1)}, f32[512,512]{1,0:T(8,128)}, u32[]{:S(2)}) copy-start(f32[512,512]{1,0:T(8,128)} %prev_ref.1) | copy-start | bytes 3145732
  8.2 10.4 %copy-start.4 = (s32[8,8]{1,0:T(8,128)S(1)}, s32[8,8]{1,0:T(8,128)}, u32[]{:S(2)}) copy-start(s32[8,8]{1,0:T(8,128)} %mask_ref.9) | copy-start | bytes 772
  8.2 17.1 %collective-permute-start.5 = (bf16[512,256]{1,0:T(8,128)(2,1)S(1)}, bf16[512,256]{1,0:T(8,128)(2,1)S(1)}, u32[]{:S(2)}, u32[]{:S(2)}) collective-permute-start(bf16[512,256]{1,0:T(8,128)(2,1)S(1)} %round_part.1.here_ref), channel_id=1, source_target_pairs={{12,0},{5,1},{0,4},{9,5},{4,8},{13,9},{8,12},{1,13},{14,2},{7,3},{... | collective-permute-start | bytes 786440 | tf_op jit(solution)/shard_map/ppermute | solution.py:28
  8.2 20.7 %collective-permute-start.4 = (bf16[512,256]{1,0:T(8,128)(2,1)S(1)}, bf16[512,256]{1,0:T(8,128)(2,1)S(1)}, u32[]{:S(2)}, u32[]{:S(2)}) collective-permute-start(bf16[512,256]{1,0:T(8,128)(2,1)S(1)} %round_part.1.here_ref), channel_id=1, source_target_pairs={{4,0},{13,1},{8,4},{1,5},{12,8},{5,9},{0,12},{9,13},{6,2},{15,3},{... | collective-permute-start | bytes 786440 | tf_op jit(solution)/shard_map/ppermute | solution.py:28
  19.7 16.9 %collective-permute-start.3 = (bf16[512,256]{1,0:T(8,128)(2,1)S(1)}, bf16[512,256]{1,0:T(8,128)(2,1)S(1)}, u32[]{:S(2)}, u32[]{:S(2)}) collective-permute-start(bf16[512,256]{1,0:T(8,128)(2,1)S(1)} %get-tuple-element.24.here_ref), channel_id=1, source_target_pairs={{12,0},{5,1},{0,4},{9,5},{4,8},{13,9},{8,12},{1,13},{14,2},{7,3},{... | collective-permute-start | bytes 786440 | tf_op jit(solution)/shard_map/ppermute | solution.py:28
  22.5 16.3 %collective-permute-start.2 = (bf16[512,256]{1,0:T(8,128)(2,1)S(1)}, bf16[512,256]{1,0:T(8,128)(2,1)S(1)}, u32[]{:S(2)}, u32[]{:S(2)}) collective-permute-start(bf16[512,256]{1,0:T(8,128)(2,1)S(1)} %get-tuple-element.24.here_ref), channel_id=1, source_target_pairs={{4,0},{13,1},{8,4},{1,5},{12,8},{5,9},{0,12},{9,13},{6,2},{15,3},{... | collective-permute-start | bytes 786440 | tf_op jit(solution)/shard_map/ppermute | solution.py:28
  28.9 9.9 %copy-start.1 = (f32[512,512]{1,0:T(8,128)S(1)}, f32[512,512]{1,0:T(8,128)}, u32[]{:S(2)}) copy-start(f32[512,512]{1,0:T(8,128)} %now_ref.2) | copy-start | bytes 3145732
  28.9 9.9 %copy-start.5 = (f32[2]{0:T(128)S(1)}, f32[2]{0:T(128)}, u32[]{:S(2)}) copy-start(f32[2]{0:T(128)} %coeffs_ref.5) | copy-start | bytes 28
  30.1 17.6 %collective-permute-start.7 = (bf16[512,256]{1,0:T(8,128)(2,1)S(1)}, bf16[512,256]{1,0:T(8,128)(2,1)S(1)}, u32[]{:S(2)}, u32[]{:S(2)}) collective-permute-start(bf16[512,256]{1,0:T(8,128)(2,1)S(1)} %get-tuple-element.30.here_ref), channel_id=1, source_target_pairs={{12,0},{13,1},{0,4},{1,5},{4,8},{5,9},{8,12},{9,13},{14,2},{15,3},... | collective-permute-start | bytes 786440 | tf_op jit(solution)/shard_map/ppermute | solution.py:28
  32.7 15.5 %collective-permute-start.8 = (bf16[512,128]{1,0:T(8,128)(2,1)S(1)}, bf16[512,128]{1,0:T(8,128)(2,1)S(1)}, u32[]{:S(2)}, u32[]{:S(2)}) collective-permute-start(bf16[512,128]{1,0:T(8,128)(2,1)S(1)} %get-tuple-element.32), channel_id=1, source_target_pairs={{4,0},{5,1},{8,4},{9,5},{12,8},{13,9},{0,12},{1,13},{6,2},{7,3},{1... | collective-permute-start | bytes 393224 | tf_op jit(solution)/shard_map/ppermute | solution.py:28
  34.2 16.3 %collective-permute-start.6 = (bf16[512,128]{1,0:T(8,128)(2,1)S(1)}, bf16[512,128]{1,0:T(8,128)(2,1)S(1)}, u32[]{:S(2)}, u32[]{:S(2)}) collective-permute-start(bf16[512,128]{1,0:T(8,128)(2,1)S(1)} %get-tuple-element.29), channel_id=1, source_target_pairs={{4,0},{5,1},{8,4},{9,5},{12,8},{13,9},{0,12},{1,13},{6,2},{7,3},{1... | collective-permute-start | bytes 393224 | tf_op jit(solution)/shard_map/ppermute | solution.py:28
where the time goes:
time: 52.4 us; the launch traced here: 52.1 us
  waiting for transfers between devices  19.4 us (37%)
  starting transfers between devices  18.9 us (36%)
  Pallas kernels  10.7 us (20%)
  local copies, waits for them, and re-layouts  2.33 us (4%)
  between operations  0.74 us (1%)
    ppermute x9, waiting for transfers between devices, from_side(): return lax.ppermute(block, ('row', 'rep'), route)  19.4 us
    ppermute x9, starting transfers between devices, from_side(): return lax.ppermute(block, ('row', 'rep'), route)  18.9 us
    pallas_call x2, Pallas kernels, last_part(): pl.pallas_call(functools.partial(last_kernel, begin, column), in_specs=[S...  3.28 us
    pallas_call x1, Pallas kernels, next_part(): pl.pallas_call(next_kernel, in_specs=[SMEM] * 2 + [VMEM] * 7, out_specs=[...  2.44 us
    pallas_call x2, Pallas kernels, mid_part(): pl.pallas_call(functools.partial(mid_kernel, span[0], pieces), in_specs=[...  2.35 us
    pallas_call x1, Pallas kernels, banded(): pl.pallas_call(band_kernel, in_specs=[SMEM, VMEM], out_specs=VMEM, out_sh...  2.17 us
    unnamed x14, local copies, waits for them, and re-layouts  1.25 us
    slice x1, local copies, waits for them, and re-layouts, local(): low = t_now[:, :width].astype(jnp.bfloat16)  1.07 us
  transfers between devices with their start and end apart: 9, of which 7 were waited for; matrix products, arithmetic and copies ran while one was open for 0% of the time, Pallas kernels for 17%

commit v1 on v0

--- a/solution.py
+++ b/solution.py
@@ -167,7 +167,7 @@
     token_ref[...] = jnp.zeros_like(token_ref)
     copies = start_writes(
         [(mid_ref, t_mid_ref, everything, 0), (other_mid_ref, t_mid_ref, everything, width)], sems, 0)
-    term = 2.0 * product(band_ref, here_ref, first_ref, second_ref) - now_ref[:, :width]
+    term = 2.0 * product(band_ref, here_ref, first_ref, second_ref, mixed=False) - now_ref[:, :width]
     for at, value in masked(0, mask_ref, term):
         held_next[at, :] = value
         held_density[at, :] = coeffs_ref[0] * mid_ref[at, :] + coeffs_ref[1] * value
@@ -209,13 +209,38 @@
     )(band, here, first, now, *after)
 
 
-def last_kernel(begin, column, mask_ref, coeffs_ref, band_ref, second_ref, sums_ref, mid_ref, *rest):
+def piece_kernel(begin, column, mask_ref, coeffs_ref, band_ref, second_ref, sums_ref, mid_ref, next_ref, density_ref):
+    rows, width = second_ref.shape
+    inside = slice(column, column + width)
+    total = jnp.dot(band_ref[:, side_columns(rows, 1, False)], second_ref[...], preferred_element_type=jnp.float32)
+    for at, value in masked(begin + column, mask_ref, 2.0 * total + sums_ref[:, inside]):
+        next_ref[at, :] = value
+        density_ref[at, :] = coeffs_ref[0] * mid_ref[at, inside] + coeffs_ref[1] * value
+
+
+def piece_part(begin, column, mask, coeffs, band, second, sums, mid):
+    rows, width = second.shape
+    return pl.pallas_call(
+        functools.partial(piece_kernel, begin, column),
+        in_specs=[SMEM] * 2 + [VMEM] * 4,
+        out_specs=[VMEM] * 2,
+        out_shape=[jax.ShapeDtypeStruct(second.shape, jnp.float32)] * 2,
+        compiler_params=params(),
+        cost_estimate=cost(2 * rows * rows * width, 2 * rows * rows + 22 * rows * width),
+        name="piece_part",
+    )(mask, coeffs, band, second, sums, mid)
+
+
+def last_kernel(begin, column, mask_ref, coeffs_ref, band_ref, second_ref, sums_ref, mid_ref, piece_next_ref,
+                piece_density_ref, *rest):
     next_ref, density_ref, held_next, held_density, sems = rest[-5:]
     rows, width = second_ref.shape
     block = rows // mask_ref.shape[0]
     step = rows // CHUNKS
     inside = slice(column, column + width)
-    copies = []
+    everything = pl.ds(0, rows)
+    copies = start_writes(
+        [(piece_next_ref, next_ref, everything, begin), (piece_density_ref, density_ref, everything, begin)], sems, 0)
     for c in range(CHUNKS):
         total = jnp.dot(
             band_ref[c * step:(c + 1) * step, side_columns(rows, 1, False)], second_ref[...],
@@ -234,19 +259,19 @@
         copy.wait()
 
 
-def last_part(begin, column, mask, coeffs, band, second, sums, mid, outs):
+def last_part(begin, column, mask, coeffs, band, second, sums, mid, piece, outs):
     rows, width = second.shape
     return pl.pallas_call(
         functools.partial(last_kernel, begin, column),
-        in_specs=[SMEM] * 2 + [VMEM] * 4 + [HBM] * 2,
+        in_specs=[SMEM] * 2 + [VMEM] * 6 + [HBM] * 2,
         out_specs=[HBM] * 2,
         out_shape=[jax.ShapeDtypeStruct(out.shape, jnp.float32) for out in outs],
-        scratch_shapes=[pltpu.VMEM((rows, width), jnp.float32)] * 2 + [pltpu.SemaphoreType.DMA((2 * CHUNKS,))],
-        input_output_aliases={6: 0, 7: 1},
+        scratch_shapes=[pltpu.VMEM((rows, width), jnp.float32)] * 2 + [pltpu.SemaphoreType.DMA((2 + 2 * CHUNKS,))],
+        input_output_aliases={8: 0, 9: 1},
         compiler_params=params(),
         cost_estimate=cost(2 * rows * rows * width, 2 * rows * rows + 22 * rows * width),
         name="last_part",
-    )(mask, coeffs, band, second, sums, mid, *outs)
+    )(mask, coeffs, band, second, sums, mid, *piece, *outs)
 
 
 def local(h_strips, h_slots, t_prev, t_now, t_mask, coeffs):
@@ -257,7 +282,7 @@
     band = banded(h_slots, h_strips)
     low_sides, high_sides = both_sides(low), both_sides(high)
     mid_low, low_again = mid_part((0, width), [(0, width)], t_mask, band, low, *low_sides, t_prev, [])
-    low_sides = both_sides(low_again)
+    low_sides = [from_side(low_again, order, False) for order in (0, 1)]
     pieces = [(column, width // 2) for column in (0, width // 2)]
     mid_high, high_again, *cuts = mid_part(
         (width, width), [(0, width)] + pieces, t_mask, band, high, *high_sides, t_prev, [mid_low])
@@ -265,8 +290,8 @@
     seconds = [from_side(cut, 1, False) for cut in cuts]
     t_mid, *outs, token = next_part(t_mask, coeffs, band, low_again, *low_sides, t_now, [mid_low, mid_high])
     sums = begun_part((width, width), band, high_again, first, t_now, [token])
-    for (column, _), second in zip(pieces, seconds):
-        outs = last_part(width, column, t_mask, coeffs, band, second, sums, mid_high, outs)
+    piece = piece_part(width, 0, t_mask, coeffs, band, seconds[0], sums, mid_high)
+    outs = last_part(width, width // 2, t_mask, coeffs, band, seconds[1], sums, mid_high, piece, outs)
     return (t_mid, outs[0], outs[1])
 
 

time: 52.4 us -> 52.5 us (level)
  starting transfers between devices: 18.9 us -> 22.5 us
  waiting for transfers between devices: 19.4 us -> 16.8 us
  Pallas kernels: 10.7 us -> 10.1 us
    ppermute x9, starting transfers between devices: 18.9 us -> 22.5 us  [from_side(): return lax.ppermute(block, ('row', 'rep'), route)]
    ppermute x9, waiting for transfers between devices: 19.4 us -> 16.8 us  [from_side(): return lax.ppermute(block, ('row', 'rep'), route)]
    pallas_call x2 -> x1, Pallas kernels: 3.28 us -> 1.72 us  [last_part(): pl.pallas_call(functools.partial(last_kernel, begin, column), in_specs=[S...]
    pallas_call x0 -> x1, Pallas kernels: none -> 0.9 us  [piece_part(): pl.pallas_call(functools.partial(piece_kernel, begin, column), in_specs=[...]
  transfers between devices with their start and end apart: 9 -> 9, of which waited for: 7 -> 7; matrix products, arithmetic and copies ran while one was open for 0% -> 0% of each run, Pallas kernels for 17% -> 16%
where the time goes in v1:
time: 52.5 us; the launch traced here: 52.3 us
  starting transfers between devices  22.5 us (43%)
  waiting for transfers between devices  16.8 us (32%)
  Pallas kernels  10.1 us (19%)
  local copies, waits for them, and re-layouts  2.33 us (4%)
  between operations  0.73 us (1%)
    ppermute x9, starting transfers between devices, from_side(): return lax.ppermute(block, ('row', 'rep'), route)  22.5 us
    ppermute x9, waiting for transfers between devices, from_side(): return lax.ppermute(block, ('row', 'rep'), route)  16.8 us
    pallas_call x1, Pallas kernels, next_part(): pl.pallas_call(next_kernel, in_specs=[SMEM] * 2 + [VMEM] * 7, out_specs=[...  2.44 us
    pallas_call x2, Pallas kernels, mid_part(): pl.pallas_call(functools.partial(mid_kernel, span[0], pieces), in_specs=[...  2.35 us
    pallas_call x1, Pallas kernels, banded(): pl.pallas_call(band_kernel, in_specs=[SMEM, VMEM], out_specs=VMEM, out_sh...  2.17 us
    pallas_call x1, Pallas kernels, last_part(): pl.pallas_call(functools.partial(last_kernel, begin, column), in_specs=[S...  1.72 us
    unnamed x14, local copies, waits for them, and re-layouts  1.25 us
    slice x1, local copies, waits for them, and re-layouts, local(): low = t_now[:, :width].astype(jnp.bfloat16)  1.07 us
  transfers between devices with their start and end apart: 9, of which 7 were waited for; matrix products, arithmetic and copies ran while one was open for 0% of the time, Pallas kernels for 16%

profile of v1, /device:TPU:0, one launch (start us, length us, event | category | flops | bytes accessed | tf_op | source)
XLA Modules:
  0.0 52.3 jit_solution(14959314984748212879)
XLA Ops:
  0.6 0.0 copy-start.6
  0.6 1.1 %slice.7.here_ref = bf16[512,256]{1,0:T(8,128)(2,1)S(1)} slice(f32[512,512]{1,0:T(8,128)} %now_ref.2), slice={[0:512], [0:256]} | slice | bytes 524288 | tf_op jit(solution)/shard_map/slice | solution.py:279
  1.7 3.1 %collective-permute-start.1 = (bf16[512,256]{1,0:T(8,128)(2,1)S(1)}, bf16[512,256]{1,0:T(8,128)(2,1)S(1)}, u32[]{:S(2)}, u32[]{:S(2)}) collective-permute-start(bf16[512,256]{1,0:T(8,128)(2,1)S(1)} %slice.7.here_ref), channel_id=1, source_target_pairs={{12,0},{5,1},{0,4},{9,5},{4,8},{13,9},{8,12},{1,13},{14,2},{7,3},{... | collective-permute-start | bytes 786440 | tf_op jit(solution)/shard_map/ppermute | solution.py:28
  4.8 2.1 %collective-permute-start = (bf16[512,256]{1,0:T(8,128)(2,1)S(1)}, bf16[512,256]{1,0:T(8,128)(2,1)S(1)}, u32[]{:S(2)}, u32[]{:S(2)}) collective-permute-start(bf16[512,256]{1,0:T(8,128)(2,1)S(1)} %slice.7.here_ref), channel_id=1, source_target_pairs={{4,0},{13,1},{8,4},{1,5},{12,8},{5,9},{0,12},{9,13},{6,2},{15,3},{... | collective-permute-start | bytes 786440 | tf_op jit(solution)/shard_map/ppermute | solution.py:28
  6.9 0.0 copy-start
  6.9 1.2 %copy-done = f32[512,512]{1,0:T(8,128)S(1)} copy-done((f32[512,512]{1,0:T(8,128)S(1)}, f32[512,512]{1,0:T(8,128)}, u32[]{:S(2)}) %copy-start) | copy-done | bytes 1048600
  8.1 0.0 copy-start.3
  8.2 0.0 copy-start.2
  8.2 0.0 copy-start.4
  8.2 0.1 collective-permute-start.5
  8.2 3.8 %collective-permute-start.4 = (bf16[512,256]{1,0:T(8,128)(2,1)S(1)}, bf16[512,256]{1,0:T(8,128)(2,1)S(1)}, u32[]{:S(2)}, u32[]{:S(2)}) collective-permute-start(bf16[512,256]{1,0:T(8,128)(2,1)S(1)} %round_part.1.here_ref), channel_id=1, source_target_pairs={{4,0},{13,1},{8,4},{1,5},{12,8},{5,9},{0,12},{9,13},{6,2},{15,3},{... | collective-permute-start | bytes 786440 | tf_op jit(solution)/shard_map/ppermute | solution.py:28
  12.1 0.0 copy-done.6
  12.1 0.0 copy-done.3
  12.1 2.2 %band.1.band_ref = bf16[512,1536]{1,0:T(8,128)(2,1)S(1)} custom-call(s32[8,16]{1,0:T(8,128)S(1)} %copy-done.6, bf16[8,64,1024]{2,1,0:T(8,128)(2,1)S(1)} %copy-done.3), custom_call_target="tpu_custom_call" | custom-call | flops 6291456 | bytes 2621440 | tf_op jit(solution)/shard_map/band/pallas_call | solution.py:92
  14.2 0.0 collective-permute-done.1.first_ref
  14.2 4.3 %collective-permute-done.second_ref = bf16[512,256]{1,0:T(8,128)(2,1)S(1)} collective-permute-done((bf16[512,256]{1,0:T(8,128)(2,1)S(1)}, bf16[512,256]{1,0:T(8,128)(2,1)S(1)}, u32[]{:S(2)}, u32[]{:S(2)}) %collective-permute-start) | collective-permute-done | bytes 262176 | tf_op jit(solution)/shard_map/ppermute | solution.py:28
  18.6 0.0 copy-done.2
  18.6 0.0 copy-done.4
  18.6 1.2 %mid_part.2 = (f32[512,256]{1,0:T(8,128)S(1)}, bf16[512,256]{1,0:T(8,128)(2,1)S(1)}) custom-call(s32[8,8]{1,0:T(8,128)S(1)} %copy-done.4, bf16[512,1536]{1,0:T(8,128)(2,1)S(1)} %band.1.band_ref, bf16[512,256]{1,0:T(8,128)(2,1)S(1)} %slice.7.here_ref, bf16[512,256]{1,0:T(8,128)(2,1)S(1)} %collective-permute-done.second_ref, ...), custom_call_target="tpu_custom_call" | custom-call | flops 402653184 | bytes 3670016 | tf_op jit(solution)/shard_map/mid_part/pallas_call | solution.py:150
  19.7 2.8 %collective-permute-start.3 = (bf16[512,256]{1,0:T(8,128)(2,1)S(1)}, bf16[512,256]{1,0:T(8,128)(2,1)S(1)}, u32[]{:S(2)}, u32[]{:S(2)}) collective-permute-start(bf16[512,256]{1,0:T(8,128)(2,1)S(1)} %get-tuple-element.24.here_ref), channel_id=1, source_target_pairs={{12,0},{13,1},{0,4},{1,5},{4,8},{5,9},{8,12},{9,13},{14,2},{15,3},... | collective-permute-start | bytes 786440 | tf_op jit(solution)/shard_map/ppermute | solution.py:28
  22.5 1.1 %collective-permute-start.2 = (bf16[512,256]{1,0:T(8,128)(2,1)S(1)}, bf16[512,256]{1,0:T(8,128)(2,1)S(1)}, u32[]{:S(2)}, u32[]{:S(2)}) collective-permute-start(bf16[512,256]{1,0:T(8,128)(2,1)S(1)} %get-tuple-element.24.here_ref), channel_id=1, source_target_pairs={{4,0},{5,1},{8,4},{9,5},{12,8},{13,9},{0,12},{1,13},{6,2},{7,3},{1... | collective-permute-start | bytes 786440 | tf_op jit(solution)/shard_map/ppermute | solution.py:28
  23.6 1.7 %collective-permute-done.5.first_ref = bf16[512,256]{1,0:T(8,128)(2,1)S(1)} collective-permute-done((bf16[512,256]{1,0:T(8,128)(2,1)S(1)}, bf16[512,256]{1,0:T(8,128)(2,1)S(1)}, u32[]{:S(2)}, u32[]{:S(2)}) %collective-permute-start.5) | collective-permute-done | bytes 262176 | tf_op jit(solution)/shard_map/ppermute | solution.py:28
  25.3 2.2 %collective-permute-done.4.second_ref = bf16[512,256]{1,0:T(8,128)(2,1)S(1)} collective-permute-done((bf16[512,256]{1,0:T(8,128)(2,1)S(1)}, bf16[512,256]{1,0:T(8,128)(2,1)S(1)}, u32[]{:S(2)}, u32[]{:S(2)}) %collective-permute-start.4) | collective-permute-done | bytes 262176 | tf_op jit(solution)/shard_map/ppermute | solution.py:28
  27.5 0.0 copy-start.1
  27.5 0.0 copy-start.5
  27.5 1.2 %mid_part.3 = (f32[512,256]{1,0:T(8,128)S(1)}, bf16[512,256]{1,0:T(8,128)(2,1)S(1)}, bf16[512,128]{1,0:T(8,128)(2,1)S(1)}, bf16[512,128]{1,0:T(8,128)(2,1)S(1)}) custom-call(s32[8,8]{1,0:T(8,128)S(1)} %copy-done.4, bf16[512,1536]{1,0:T(8,128)(2,1)S(1)} %band.1.band_ref, bf16[512,256]{1,0:T(8,128)(2,1)S(1)} %round_part.1.here_ref, ...), custom_call_target="tpu_custom_call" | custom-call | flops 402653184 | bytes 3670016 | tf_op jit(solution)/shard_map/mid_part/pallas_call | solution.py:150
  28.7 9.5 %collective-permute-start.7 = (bf16[512,256]{1,0:T(8,128)(2,1)S(1)}, bf16[512,256]{1,0:T(8,128)(2,1)S(1)}, u32[]{:S(2)}, u32[]{:S(2)}) collective-permute-start(bf16[512,256]{1,0:T(8,128)(2,1)S(1)} %get-tuple-element.30.here_ref), channel_id=1, source_target_pairs={{12,0},{13,1},{0,4},{1,5},{4,8},{5,9},{8,12},{9,13},{14,2},{15,3},... | collective-permute-start | bytes 786440 | tf_op jit(solution)/shard_map/ppermute | solution.py:28
  38.2 0.0 collective-permute-start.8
  38.2 0.0 collective-permute-start.6
  38.2 0.0 collective-permute-done.3.first_ref
  38.2 1.5 %collective-permute-done.2.second_ref = bf16[512,256]{1,0:T(8,128)(2,1)S(1)} collective-permute-done((bf16[512,256]{1,0:T(8,128)(2,1)S(1)}, bf16[512,256]{1,0:T(8,128)(2,1)S(1)}, u32[]{:S(2)}, u32[]{:S(2)}) %collective-permute-start.2) | collective-permute-done | bytes 262176 | tf_op jit(solution)/shard_map/ppermute | solution.py:28
  39.8 0.0 copy-done.1
  39.8 0.0 copy-done.5
  39.8 2.4 %next_part.1 = (f32[512,512]{1,0:T(8,128)}, f32[512,512]{1,0:T(8,128)}, f32[512,512]{1,0:T(8,128)}, f32[8,128]{1,0:T(8,128)S(1)}) custom-call(s32[8,8]{1,0:T(8,128)S(1)} %copy-done.4, f32[2]{0:T(128)S(1)} %copy-done.5, bf16[512,1536]{1,0:T(8,128)(2,1)S(1)} %band.1.band_ref, bf16[512,256]{1,0:T(8,128)(2,1)S(1)} %get-tuple-element.24.here_ref, ...), custom_call_target="tpu_custom_call" | custom-call | flops 402653184 | bytes 5505024 | tf_op jit(solution)/shard_map/next_part/pallas_call | solution.py:182
  42.2 5.5 %collective-permute-done.7.first_ref = bf16[512,256]{1,0:T(8,128)(2,1)S(1)} collective-permute-done((bf16[512,256]{1,0:T(8,128)(2,1)S(1)}, bf16[512,256]{1,0:T(8,128)(2,1)S(1)}, u32[]{:S(2)}, u32[]{:S(2)}) %collective-permute-start.7) | collective-permute-done | bytes 262176 | tf_op jit(solution)/shard_map/ppermute | solution.py:28
  47.7 0.4 begun_part.1.sums_ref
  48.2 0.9 %collective-permute-done.8.second_ref = bf16[512,128]{1,0:T(8,128)(2,1)S(1)} collective-permute-done((bf16[512,128]{1,0:T(8,128)(2,1)S(1)}, bf16[512,128]{1,0:T(8,128)(2,1)S(1)}, u32[]{:S(2)}, u32[]{:S(2)}) %collective-permute-start.8) | collective-permute-done | bytes 131104 | tf_op jit(solution)/shard_map/ppermute | solution.py:28
  49.1 0.9 %piece_part.1 = (f32[512,128]{1,0:T(8,128)S(1)}, f32[512,128]{1,0:T(8,128)S(1)}) custom-call(s32[8,8]{1,0:T(8,128)S(1)} %copy-done.4, f32[2]{0:T(128)S(1)} %copy-done.5, bf16[512,1536]{1,0:T(8,128)(2,1)S(1)} %band.1.band_ref, bf16[512,128]{1,0:T(8,128)(2,1)S(1)} %collective-permute-done.8.second_ref, f32[512,256]{1,0:T(8,128)S(1)} %begun_part.1.sums_ref, ...), custom_call_target="tpu_custom_call" | custom-call | flops 67108864 | bytes 1966080 | tf_op jit(solution)/shard_map/piece_part/pallas_call | solution.py:223
  50.0 0.6 %collective-permute-done.6.second_ref = bf16[512,128]{1,0:T(8,128)(2,1)S(1)} collective-permute-done((bf16[512,128]{1,0:T(8,128)(2,1)S(1)}, bf16[512,128]{1,0:T(8,128)(2,1)S(1)}, u32[]{:S(2)}, u32[]{:S(2)}) %collective-permute-start.6) | collective-permute-done | bytes 131104 | tf_op jit(solution)/shard_map/ppermute | solution.py:28
  50.6 1.7 %last_part.1 = (f32[512,512]{1,0:T(8,128)}, f32[512,512]{1,0:T(8,128)}) custom-call(s32[8,8]{1,0:T(8,128)S(1)} %copy-done.4, f32[2]{0:T(128)S(1)} %copy-done.5, bf16[512,1536]{1,0:T(8,128)(2,1)S(1)} %band.1.band_ref, bf16[512,128]{1,0:T(8,128)(2,1)S(1)} %collective-permute-done.6.second_ref, ...), custom_call_target="tpu_custom_call", output_to_operand_aliasing={{0}: (8, {}), {1}: (9, {})} | custom-call | flops 67108864 | bytes 1966080 | tf_op jit(solution)/shard_map/last_part/pallas_call | solution.py:264
  (1 shorter events, 0.0 us)
Async XLA Ops:
  0.6 11.4 %copy-start.6 = (s32[8,16]{1,0:T(8,128)S(1)}, s32[8,16]{1,0:T(8,128)}, u32[]{:S(2)}) copy-start(s32[8,16]{1,0:T(8,128)} %slots_ref.1) | copy-start | bytes 1540
  1.7 12.5 %collective-permute-start.1 = (bf16[512,256]{1,0:T(8,128)(2,1)S(1)}, bf16[512,256]{1,0:T(8,128)(2,1)S(1)}, u32[]{:S(2)}, u32[]{:S(2)}) collective-permute-start(bf16[512,256]{1,0:T(8,128)(2,1)S(1)} %slice.7.here_ref), channel_id=1, source_target_pairs={{12,0},{5,1},{0,4},{9,5},{4,8},{13,9},{8,12},{1,13},{14,2},{7,3},{... | collective-permute-start | bytes 786440 | tf_op jit(solution)/shard_map/ppermute | solution.py:28
  4.8 13.8 %collective-permute-start = (bf16[512,256]{1,0:T(8,128)(2,1)S(1)}, bf16[512,256]{1,0:T(8,128)(2,1)S(1)}, u32[]{:S(2)}, u32[]{:S(2)}) collective-permute-start(bf16[512,256]{1,0:T(8,128)(2,1)S(1)} %slice.7.here_ref), channel_id=1, source_target_pairs={{4,0},{13,1},{8,4},{1,5},{12,8},{5,9},{0,12},{9,13},{6,2},{15,3},{... | collective-permute-start | bytes 786440 | tf_op jit(solution)/shard_map/ppermute | solution.py:28
  6.9 1.2 %copy-start = (f32[512,512]{1,0:T(8,128)S(1)}, f32[512,512]{1,0:T(8,128)}, u32[]{:S(2)}) copy-start(f32[512,512]{1,0:T(8,128)} %now_ref.2) | copy-start | bytes 3145732
  8.1 3.9 %copy-start.3 = (bf16[8,64,1024]{2,1,0:T(8,128)(2,1)S(1)}, bf16[8,64,1024]{2,1,0:T(8,128)(2,1)}, u32[]{:S(2)}) copy-start(bf16[8,64,1024]{2,1,0:T(8,128)(2,1)} %strips_ref) | copy-start | bytes 3145732
  8.2 10.4 %copy-start.2 = (f32[512,512]{1,0:T(8,128)S(1)}, f32[512,512]{1,0:T(8,128)}, u32[]{:S(2)}) copy-start(f32[512,512]{1,0:T(8,128)} %prev_ref.1) | copy-start | bytes 3145732
  8.2 10.4 %copy-start.4 = (s32[8,8]{1,0:T(8,128)S(1)}, s32[8,8]{1,0:T(8,128)}, u32[]{:S(2)}) copy-start(s32[8,8]{1,0:T(8,128)} %mask_ref.9) | copy-start | bytes 772
  8.2 17.1 %collective-permute-start.5 = (bf16[512,256]{1,0:T(8,128)(2,1)S(1)}, bf16[512,256]{1,0:T(8,128)(2,1)S(1)}, u32[]{:S(2)}, u32[]{:S(2)}) collective-permute-start(bf16[512,256]{1,0:T(8,128)(2,1)S(1)} %round_part.1.here_ref), channel_id=1, source_target_pairs={{12,0},{5,1},{0,4},{9,5},{4,8},{13,9},{8,12},{1,13},{14,2},{7,3},{... | collective-permute-start | bytes 786440 | tf_op jit(solution)/shard_map/ppermute | solution.py:28
  8.2 19.3 %collective-permute-start.4 = (bf16[512,256]{1,0:T(8,128)(2,1)S(1)}, bf16[512,256]{1,0:T(8,128)(2,1)S(1)}, u32[]{:S(2)}, u32[]{:S(2)}) collective-permute-start(bf16[512,256]{1,0:T(8,128)(2,1)S(1)} %round_part.1.here_ref), channel_id=1, source_target_pairs={{4,0},{13,1},{8,4},{1,5},{12,8},{5,9},{0,12},{9,13},{6,2},{15,3},{... | collective-permute-start | bytes 786440 | tf_op jit(solution)/shard_map/ppermute | solution.py:28
  19.7 18.5 %collective-permute-start.3 = (bf16[512,256]{1,0:T(8,128)(2,1)S(1)}, bf16[512,256]{1,0:T(8,128)(2,1)S(1)}, u32[]{:S(2)}, u32[]{:S(2)}) collective-permute-start(bf16[512,256]{1,0:T(8,128)(2,1)S(1)} %get-tuple-element.24.here_ref), channel_id=1, source_target_pairs={{12,0},{13,1},{0,4},{1,5},{4,8},{5,9},{8,12},{9,13},{14,2},{15,3},... | collective-permute-start | bytes 786440 | tf_op jit(solution)/shard_map/ppermute | solution.py:28
  22.5 17.2 %collective-permute-start.2 = (bf16[512,256]{1,0:T(8,128)(2,1)S(1)}, bf16[512,256]{1,0:T(8,128)(2,1)S(1)}, u32[]{:S(2)}, u32[]{:S(2)}) collective-permute-start(bf16[512,256]{1,0:T(8,128)(2,1)S(1)} %get-tuple-element.24.here_ref), channel_id=1, source_target_pairs={{4,0},{5,1},{8,4},{9,5},{12,8},{13,9},{0,12},{1,13},{6,2},{7,3},{1... | collective-permute-start | bytes 786440 | tf_op jit(solution)/shard_map/ppermute | solution.py:28
  27.5 12.2 %copy-start.1 = (f32[512,512]{1,0:T(8,128)S(1)}, f32[512,512]{1,0:T(8,128)}, u32[]{:S(2)}) copy-start(f32[512,512]{1,0:T(8,128)} %now_ref.2) | copy-start | bytes 3145732
  27.5 12.2 %copy-start.5 = (f32[2]{0:T(128)S(1)}, f32[2]{0:T(128)}, u32[]{:S(2)}) copy-start(f32[2]{0:T(128)} %coeffs_ref.5) | copy-start | bytes 28
  28.7 19.0 %collective-permute-start.7 = (bf16[512,256]{1,0:T(8,128)(2,1)S(1)}, bf16[512,256]{1,0:T(8,128)(2,1)S(1)}, u32[]{:S(2)}, u32[]{:S(2)}) collective-permute-start(bf16[512,256]{1,0:T(8,128)(2,1)S(1)} %get-tuple-element.30.here_ref), channel_id=1, source_target_pairs={{12,0},{13,1},{0,4},{1,5},{4,8},{5,9},{8,12},{9,13},{14,2},{15,3},... | collective-permute-start | bytes 786440 | tf_op jit(solution)/shard_map/ppermute | solution.py:28
  38.2 10.9 %collective-permute-start.8 = (bf16[512,128]{1,0:T(8,128)(2,1)S(1)}, bf16[512,128]{1,0:T(8,128)(2,1)S(1)}, u32[]{:S(2)}, u32[]{:S(2)}) collective-permute-start(bf16[512,128]{1,0:T(8,128)(2,1)S(1)} %get-tuple-element.32), channel_id=1, source_target_pairs={{4,0},{5,1},{8,4},{9,5},{12,8},{13,9},{0,12},{1,13},{6,2},{7,3},{1... | collective-permute-start | bytes 393224 | tf_op jit(solution)/shard_map/ppermute | solution.py:28
  38.2 12.4 %collective-permute-start.6 = (bf16[512,128]{1,0:T(8,128)(2,1)S(1)}, bf16[512,128]{1,0:T(8,128)(2,1)S(1)}, u32[]{:S(2)}, u32[]{:S(2)}) collective-permute-start(bf16[512,128]{1,0:T(8,128)(2,1)S(1)} %get-tuple-element.29), channel_id=1, source_target_pairs={{4,0},{5,1},{8,4},{9,5},{12,8},{13,9},{0,12},{1,13},{6,2},{7,3},{1... | collective-permute-start | bytes 393224 | tf_op jit(solution)/shard_map/ppermute | solution.py:28

commit v2 on v1

--- a/solution.py
+++ b/solution.py
@@ -28,8 +28,8 @@
     return lax.ppermute(block, ("row", "rep"), route)
 
 
-def both_sides(block):
-    return tuple(from_side(block, order, True) for order in (0, 1))
+def both_sides(block, mixed):
+    return tuple(from_side(block, order, mixed) for order in (0, 1))
 
 
 def side_columns(depth, order, mixed):
@@ -134,9 +134,9 @@
     return copies
 
 
-def mid_kernel(start, pieces, mask_ref, band_ref, here_ref, second_ref, first_ref, prev_ref, *rest):
+def mid_kernel(start, pieces, mixed, mask_ref, band_ref, here_ref, second_ref, first_ref, prev_ref, *rest):
     mid_ref, round_refs = rest[-len(pieces) - 1], rest[-len(pieces):]
-    total = product(band_ref, here_ref, first_ref, second_ref)
+    total = product(band_ref, here_ref, first_ref, second_ref, mixed)
     term = 2.0 * total - prev_ref[:, start:start + here_ref.shape[1]]
     for at, value in masked(start, mask_ref, term):
         mid_ref[at, :] = value
@@ -145,10 +145,10 @@
             round_ref[at, :] = low[:, column:column + size]
 
 
-def mid_part(span, pieces, mask, band, here, first, second, prev, after):
+def mid_part(span, pieces, mixed, mask, band, here, first, second, prev, after):
     rows, width = here.shape
     return pl.pallas_call(
-        functools.partial(mid_kernel, span[0], pieces),
+        functools.partial(mid_kernel, span[0], pieces, mixed),
         in_specs=[SMEM] + [VMEM] * 5 + [ANY] * len(after),
         out_specs=[VMEM] * (1 + len(pieces)),
         out_shape=[jax.ShapeDtypeStruct(here.shape, jnp.float32)]
@@ -280,12 +280,12 @@
     low, t_now, t_prev, h_strips = lax.optimization_barrier((low, t_now, t_prev, h_strips))
     (high,) = rounded(t_now, [(width, width)])
     band = banded(h_slots, h_strips)
-    low_sides, high_sides = both_sides(low), both_sides(high)
-    mid_low, low_again = mid_part((0, width), [(0, width)], t_mask, band, low, *low_sides, t_prev, [])
-    low_sides = [from_side(low_again, order, False) for order in (0, 1)]
+    low_sides, high_sides = both_sides(low, False), both_sides(high, True)
+    mid_low, low_again = mid_part((0, width), [(0, width)], False, t_mask, band, low, *low_sides, t_prev, [])
+    low_sides = both_sides(low_again, False)
     pieces = [(column, width // 2) for column in (0, width // 2)]
     mid_high, high_again, *cuts = mid_part(
-        (width, width), [(0, width)] + pieces, t_mask, band, high, *high_sides, t_prev, [mid_low])
+        (width, width), [(0, width)] + pieces, True, t_mask, band, high, *high_sides, t_prev, [mid_low])
     first = from_side(high_again, 0, False)
     seconds = [from_side(cut, 1, False) for cut in cuts]
     t_mid, *outs, token = next_part(t_mask, coeffs, band, low_again, *low_sides, t_now, [mid_low, mid_high])

time: 52.5 us -> 53.8 us (1.025)
  waiting for transfers between devices: 16.8 us -> 22.2 us
  starting transfers between devices: 22.5 us -> 18.3 us
    ppermute x9, waiting for transfers between devices: 16.8 us -> 22.2 us  [from_side(): return lax.ppermute(block, ('row', 'rep'), route)]
    ppermute x9, starting transfers between devices: 22.5 us -> 18.3 us  [from_side(): return lax.ppermute(block, ('row', 'rep'), route)]
  transfers between devices with their start and end apart: 9 -> 9, of which waited for: 7 -> 6; matrix products, arithmetic and copies ran while one was open for 0% -> 0% of each run, Pallas kernels for 16% -> 16%
where the time goes in v2:
time: 53.8 us; the launch traced here: 53.6 us
  waiting for transfers between devices  22.2 us (41%)
  starting transfers between devices  18.3 us (34%)
  Pallas kernels  10.1 us (19%)
  local copies, waits for them, and re-layouts  2.33 us (4%)
  between operations  0.74 us (1%)
    ppermute x9, waiting for transfers between devices, from_side(): return lax.ppermute(block, ('row', 'rep'), route)  22.2 us
    ppermute x9, starting transfers between devices, from_side(): return lax.ppermute(block, ('row', 'rep'), route)  18.3 us
    pallas_call x1, Pallas kernels, next_part(): pl.pallas_call(next_kernel, in_specs=[SMEM] * 2 + [VMEM] * 7, out_specs=[...  2.44 us
    pallas_call x2, Pallas kernels, mid_part(): pl.pallas_call(functools.partial(mid_kernel, span[0], pieces, mixed), in_...  2.35 us
    pallas_call x1, Pallas kernels, banded(): pl.pallas_call(band_kernel, in_specs=[SMEM, VMEM], out_specs=VMEM, out_sh...  2.17 us
    pallas_call x1, Pallas kernels, last_part(): pl.pallas_call(functools.partial(last_kernel, begin, column), in_specs=[S...  1.72 us
    unnamed x14, local copies, waits for them, and re-layouts  1.25 us
  transfers between devices with their start and end apart: 9, of which 6 were waited for; matrix products, arithmetic and copies ran while one was open for 0% of the time, Pallas kernels for 16%

profile of v2, /device:TPU:0, one launch (start us, length us, event | category | flops | bytes accessed | tf_op | source)
XLA Modules:
  0.0 53.6 jit_solution(13459370944303407049)
XLA Ops:
  0.6 0.0 copy-start.6
  0.6 1.1 %slice.7.here_ref = bf16[512,256]{1,0:T(8,128)(2,1)S(1)} slice(f32[512,512]{1,0:T(8,128)} %now_ref.2), slice={[0:512], [0:256]} | slice | bytes 524288 | tf_op jit(solution)/shard_map/slice | solution.py:279
  1.7 3.1 %collective-permute-start.1 = (bf16[512,256]{1,0:T(8,128)(2,1)S(1)}, bf16[512,256]{1,0:T(8,128)(2,1)S(1)}, u32[]{:S(2)}, u32[]{:S(2)}) collective-permute-start(bf16[512,256]{1,0:T(8,128)(2,1)S(1)} %slice.7.here_ref), channel_id=1, source_target_pairs={{12,0},{13,1},{0,4},{1,5},{4,8},{5,9},{8,12},{9,13},{14,2},{15,3},... | collective-permute-start | bytes 786440 | tf_op jit(solution)/shard_map/ppermute | solution.py:28
  4.8 2.1 %collective-permute-start = (bf16[512,256]{1,0:T(8,128)(2,1)S(1)}, bf16[512,256]{1,0:T(8,128)(2,1)S(1)}, u32[]{:S(2)}, u32[]{:S(2)}) collective-permute-start(bf16[512,256]{1,0:T(8,128)(2,1)S(1)} %slice.7.here_ref), channel_id=1, source_target_pairs={{4,0},{5,1},{8,4},{9,5},{12,8},{13,9},{0,12},{1,13},{6,2},{7,3},{1... | collective-permute-start | bytes 786440 | tf_op jit(solution)/shard_map/ppermute | solution.py:28
  6.9 0.0 copy-start
  6.9 1.2 %copy-done = f32[512,512]{1,0:T(8,128)S(1)} copy-done((f32[512,512]{1,0:T(8,128)S(1)}, f32[512,512]{1,0:T(8,128)}, u32[]{:S(2)}) %copy-start) | copy-done | bytes 1048600
  8.1 0.0 copy-start.3
  8.2 0.0 copy-start.2
  8.2 0.0 copy-start.4
  8.2 0.1 collective-permute-start.5
  8.2 3.8 %collective-permute-start.4 = (bf16[512,256]{1,0:T(8,128)(2,1)S(1)}, bf16[512,256]{1,0:T(8,128)(2,1)S(1)}, u32[]{:S(2)}, u32[]{:S(2)}) collective-permute-start(bf16[512,256]{1,0:T(8,128)(2,1)S(1)} %round_part.1.here_ref), channel_id=1, source_target_pairs={{4,0},{13,1},{8,4},{1,5},{12,8},{5,9},{0,12},{9,13},{6,2},{15,3},{... | collective-permute-start | bytes 786440 | tf_op jit(solution)/shard_map/ppermute | solution.py:28
  12.1 0.0 copy-done.6
  12.1 0.0 copy-done.3
  12.1 2.2 %band.1.band_ref = bf16[512,1536]{1,0:T(8,128)(2,1)S(1)} custom-call(s32[8,16]{1,0:T(8,128)S(1)} %copy-done.6, bf16[8,64,1024]{2,1,0:T(8,128)(2,1)S(1)} %copy-done.3), custom_call_target="tpu_custom_call" | custom-call | flops 6291456 | bytes 2621440 | tf_op jit(solution)/shard_map/band/pallas_call | solution.py:92
  14.2 0.0 collective-permute-done.1.first_ref
  14.2 4.6 %collective-permute-done.second_ref = bf16[512,256]{1,0:T(8,128)(2,1)S(1)} collective-permute-done((bf16[512,256]{1,0:T(8,128)(2,1)S(1)}, bf16[512,256]{1,0:T(8,128)(2,1)S(1)}, u32[]{:S(2)}, u32[]{:S(2)}) %collective-permute-start) | collective-permute-done | bytes 262176 | tf_op jit(solution)/shard_map/ppermute | solution.py:28
  18.9 0.0 copy-done.2
  18.9 0.0 copy-done.4
  18.9 1.2 %mid_part.2 = (f32[512,256]{1,0:T(8,128)S(1)}, bf16[512,256]{1,0:T(8,128)(2,1)S(1)}) custom-call(s32[8,8]{1,0:T(8,128)S(1)} %copy-done.4, bf16[512,1536]{1,0:T(8,128)(2,1)S(1)} %band.1.band_ref, bf16[512,256]{1,0:T(8,128)(2,1)S(1)} %slice.7.here_ref, bf16[512,256]{1,0:T(8,128)(2,1)S(1)} %collective-permute-done.second_ref, ...), custom_call_target="tpu_custom_call" | custom-call | flops 402653184 | bytes 3670016 | tf_op jit(solution)/shard_map/mid_part/pallas_call | solution.py:150
  20.1 1.7 %collective-permute-start.3 = (bf16[512,256]{1,0:T(8,128)(2,1)S(1)}, bf16[512,256]{1,0:T(8,128)(2,1)S(1)}, u32[]{:S(2)}, u32[]{:S(2)}) collective-permute-start(bf16[512,256]{1,0:T(8,128)(2,1)S(1)} %get-tuple-element.24.here_ref), channel_id=1, source_target_pairs={{12,0},{13,1},{0,4},{1,5},{4,8},{5,9},{8,12},{9,13},{14,2},{15,3},... | collective-permute-start | bytes 786440 | tf_op jit(solution)/shard_map/ppermute | solution.py:28
  21.8 3.6 %collective-permute-start.2 = (bf16[512,256]{1,0:T(8,128)(2,1)S(1)}, bf16[512,256]{1,0:T(8,128)(2,1)S(1)}, u32[]{:S(2)}, u32[]{:S(2)}) collective-permute-start(bf16[512,256]{1,0:T(8,128)(2,1)S(1)} %get-tuple-element.24.here_ref), channel_id=1, source_target_pairs={{4,0},{5,1},{8,4},{9,5},{12,8},{13,9},{0,12},{1,13},{6,2},{7,3},{1... | collective-permute-start | bytes 786440 | tf_op jit(solution)/shard_map/ppermute | solution.py:28
  25.4 0.0 collective-permute-done.5.first_ref
  25.4 6.1 %collective-permute-done.4.second_ref = bf16[512,256]{1,0:T(8,128)(2,1)S(1)} collective-permute-done((bf16[512,256]{1,0:T(8,128)(2,1)S(1)}, bf16[512,256]{1,0:T(8,128)(2,1)S(1)}, u32[]{:S(2)}, u32[]{:S(2)}) %collective-permute-start.4) | collective-permute-done | bytes 262176 | tf_op jit(solution)/shard_map/ppermute | solution.py:28
  31.5 0.0 copy-start.1
  31.5 0.0 copy-start.5
  31.5 1.2 %mid_part.3 = (f32[512,256]{1,0:T(8,128)S(1)}, bf16[512,256]{1,0:T(8,128)(2,1)S(1)}, bf16[512,128]{1,0:T(8,128)(2,1)S(1)}, bf16[512,128]{1,0:T(8,128)(2,1)S(1)}) custom-call(s32[8,8]{1,0:T(8,128)S(1)} %copy-done.4, bf16[512,1536]{1,0:T(8,128)(2,1)S(1)} %band.1.band_ref, bf16[512,256]{1,0:T(8,128)(2,1)S(1)} %round_part.1.here_ref, ...), custom_call_target="tpu_custom_call" | custom-call | flops 402653184 | bytes 3670016 | tf_op jit(solution)/shard_map/mid_part/pallas_call | solution.py:150
  32.7 0.1 collective-permute-start.7
  32.8 3.8 %collective-permute-start.8 = (bf16[512,128]{1,0:T(8,128)(2,1)S(1)}, bf16[512,128]{1,0:T(8,128)(2,1)S(1)}, u32[]{:S(2)}, u32[]{:S(2)}) collective-permute-start(bf16[512,128]{1,0:T(8,128)(2,1)S(1)} %get-tuple-element.32), channel_id=1, source_target_pairs={{4,0},{5,1},{8,4},{9,5},{12,8},{13,9},{0,12},{1,13},{6,2},{7,3},{1... | collective-permute-start | bytes 393224 | tf_op jit(solution)/shard_map/ppermute | solution.py:28
  36.6 0.0 collective-permute-start.6
  36.6 0.0 collective-permute-done.3.first_ref
  36.6 5.6 %collective-permute-done.2.second_ref = bf16[512,256]{1,0:T(8,128)(2,1)S(1)} collective-permute-done((bf16[512,256]{1,0:T(8,128)(2,1)S(1)}, bf16[512,256]{1,0:T(8,128)(2,1)S(1)}, u32[]{:S(2)}, u32[]{:S(2)}) %collective-permute-start.2) | collective-permute-done | bytes 262176 | tf_op jit(solution)/shard_map/ppermute | solution.py:28
  42.2 0.0 copy-done.1
  42.2 0.0 copy-done.5
  42.2 2.4 %next_part.1 = (f32[512,512]{1,0:T(8,128)}, f32[512,512]{1,0:T(8,128)}, f32[512,512]{1,0:T(8,128)}, f32[8,128]{1,0:T(8,128)S(1)}) custom-call(s32[8,8]{1,0:T(8,128)S(1)} %copy-done.4, f32[2]{0:T(128)S(1)} %copy-done.5, bf16[512,1536]{1,0:T(8,128)(2,1)S(1)} %band.1.band_ref, bf16[512,256]{1,0:T(8,128)(2,1)S(1)} %get-tuple-element.24.here_ref, ...), custom_call_target="tpu_custom_call" | custom-call | flops 402653184 | bytes 5505024 | tf_op jit(solution)/shard_map/next_part/pallas_call | solution.py:182
  44.7 3.1 %collective-permute-done.7.first_ref = bf16[512,256]{1,0:T(8,128)(2,1)S(1)} collective-permute-done((bf16[512,256]{1,0:T(8,128)(2,1)S(1)}, bf16[512,256]{1,0:T(8,128)(2,1)S(1)}, u32[]{:S(2)}, u32[]{:S(2)}) %collective-permute-start.7) | collective-permute-done | bytes 262176 | tf_op jit(solution)/shard_map/ppermute | solution.py:28
  47.8 0.4 begun_part.1.sums_ref
  48.2 1.5 %collective-permute-done.8.second_ref = bf16[512,128]{1,0:T(8,128)(2,1)S(1)} collective-permute-done((bf16[512,128]{1,0:T(8,128)(2,1)S(1)}, bf16[512,128]{1,0:T(8,128)(2,1)S(1)}, u32[]{:S(2)}, u32[]{:S(2)}) %collective-permute-start.8) | collective-permute-done | bytes 131104 | tf_op jit(solution)/shard_map/ppermute | solution.py:28
  49.8 0.9 %piece_part.1 = (f32[512,128]{1,0:T(8,128)S(1)}, f32[512,128]{1,0:T(8,128)S(1)}) custom-call(s32[8,8]{1,0:T(8,128)S(1)} %copy-done.4, f32[2]{0:T(128)S(1)} %copy-done.5, bf16[512,1536]{1,0:T(8,128)(2,1)S(1)} %band.1.band_ref, bf16[512,128]{1,0:T(8,128)(2,1)S(1)} %collective-permute-done.8.second_ref, f32[512,256]{1,0:T(8,128)S(1)} %begun_part.1.sums_ref, ...), custom_call_target="tpu_custom_call" | custom-call | flops 67108864 | bytes 1966080 | tf_op jit(solution)/shard_map/piece_part/pallas_call | solution.py:223
  50.7 1.2 %collective-permute-done.6.second_ref = bf16[512,128]{1,0:T(8,128)(2,1)S(1)} collective-permute-done((bf16[512,128]{1,0:T(8,128)(2,1)S(1)}, bf16[512,128]{1,0:T(8,128)(2,1)S(1)}, u32[]{:S(2)}, u32[]{:S(2)}) %collective-permute-start.6) | collective-permute-done | bytes 131104 | tf_op jit(solution)/shard_map/ppermute | solution.py:28
  51.9 1.7 %last_part.1 = (f32[512,512]{1,0:T(8,128)}, f32[512,512]{1,0:T(8,128)}) custom-call(s32[8,8]{1,0:T(8,128)S(1)} %copy-done.4, f32[2]{0:T(128)S(1)} %copy-done.5, bf16[512,1536]{1,0:T(8,128)(2,1)S(1)} %band.1.band_ref, bf16[512,128]{1,0:T(8,128)(2,1)S(1)} %collective-permute-done.6.second_ref, ...), custom_call_target="tpu_custom_call", output_to_operand_aliasing={{0}: (8, {}), {1}: (9, {})} | custom-call | flops 67108864 | bytes 1966080 | tf_op jit(solution)/shard_map/last_part/pallas_call | solution.py:264
  (1 shorter events, 0.0 us)
Async XLA Ops:
  0.6 11.4 %copy-start.6 = (s32[8,16]{1,0:T(8,128)S(1)}, s32[8,16]{1,0:T(8,128)}, u32[]{:S(2)}) copy-start(s32[8,16]{1,0:T(8,128)} %slots_ref.1) | copy-start | bytes 1540
  1.7 12.5 %collective-permute-start.1 = (bf16[512,256]{1,0:T(8,128)(2,1)S(1)}, bf16[512,256]{1,0:T(8,128)(2,1)S(1)}, u32[]{:S(2)}, u32[]{:S(2)}) collective-permute-start(bf16[512,256]{1,0:T(8,128)(2,1)S(1)} %slice.7.here_ref), channel_id=1, source_target_pairs={{12,0},{13,1},{0,4},{1,5},{4,8},{5,9},{8,12},{9,13},{14,2},{15,3},... | collective-permute-start | bytes 786440 | tf_op jit(solution)/shard_map/ppermute | solution.py:28
  4.8 14.1 %collective-permute-start = (bf16[512,256]{1,0:T(8,128)(2,1)S(1)}, bf16[512,256]{1,0:T(8,128)(2,1)S(1)}, u32[]{:S(2)}, u32[]{:S(2)}) collective-permute-start(bf16[512,256]{1,0:T(8,128)(2,1)S(1)} %slice.7.here_ref), channel_id=1, source_target_pairs={{4,0},{5,1},{8,4},{9,5},{12,8},{13,9},{0,12},{1,13},{6,2},{7,3},{1... | collective-permute-start | bytes 786440 | tf_op jit(solution)/shard_map/ppermute | solution.py:28
  6.9 1.2 %copy-start = (f32[512,512]{1,0:T(8,128)S(1)}, f32[512,512]{1,0:T(8,128)}, u32[]{:S(2)}) copy-start(f32[512,512]{1,0:T(8,128)} %now_ref.2) | copy-start | bytes 3145732
  8.1 3.9 %copy-start.3 = (bf16[8,64,1024]{2,1,0:T(8,128)(2,1)S(1)}, bf16[8,64,1024]{2,1,0:T(8,128)(2,1)}, u32[]{:S(2)}) copy-start(bf16[8,64,1024]{2,1,0:T(8,128)(2,1)} %strips_ref) | copy-start | bytes 3145732
  8.2 10.7 %copy-start.2 = (f32[512,512]{1,0:T(8,128)S(1)}, f32[512,512]{1,0:T(8,128)}, u32[]{:S(2)}) copy-start(f32[512,512]{1,0:T(8,128)} %prev_ref.1) | copy-start | bytes 3145732
  8.2 10.7 %copy-start.4 = (s32[8,8]{1,0:T(8,128)S(1)}, s32[8,8]{1,0:T(8,128)}, u32[]{:S(2)}) copy-start(s32[8,8]{1,0:T(8,128)} %mask_ref.9) | copy-start | bytes 772
  8.2 17.2 %collective-permute-start.5 = (bf16[512,256]{1,0:T(8,128)(2,1)S(1)}, bf16[512,256]{1,0:T(8,128)(2,1)S(1)}, u32[]{:S(2)}, u32[]{:S(2)}) collective-permute-start(bf16[512,256]{1,0:T(8,128)(2,1)S(1)} %round_part.1.here_ref), channel_id=1, source_target_pairs={{12,0},{5,1},{0,4},{9,5},{4,8},{13,9},{8,12},{1,13},{14,2},{7,3},{... | collective-permute-start | bytes 786440 | tf_op jit(solution)/shard_map/ppermute | solution.py:28
  8.2 23.3 %collective-permute-start.4 = (bf16[512,256]{1,0:T(8,128)(2,1)S(1)}, bf16[512,256]{1,0:T(8,128)(2,1)S(1)}, u32[]{:S(2)}, u32[]{:S(2)}) collective-permute-start(bf16[512,256]{1,0:T(8,128)(2,1)S(1)} %round_part.1.here_ref), channel_id=1, source_target_pairs={{4,0},{13,1},{8,4},{1,5},{12,8},{5,9},{0,12},{9,13},{6,2},{15,3},{... | collective-permute-start | bytes 786440 | tf_op jit(solution)/shard_map/ppermute | solution.py:28
  20.1 16.5 %collective-permute-start.3 = (bf16[512,256]{1,0:T(8,128)(2,1)S(1)}, bf16[512,256]{1,0:T(8,128)(2,1)S(1)}, u32[]{:S(2)}, u32[]{:S(2)}) collective-permute-start(bf16[512,256]{1,0:T(8,128)(2,1)S(1)} %get-tuple-element.24.here_ref), channel_id=1, source_target_pairs={{12,0},{13,1},{0,4},{1,5},{4,8},{5,9},{8,12},{9,13},{14,2},{15,3},... | collective-permute-start | bytes 786440 | tf_op jit(solution)/shard_map/ppermute | solution.py:28
  21.8 20.4 %collective-permute-start.2 = (bf16[512,256]{1,0:T(8,128)(2,1)S(1)}, bf16[512,256]{1,0:T(8,128)(2,1)S(1)}, u32[]{:S(2)}, u32[]{:S(2)}) collective-permute-start(bf16[512,256]{1,0:T(8,128)(2,1)S(1)} %get-tuple-element.24.here_ref), channel_id=1, source_target_pairs={{4,0},{5,1},{8,4},{9,5},{12,8},{13,9},{0,12},{1,13},{6,2},{7,3},{1... | collective-permute-start | bytes 786440 | tf_op jit(solution)/shard_map/ppermute | solution.py:28
  31.5 10.7 %copy-start.1 = (f32[512,512]{1,0:T(8,128)S(1)}, f32[512,512]{1,0:T(8,128)}, u32[]{:S(2)}) copy-start(f32[512,512]{1,0:T(8,128)} %now_ref.2) | copy-start | bytes 3145732
  31.5 10.7 %copy-start.5 = (f32[2]{0:T(128)S(1)}, f32[2]{0:T(128)}, u32[]{:S(2)}) copy-start(f32[2]{0:T(128)} %coeffs_ref.5) | copy-start | bytes 28
  32.7 15.1 %collective-permute-start.7 = (bf16[512,256]{1,0:T(8,128)(2,1)S(1)}, bf16[512,256]{1,0:T(8,128)(2,1)S(1)}, u32[]{:S(2)}, u32[]{:S(2)}) collective-permute-start(bf16[512,256]{1,0:T(8,128)(2,1)S(1)} %get-tuple-element.30.here_ref), channel_id=1, source_target_pairs={{12,0},{13,1},{0,4},{1,5},{4,8},{5,9},{8,12},{9,13},{14,2},{15,3},... | collective-permute-start | bytes 786440 | tf_op jit(solution)/shard_map/ppermute | solution.py:28
  32.8 17.0 %collective-permute-start.8 = (bf16[512,128]{1,0:T(8,128)(2,1)S(1)}, bf16[512,128]{1,0:T(8,128)(2,1)S(1)}, u32[]{:S(2)}, u32[]{:S(2)}) collective-permute-start(bf16[512,128]{1,0:T(8,128)(2,1)S(1)} %get-tuple-element.32), channel_id=1, source_target_pairs={{4,0},{5,1},{8,4},{9,5},{12,8},{13,9},{0,12},{1,13},{6,2},{7,3},{1... | collective-permute-start | bytes 393224 | tf_op jit(solution)/shard_map/ppermute | solution.py:28
  36.6 15.3 %collective-permute-start.6 = (bf16[512,128]{1,0:T(8,128)(2,1)S(1)}, bf16[512,128]{1,0:T(8,128)(2,1)S(1)}, u32[]{:S(2)}, u32[]{:S(2)}) collective-permute-start(bf16[512,128]{1,0:T(8,128)(2,1)S(1)} %get-tuple-element.29), channel_id=1, source_target_pairs={{4,0},{5,1},{8,4},{9,5},{12,8},{13,9},{0,12},{1,13},{6,2},{7,3},{1... | collective-permute-start | bytes 393224 | tf_op jit(solution)/shard_map/ppermute | solution.py:28

commit v3 on v2

--- a/solution.py
+++ b/solution.py
@@ -280,12 +280,12 @@
     low, t_now, t_prev, h_strips = lax.optimization_barrier((low, t_now, t_prev, h_strips))
     (high,) = rounded(t_now, [(width, width)])
     band = banded(h_slots, h_strips)
-    low_sides, high_sides = both_sides(low, False), both_sides(high, True)
-    mid_low, low_again = mid_part((0, width), [(0, width)], False, t_mask, band, low, *low_sides, t_prev, [])
+    low_sides, high_sides = both_sides(low, True), both_sides(high, False)
+    mid_low, low_again = mid_part((0, width), [(0, width)], True, t_mask, band, low, *low_sides, t_prev, [])
     low_sides = both_sides(low_again, False)
     pieces = [(column, width // 2) for column in (0, width // 2)]
     mid_high, high_again, *cuts = mid_part(
-        (width, width), [(0, width)] + pieces, True, t_mask, band, high, *high_sides, t_prev, [mid_low])
+        (width, width), [(0, width)] + pieces, False, t_mask, band, high, *high_sides, t_prev, [mid_low])
     first = from_side(high_again, 0, False)
     seconds = [from_side(cut, 1, False) for cut in cuts]
     t_mid, *outs, token = next_part(t_mask, coeffs, band, low_again, *low_sides, t_now, [mid_low, mid_high])

time: 53.8 us -> 52.7 us (0.980)
  waiting for transfers between devices: 22.2 us -> 15.9 us
  starting transfers between devices: 18.3 us -> 23.6 us
    ppermute x9, waiting for transfers between devices: 22.2 us -> 15.9 us  [from_side(): return lax.ppermute(block, ('row', 'rep'), route)]
    ppermute x9, starting transfers between devices: 18.3 us -> 23.6 us  [from_side(): return lax.ppermute(block, ('row', 'rep'), route)]
where the time goes in v3:
time: 52.7 us; the launch traced here: 52.6 us
  starting transfers between devices  23.6 us (45%)
  waiting for transfers between devices  15.9 us (30%)
  Pallas kernels  10.1 us (19%)
  local copies, waits for them, and re-layouts  2.33 us (4%)
  between operations  0.74 us (1%)
    ppermute x9, starting transfers between devices, from_side(): return lax.ppermute(block, ('row', 'rep'), route)  23.6 us
    ppermute x9, waiting for transfers between devices, from_side(): return lax.ppermute(block, ('row', 'rep'), route)  15.9 us
    pallas_call x1, Pallas kernels, next_part(): pl.pallas_call(next_kernel, in_specs=[SMEM] * 2 + [VMEM] * 7, out_specs=[...  2.44 us
    pallas_call x2, Pallas kernels, mid_part(): pl.pallas_call(functools.partial(mid_kernel, span[0], pieces, mixed), in_...  2.35 us
    pallas_call x1, Pallas kernels, banded(): pl.pallas_call(band_kernel, in_specs=[SMEM, VMEM], out_specs=VMEM, out_sh...  2.17 us
    pallas_call x1, Pallas kernels, last_part(): pl.pallas_call(functools.partial(last_kernel, begin, column), in_specs=[S...  1.72 us
    unnamed x14, local copies, waits for them, and re-layouts  1.25 us
    slice x1, local copies, waits for them, and re-layouts, local(): low = t_now[:, :width].astype(jnp.bfloat16)  1.07 us
  transfers between devices with their start and end apart: 9, of which 6 were waited for; matrix products, arithmetic and copies ran while one was open for 0% of the time, Pallas kernels for 16%

profile of v3, /device:TPU:0, one launch (start us, length us, event | category | flops | bytes accessed | tf_op | source)
XLA Modules:
  0.0 52.6 jit_solution(4557280163494377650)
XLA Ops:
  0.6 0.0 copy-start.6
  0.6 1.1 %slice.7.here_ref = bf16[512,256]{1,0:T(8,128)(2,1)S(1)} slice(f32[512,512]{1,0:T(8,128)} %now_ref.2), slice={[0:512], [0:256]} | slice | bytes 524288 | tf_op jit(solution)/shard_map/slice | solution.py:279
  1.7 3.1 %collective-permute-start.1 = (bf16[512,256]{1,0:T(8,128)(2,1)S(1)}, bf16[512,256]{1,0:T(8,128)(2,1)S(1)}, u32[]{:S(2)}, u32[]{:S(2)}) collective-permute-start(bf16[512,256]{1,0:T(8,128)(2,1)S(1)} %slice.7.here_ref), channel_id=1, source_target_pairs={{12,0},{5,1},{0,4},{9,5},{4,8},{13,9},{8,12},{1,13},{14,2},{7,3},{... | collective-permute-start | bytes 786440 | tf_op jit(solution)/shard_map/ppermute | solution.py:28
  4.8 2.1 %collective-permute-start = (bf16[512,256]{1,0:T(8,128)(2,1)S(1)}, bf16[512,256]{1,0:T(8,128)(2,1)S(1)}, u32[]{:S(2)}, u32[]{:S(2)}) collective-permute-start(bf16[512,256]{1,0:T(8,128)(2,1)S(1)} %slice.7.here_ref), channel_id=1, source_target_pairs={{4,0},{13,1},{8,4},{1,5},{12,8},{5,9},{0,12},{9,13},{6,2},{15,3},{... | collective-permute-start | bytes 786440 | tf_op jit(solution)/shard_map/ppermute | solution.py:28
  6.9 0.0 copy-start
  6.9 1.2 %copy-done = f32[512,512]{1,0:T(8,128)S(1)} copy-done((f32[512,512]{1,0:T(8,128)S(1)}, f32[512,512]{1,0:T(8,128)}, u32[]{:S(2)}) %copy-start) | copy-done | bytes 1048600
  8.1 0.0 copy-start.3
  8.2 0.0 copy-start.2
  8.2 0.0 copy-start.4
  8.2 0.1 collective-permute-start.5
  8.2 3.8 %collective-permute-start.4 = (bf16[512,256]{1,0:T(8,128)(2,1)S(1)}, bf16[512,256]{1,0:T(8,128)(2,1)S(1)}, u32[]{:S(2)}, u32[]{:S(2)}) collective-permute-start(bf16[512,256]{1,0:T(8,128)(2,1)S(1)} %round_part.1.here_ref), channel_id=1, source_target_pairs={{4,0},{5,1},{8,4},{9,5},{12,8},{13,9},{0,12},{1,13},{6,2},{7,3},{1... | collective-permute-start | bytes 786440 | tf_op jit(solution)/shard_map/ppermute | solution.py:28
  12.1 0.0 copy-done.6
  12.1 0.0 copy-done.3
  12.1 2.2 %band.1.band_ref = bf16[512,1536]{1,0:T(8,128)(2,1)S(1)} custom-call(s32[8,16]{1,0:T(8,128)S(1)} %copy-done.6, bf16[8,64,1024]{2,1,0:T(8,128)(2,1)S(1)} %copy-done.3), custom_call_target="tpu_custom_call" | custom-call | flops 6291456 | bytes 2621440 | tf_op jit(solution)/shard_map/band/pallas_call | solution.py:92
  14.2 0.0 collective-permute-done.1.first_ref
  14.2 4.5 %collective-permute-done.second_ref = bf16[512,256]{1,0:T(8,128)(2,1)S(1)} collective-permute-done((bf16[512,256]{1,0:T(8,128)(2,1)S(1)}, bf16[512,256]{1,0:T(8,128)(2,1)S(1)}, u32[]{:S(2)}, u32[]{:S(2)}) %collective-permute-start) | collective-permute-done | bytes 262176 | tf_op jit(solution)/shard_map/ppermute | solution.py:28
  18.8 0.0 copy-done.2
  18.8 0.0 copy-done.4
  18.8 1.2 %mid_part.2 = (f32[512,256]{1,0:T(8,128)S(1)}, bf16[512,256]{1,0:T(8,128)(2,1)S(1)}) custom-call(s32[8,8]{1,0:T(8,128)S(1)} %copy-done.4, bf16[512,1536]{1,0:T(8,128)(2,1)S(1)} %band.1.band_ref, bf16[512,256]{1,0:T(8,128)(2,1)S(1)} %slice.7.here_ref, bf16[512,256]{1,0:T(8,128)(2,1)S(1)} %collective-permute-done.second_ref, ...), custom_call_target="tpu_custom_call" | custom-call | flops 402653184 | bytes 3670016 | tf_op jit(solution)/shard_map/mid_part/pallas_call | solution.py:150
  20.0 7.2 %collective-permute-start.3 = (bf16[512,256]{1,0:T(8,128)(2,1)S(1)}, bf16[512,256]{1,0:T(8,128)(2,1)S(1)}, u32[]{:S(2)}, u32[]{:S(2)}) collective-permute-start(bf16[512,256]{1,0:T(8,128)(2,1)S(1)} %get-tuple-element.24.here_ref), channel_id=1, source_target_pairs={{12,0},{13,1},{0,4},{1,5},{4,8},{5,9},{8,12},{9,13},{14,2},{15,3},... | collective-permute-start | bytes 786440 | tf_op jit(solution)/shard_map/ppermute | solution.py:28
  27.2 0.0 collective-permute-start.2
  27.2 0.0 collective-permute-done.5.first_ref
  27.2 2.9 %collective-permute-done.4.second_ref = bf16[512,256]{1,0:T(8,128)(2,1)S(1)} collective-permute-done((bf16[512,256]{1,0:T(8,128)(2,1)S(1)}, bf16[512,256]{1,0:T(8,128)(2,1)S(1)}, u32[]{:S(2)}, u32[]{:S(2)}) %collective-permute-start.4) | collective-permute-done | bytes 262176 | tf_op jit(solution)/shard_map/ppermute | solution.py:28
  30.0 0.0 copy-start.1
  30.0 0.0 copy-start.5
  30.0 1.2 %mid_part.3 = (f32[512,256]{1,0:T(8,128)S(1)}, bf16[512,256]{1,0:T(8,128)(2,1)S(1)}, bf16[512,128]{1,0:T(8,128)(2,1)S(1)}, bf16[512,128]{1,0:T(8,128)(2,1)S(1)}) custom-call(s32[8,8]{1,0:T(8,128)S(1)} %copy-done.4, bf16[512,1536]{1,0:T(8,128)(2,1)S(1)} %band.1.band_ref, bf16[512,256]{1,0:T(8,128)(2,1)S(1)} %round_part.1.here_ref, ...), custom_call_target="tpu_custom_call" | custom-call | flops 402653184 | bytes 3670016 | tf_op jit(solution)/shard_map/mid_part/pallas_call | solution.py:150
  31.2 7.2 %collective-permute-start.7 = (bf16[512,256]{1,0:T(8,128)(2,1)S(1)}, bf16[512,256]{1,0:T(8,128)(2,1)S(1)}, u32[]{:S(2)}, u32[]{:S(2)}) collective-permute-start(bf16[512,256]{1,0:T(8,128)(2,1)S(1)} %get-tuple-element.30.here_ref), channel_id=1, source_target_pairs={{12,0},{13,1},{0,4},{1,5},{4,8},{5,9},{8,12},{9,13},{14,2},{15,3},... | collective-permute-start | bytes 786440 | tf_op jit(solution)/shard_map/ppermute | solution.py:28
  38.4 0.0 collective-permute-start.8
  38.4 0.1 collective-permute-start.6
  38.6 0.0 collective-permute-done.3.first_ref
  38.6 3.5 %collective-permute-done.2.second_ref = bf16[512,256]{1,0:T(8,128)(2,1)S(1)} collective-permute-done((bf16[512,256]{1,0:T(8,128)(2,1)S(1)}, bf16[512,256]{1,0:T(8,128)(2,1)S(1)}, u32[]{:S(2)}, u32[]{:S(2)}) %collective-permute-start.2) | collective-permute-done | bytes 262176 | tf_op jit(solution)/shard_map/ppermute | solution.py:28
  42.0 0.0 copy-done.1
  42.0 0.0 copy-done.5
  42.0 2.4 %next_part.1 = (f32[512,512]{1,0:T(8,128)}, f32[512,512]{1,0:T(8,128)}, f32[512,512]{1,0:T(8,128)}, f32[8,128]{1,0:T(8,128)S(1)}) custom-call(s32[8,8]{1,0:T(8,128)S(1)} %copy-done.4, f32[2]{0:T(128)S(1)} %copy-done.5, bf16[512,1536]{1,0:T(8,128)(2,1)S(1)} %band.1.band_ref, bf16[512,256]{1,0:T(8,128)(2,1)S(1)} %get-tuple-element.24.here_ref, ...), custom_call_target="tpu_custom_call" | custom-call | flops 402653184 | bytes 5505024 | tf_op jit(solution)/shard_map/next_part/pallas_call | solution.py:182
  44.5 3.2 %collective-permute-done.7.first_ref = bf16[512,256]{1,0:T(8,128)(2,1)S(1)} collective-permute-done((bf16[512,256]{1,0:T(8,128)(2,1)S(1)}, bf16[512,256]{1,0:T(8,128)(2,1)S(1)}, u32[]{:S(2)}, u32[]{:S(2)}) %collective-permute-start.7) | collective-permute-done | bytes 262176 | tf_op jit(solution)/shard_map/ppermute | solution.py:28
  47.7 0.4 begun_part.1.sums_ref
  48.2 0.9 %collective-permute-done.8.second_ref = bf16[512,128]{1,0:T(8,128)(2,1)S(1)} collective-permute-done((bf16[512,128]{1,0:T(8,128)(2,1)S(1)}, bf16[512,128]{1,0:T(8,128)(2,1)S(1)}, u32[]{:S(2)}, u32[]{:S(2)}) %collective-permute-start.8) | collective-permute-done | bytes 131104 | tf_op jit(solution)/shard_map/ppermute | solution.py:28
  49.1 0.9 %piece_part.1 = (f32[512,128]{1,0:T(8,128)S(1)}, f32[512,128]{1,0:T(8,128)S(1)}) custom-call(s32[8,8]{1,0:T(8,128)S(1)} %copy-done.4, f32[2]{0:T(128)S(1)} %copy-done.5, bf16[512,1536]{1,0:T(8,128)(2,1)S(1)} %band.1.band_ref, bf16[512,128]{1,0:T(8,128)(2,1)S(1)} %collective-permute-done.8.second_ref, f32[512,256]{1,0:T(8,128)S(1)} %begun_part.1.sums_ref, ...), custom_call_target="tpu_custom_call" | custom-call | flops 67108864 | bytes 1966080 | tf_op jit(solution)/shard_map/piece_part/pallas_call | solution.py:223
  50.0 0.8 %collective-permute-done.6.second_ref = bf16[512,128]{1,0:T(8,128)(2,1)S(1)} collective-permute-done((bf16[512,128]{1,0:T(8,128)(2,1)S(1)}, bf16[512,128]{1,0:T(8,128)(2,1)S(1)}, u32[]{:S(2)}, u32[]{:S(2)}) %collective-permute-start.6) | collective-permute-done | bytes 131104 | tf_op jit(solution)/shard_map/ppermute | solution.py:28
  50.8 1.7 %last_part.1 = (f32[512,512]{1,0:T(8,128)}, f32[512,512]{1,0:T(8,128)}) custom-call(s32[8,8]{1,0:T(8,128)S(1)} %copy-done.4, f32[2]{0:T(128)S(1)} %copy-done.5, bf16[512,1536]{1,0:T(8,128)(2,1)S(1)} %band.1.band_ref, bf16[512,128]{1,0:T(8,128)(2,1)S(1)} %collective-permute-done.6.second_ref, ...), custom_call_target="tpu_custom_call", output_to_operand_aliasing={{0}: (8, {}), {1}: (9, {})} | custom-call | flops 67108864 | bytes 1966080 | tf_op jit(solution)/shard_map/last_part/pallas_call | solution.py:264
  (1 shorter events, 0.0 us)
Async XLA Ops:
  0.6 11.4 %copy-start.6 = (s32[8,16]{1,0:T(8,128)S(1)}, s32[8,16]{1,0:T(8,128)}, u32[]{:S(2)}) copy-start(s32[8,16]{1,0:T(8,128)} %slots_ref.1) | copy-start | bytes 1540
  1.7 12.5 %collective-permute-start.1 = (bf16[512,256]{1,0:T(8,128)(2,1)S(1)}, bf16[512,256]{1,0:T(8,128)(2,1)S(1)}, u32[]{:S(2)}, u32[]{:S(2)}) collective-permute-start(bf16[512,256]{1,0:T(8,128)(2,1)S(1)} %slice.7.here_ref), channel_id=1, source_target_pairs={{12,0},{5,1},{0,4},{9,5},{4,8},{13,9},{8,12},{1,13},{14,2},{7,3},{... | collective-permute-start | bytes 786440 | tf_op jit(solution)/shard_map/ppermute | solution.py:28
  4.8 14.0 %collective-permute-start = (bf16[512,256]{1,0:T(8,128)(2,1)S(1)}, bf16[512,256]{1,0:T(8,128)(2,1)S(1)}, u32[]{:S(2)}, u32[]{:S(2)}) collective-permute-start(bf16[512,256]{1,0:T(8,128)(2,1)S(1)} %slice.7.here_ref), channel_id=1, source_target_pairs={{4,0},{13,1},{8,4},{1,5},{12,8},{5,9},{0,12},{9,13},{6,2},{15,3},{... | collective-permute-start | bytes 786440 | tf_op jit(solution)/shard_map/ppermute | solution.py:28
  6.9 1.2 %copy-start = (f32[512,512]{1,0:T(8,128)S(1)}, f32[512,512]{1,0:T(8,128)}, u32[]{:S(2)}) copy-start(f32[512,512]{1,0:T(8,128)} %now_ref.2) | copy-start | bytes 3145732
  8.1 3.9 %copy-start.3 = (bf16[8,64,1024]{2,1,0:T(8,128)(2,1)S(1)}, bf16[8,64,1024]{2,1,0:T(8,128)(2,1)}, u32[]{:S(2)}) copy-start(bf16[8,64,1024]{2,1,0:T(8,128)(2,1)} %strips_ref) | copy-start | bytes 3145732
  8.2 10.6 %copy-start.2 = (f32[512,512]{1,0:T(8,128)S(1)}, f32[512,512]{1,0:T(8,128)}, u32[]{:S(2)}) copy-start(f32[512,512]{1,0:T(8,128)} %prev_ref.1) | copy-start | bytes 3145732
  8.2 10.6 %copy-start.4 = (s32[8,8]{1,0:T(8,128)S(1)}, s32[8,8]{1,0:T(8,128)}, u32[]{:S(2)}) copy-start(s32[8,8]{1,0:T(8,128)} %mask_ref.9) | copy-start | bytes 772
  8.2 19.0 %collective-permute-start.5 = (bf16[512,256]{1,0:T(8,128)(2,1)S(1)}, bf16[512,256]{1,0:T(8,128)(2,1)S(1)}, u32[]{:S(2)}, u32[]{:S(2)}) collective-permute-start(bf16[512,256]{1,0:T(8,128)(2,1)S(1)} %round_part.1.here_ref), channel_id=1, source_target_pairs={{12,0},{13,1},{0,4},{1,5},{4,8},{5,9},{8,12},{9,13},{14,2},{15,3},... | collective-permute-start | bytes 786440 | tf_op jit(solution)/shard_map/ppermute | solution.py:28
  8.2 21.8 %collective-permute-start.4 = (bf16[512,256]{1,0:T(8,128)(2,1)S(1)}, bf16[512,256]{1,0:T(8,128)(2,1)S(1)}, u32[]{:S(2)}, u32[]{:S(2)}) collective-permute-start(bf16[512,256]{1,0:T(8,128)(2,1)S(1)} %round_part.1.here_ref), channel_id=1, source_target_pairs={{4,0},{5,1},{8,4},{9,5},{12,8},{13,9},{0,12},{1,13},{6,2},{7,3},{1... | collective-permute-start | bytes 786440 | tf_op jit(solution)/shard_map/ppermute | solution.py:28
  20.0 18.6 %collective-permute-start.3 = (bf16[512,256]{1,0:T(8,128)(2,1)S(1)}, bf16[512,256]{1,0:T(8,128)(2,1)S(1)}, u32[]{:S(2)}, u32[]{:S(2)}) collective-permute-start(bf16[512,256]{1,0:T(8,128)(2,1)S(1)} %get-tuple-element.24.here_ref), channel_id=1, source_target_pairs={{12,0},{13,1},{0,4},{1,5},{4,8},{5,9},{8,12},{9,13},{14,2},{15,3},... | collective-permute-start | bytes 786440 | tf_op jit(solution)/shard_map/ppermute | solution.py:28
  27.2 14.9 %collective-permute-start.2 = (bf16[512,256]{1,0:T(8,128)(2,1)S(1)}, bf16[512,256]{1,0:T(8,128)(2,1)S(1)}, u32[]{:S(2)}, u32[]{:S(2)}) collective-permute-start(bf16[512,256]{1,0:T(8,128)(2,1)S(1)} %get-tuple-element.24.here_ref), channel_id=1, source_target_pairs={{4,0},{5,1},{8,4},{9,5},{12,8},{13,9},{0,12},{1,13},{6,2},{7,3},{1... | collective-permute-start | bytes 786440 | tf_op jit(solution)/shard_map/ppermute | solution.py:28
  30.0 12.0 %copy-start.1 = (f32[512,512]{1,0:T(8,128)S(1)}, f32[512,512]{1,0:T(8,128)}, u32[]{:S(2)}) copy-start(f32[512,512]{1,0:T(8,128)} %now_ref.2) | copy-start | bytes 3145732
  30.0 12.0 %copy-start.5 = (f32[2]{0:T(128)S(1)}, f32[2]{0:T(128)}, u32[]{:S(2)}) copy-start(f32[2]{0:T(128)} %coeffs_ref.5) | copy-start | bytes 28
  31.2 16.5 %collective-permute-start.7 = (bf16[512,256]{1,0:T(8,128)(2,1)S(1)}, bf16[512,256]{1,0:T(8,128)(2,1)S(1)}, u32[]{:S(2)}, u32[]{:S(2)}) collective-permute-start(bf16[512,256]{1,0:T(8,128)(2,1)S(1)} %get-tuple-element.30.here_ref), channel_id=1, source_target_pairs={{12,0},{13,1},{0,4},{1,5},{4,8},{5,9},{8,12},{9,13},{14,2},{15,3},... | collective-permute-start | bytes 786440 | tf_op jit(solution)/shard_map/ppermute | solution.py:28
  38.4 10.7 %collective-permute-start.8 = (bf16[512,128]{1,0:T(8,128)(2,1)S(1)}, bf16[512,128]{1,0:T(8,128)(2,1)S(1)}, u32[]{:S(2)}, u32[]{:S(2)}) collective-permute-start(bf16[512,128]{1,0:T(8,128)(2,1)S(1)} %get-tuple-element.32), channel_id=1, source_target_pairs={{4,0},{5,1},{8,4},{9,5},{12,8},{13,9},{0,12},{1,13},{6,2},{7,3},{1... | collective-permute-start | bytes 393224 | tf_op jit(solution)/shard_map/ppermute | solution.py:28
  38.4 12.4 %collective-permute-start.6 = (bf16[512,128]{1,0:T(8,128)(2,1)S(1)}, bf16[512,128]{1,0:T(8,128)(2,1)S(1)}, u32[]{:S(2)}, u32[]{:S(2)}) collective-permute-start(bf16[512,128]{1,0:T(8,128)(2,1)S(1)} %get-tuple-element.29), channel_id=1, source_target_pairs={{4,0},{5,1},{8,4},{9,5},{12,8},{13,9},{0,12},{1,13},{6,2},{7,3},{1... | collective-permute-start | bytes 393224 | tf_op jit(solution)/shard_map/ppermute | solution.py:28

commit v4 on v1

--- a/solution.py
+++ b/solution.py
@@ -167,7 +167,7 @@
     token_ref[...] = jnp.zeros_like(token_ref)
     copies = start_writes(
         [(mid_ref, t_mid_ref, everything, 0), (other_mid_ref, t_mid_ref, everything, width)], sems, 0)
-    term = 2.0 * product(band_ref, here_ref, first_ref, second_ref, mixed=False) - now_ref[:, :width]
+    term = 2.0 * product(band_ref, here_ref, first_ref, second_ref) - now_ref[:, :width]
     for at, value in masked(0, mask_ref, term):
         held_next[at, :] = value
         held_density[at, :] = coeffs_ref[0] * mid_ref[at, :] + coeffs_ref[1] * value
@@ -282,7 +282,7 @@
     band = banded(h_slots, h_strips)
     low_sides, high_sides = both_sides(low), both_sides(high)
     mid_low, low_again = mid_part((0, width), [(0, width)], t_mask, band, low, *low_sides, t_prev, [])
-    low_sides = [from_side(low_again, order, False) for order in (0, 1)]
+    low_sides = both_sides(low_again)
     pieces = [(column, width // 2) for column in (0, width // 2)]
     mid_high, high_again, *cuts = mid_part(
         (width, width), [(0, width)] + pieces, t_mask, band, high, *high_sides, t_prev, [mid_low])

time: 52.5 us -> 52.5 us (level)
  starting transfers between devices: 22.5 us -> 18.9 us
  waiting for transfers between devices: 16.8 us -> 20.2 us
    ppermute x9, starting transfers between devices: 22.5 us -> 18.9 us  [from_side(): return lax.ppermute(block, ('row', 'rep'), route)]
    ppermute x9, waiting for transfers between devices: 16.8 us -> 20.2 us  [from_side(): return lax.ppermute(block, ('row', 'rep'), route)]
where the time goes in v4:
time: 52.5 us; the launch traced here: 52.2 us
  waiting for transfers between devices  20.2 us (38%)
  starting transfers between devices  18.9 us (36%)
  Pallas kernels  10.1 us (19%)
  local copies, waits for them, and re-layouts  2.33 us (4%)
  between operations  0.74 us (1%)
    ppermute x9, waiting for transfers between devices, from_side(): return lax.ppermute(block, ('row', 'rep'), route)  20.2 us
    ppermute x9, starting transfers between devices, from_side(): return lax.ppermute(block, ('row', 'rep'), route)  18.9 us
    pallas_call x1, Pallas kernels, next_part(): pl.pallas_call(next_kernel, in_specs=[SMEM] * 2 + [VMEM] * 7, out_specs=[...  2.44 us
    pallas_call x2, Pallas kernels, mid_part(): pl.pallas_call(functools.partial(mid_kernel, span[0], pieces), in_specs=[...  2.35 us
    pallas_call x1, Pallas kernels, banded(): pl.pallas_call(band_kernel, in_specs=[SMEM, VMEM], out_specs=VMEM, out_sh...  2.17 us
    pallas_call x1, Pallas kernels, last_part(): pl.pallas_call(functools.partial(last_kernel, begin, column), in_specs=[S...  1.72 us
    unnamed x14, local copies, waits for them, and re-layouts  1.25 us
    slice x1, local copies, waits for them, and re-layouts, local(): low = t_now[:, :width].astype(jnp.bfloat16)  1.07 us
  transfers between devices with their start and end apart: 9, of which 7 were waited for; matrix products, arithmetic and copies ran while one was open for 0% of the time, Pallas kernels for 16%

profile of v4, /device:TPU:0, one launch (start us, length us, event | category | flops | bytes accessed | tf_op | source)
XLA Modules:
  0.0 52.2 jit_solution(6606386003580501348)
XLA Ops:
  0.6 0.0 copy-start.6
  0.6 1.1 %slice.7.here_ref = bf16[512,256]{1,0:T(8,128)(2,1)S(1)} slice(f32[512,512]{1,0:T(8,128)} %now_ref.2), slice={[0:512], [0:256]} | slice | bytes 524288 | tf_op jit(solution)/shard_map/slice | solution.py:279
  1.7 3.1 %collective-permute-start.1 = (bf16[512,256]{1,0:T(8,128)(2,1)S(1)}, bf16[512,256]{1,0:T(8,128)(2,1)S(1)}, u32[]{:S(2)}, u32[]{:S(2)}) collective-permute-start(bf16[512,256]{1,0:T(8,128)(2,1)S(1)} %slice.7.here_ref), channel_id=1, source_target_pairs={{12,0},{5,1},{0,4},{9,5},{4,8},{13,9},{8,12},{1,13},{14,2},{7,3},{... | collective-permute-start | bytes 786440 | tf_op jit(solution)/shard_map/ppermute | solution.py:28
  4.8 2.1 %collective-permute-start = (bf16[512,256]{1,0:T(8,128)(2,1)S(1)}, bf16[512,256]{1,0:T(8,128)(2,1)S(1)}, u32[]{:S(2)}, u32[]{:S(2)}) collective-permute-start(bf16[512,256]{1,0:T(8,128)(2,1)S(1)} %slice.7.here_ref), channel_id=1, source_target_pairs={{4,0},{13,1},{8,4},{1,5},{12,8},{5,9},{0,12},{9,13},{6,2},{15,3},{... | collective-permute-start | bytes 786440 | tf_op jit(solution)/shard_map/ppermute | solution.py:28
  6.9 0.0 copy-start
  6.9 1.2 %copy-done = f32[512,512]{1,0:T(8,128)S(1)} copy-done((f32[512,512]{1,0:T(8,128)S(1)}, f32[512,512]{1,0:T(8,128)}, u32[]{:S(2)}) %copy-start) | copy-done | bytes 1048600
  8.1 0.0 copy-start.3
  8.2 0.0 copy-start.2
  8.2 0.0 copy-start.4
  8.2 0.1 collective-permute-start.5
  8.2 3.8 %collective-permute-start.4 = (bf16[512,256]{1,0:T(8,128)(2,1)S(1)}, bf16[512,256]{1,0:T(8,128)(2,1)S(1)}, u32[]{:S(2)}, u32[]{:S(2)}) collective-permute-start(bf16[512,256]{1,0:T(8,128)(2,1)S(1)} %round_part.1.here_ref), channel_id=1, source_target_pairs={{4,0},{13,1},{8,4},{1,5},{12,8},{5,9},{0,12},{9,13},{6,2},{15,3},{... | collective-permute-start | bytes 786440 | tf_op jit(solution)/shard_map/ppermute | solution.py:28
  12.1 0.0 copy-done.6
  12.1 0.0 copy-done.3
  12.1 2.2 %band.1.band_ref = bf16[512,1536]{1,0:T(8,128)(2,1)S(1)} custom-call(s32[8,16]{1,0:T(8,128)S(1)} %copy-done.6, bf16[8,64,1024]{2,1,0:T(8,128)(2,1)S(1)} %copy-done.3), custom_call_target="tpu_custom_call" | custom-call | flops 6291456 | bytes 2621440 | tf_op jit(solution)/shard_map/band/pallas_call | solution.py:92
  14.2 0.0 collective-permute-done.1.first_ref
  14.2 4.3 %collective-permute-done.second_ref = bf16[512,256]{1,0:T(8,128)(2,1)S(1)} collective-permute-done((bf16[512,256]{1,0:T(8,128)(2,1)S(1)}, bf16[512,256]{1,0:T(8,128)(2,1)S(1)}, u32[]{:S(2)}, u32[]{:S(2)}) %collective-permute-start) | collective-permute-done | bytes 262176 | tf_op jit(solution)/shard_map/ppermute | solution.py:28
  18.6 0.0 copy-done.2
  18.6 0.0 copy-done.4
  18.6 1.2 %mid_part.2 = (f32[512,256]{1,0:T(8,128)S(1)}, bf16[512,256]{1,0:T(8,128)(2,1)S(1)}) custom-call(s32[8,8]{1,0:T(8,128)S(1)} %copy-done.4, bf16[512,1536]{1,0:T(8,128)(2,1)S(1)} %band.1.band_ref, bf16[512,256]{1,0:T(8,128)(2,1)S(1)} %slice.7.here_ref, bf16[512,256]{1,0:T(8,128)(2,1)S(1)} %collective-permute-done.second_ref, ...), custom_call_target="tpu_custom_call" | custom-call | flops 402653184 | bytes 3670016 | tf_op jit(solution)/shard_map/mid_part/pallas_call | solution.py:150
  19.7 2.8 %collective-permute-start.3 = (bf16[512,256]{1,0:T(8,128)(2,1)S(1)}, bf16[512,256]{1,0:T(8,128)(2,1)S(1)}, u32[]{:S(2)}, u32[]{:S(2)}) collective-permute-start(bf16[512,256]{1,0:T(8,128)(2,1)S(1)} %get-tuple-element.24.here_ref), channel_id=1, source_target_pairs={{12,0},{5,1},{0,4},{9,5},{4,8},{13,9},{8,12},{1,13},{14,2},{7,3},{... | collective-permute-start | bytes 786440 | tf_op jit(solution)/shard_map/ppermute | solution.py:28
  22.5 1.1 %collective-permute-start.2 = (bf16[512,256]{1,0:T(8,128)(2,1)S(1)}, bf16[512,256]{1,0:T(8,128)(2,1)S(1)}, u32[]{:S(2)}, u32[]{:S(2)}) collective-permute-start(bf16[512,256]{1,0:T(8,128)(2,1)S(1)} %get-tuple-element.24.here_ref), channel_id=1, source_target_pairs={{4,0},{13,1},{8,4},{1,5},{12,8},{5,9},{0,12},{9,13},{6,2},{15,3},{... | collective-permute-start | bytes 786440 | tf_op jit(solution)/shard_map/ppermute | solution.py:28
  23.6 1.7 %collective-permute-done.5.first_ref = bf16[512,256]{1,0:T(8,128)(2,1)S(1)} collective-permute-done((bf16[512,256]{1,0:T(8,128)(2,1)S(1)}, bf16[512,256]{1,0:T(8,128)(2,1)S(1)}, u32[]{:S(2)}, u32[]{:S(2)}) %collective-permute-start.5) | collective-permute-done | bytes 262176 | tf_op jit(solution)/shard_map/ppermute | solution.py:28
  25.3 3.6 %collective-permute-done.4.second_ref = bf16[512,256]{1,0:T(8,128)(2,1)S(1)} collective-permute-done((bf16[512,256]{1,0:T(8,128)(2,1)S(1)}, bf16[512,256]{1,0:T(8,128)(2,1)S(1)}, u32[]{:S(2)}, u32[]{:S(2)}) %collective-permute-start.4) | collective-permute-done | bytes 262176 | tf_op jit(solution)/shard_map/ppermute | solution.py:28
  28.9 0.0 copy-start.1
  28.9 0.0 copy-start.5
  28.9 1.2 %mid_part.3 = (f32[512,256]{1,0:T(8,128)S(1)}, bf16[512,256]{1,0:T(8,128)(2,1)S(1)}, bf16[512,128]{1,0:T(8,128)(2,1)S(1)}, bf16[512,128]{1,0:T(8,128)(2,1)S(1)}) custom-call(s32[8,8]{1,0:T(8,128)S(1)} %copy-done.4, bf16[512,1536]{1,0:T(8,128)(2,1)S(1)} %band.1.band_ref, bf16[512,256]{1,0:T(8,128)(2,1)S(1)} %round_part.1.here_ref, ...), custom_call_target="tpu_custom_call" | custom-call | flops 402653184 | bytes 3670016 | tf_op jit(solution)/shard_map/mid_part/pallas_call | solution.py:150
  30.1 2.6 %collective-permute-start.7 = (bf16[512,256]{1,0:T(8,128)(2,1)S(1)}, bf16[512,256]{1,0:T(8,128)(2,1)S(1)}, u32[]{:S(2)}, u32[]{:S(2)}) collective-permute-start(bf16[512,256]{1,0:T(8,128)(2,1)S(1)} %get-tuple-element.30.here_ref), channel_id=1, source_target_pairs={{12,0},{13,1},{0,4},{1,5},{4,8},{5,9},{8,12},{9,13},{14,2},{15,3},... | collective-permute-start | bytes 786440 | tf_op jit(solution)/shard_map/ppermute | solution.py:28
  32.7 1.5 %collective-permute-start.8 = (bf16[512,128]{1,0:T(8,128)(2,1)S(1)}, bf16[512,128]{1,0:T(8,128)(2,1)S(1)}, u32[]{:S(2)}, u32[]{:S(2)}) collective-permute-start(bf16[512,128]{1,0:T(8,128)(2,1)S(1)} %get-tuple-element.32), channel_id=1, source_target_pairs={{4,0},{5,1},{8,4},{9,5},{12,8},{13,9},{0,12},{1,13},{6,2},{7,3},{1... | collective-permute-start | bytes 393224 | tf_op jit(solution)/shard_map/ppermute | solution.py:28
  34.2 2.0 %collective-permute-start.6 = (bf16[512,128]{1,0:T(8,128)(2,1)S(1)}, bf16[512,128]{1,0:T(8,128)(2,1)S(1)}, u32[]{:S(2)}, u32[]{:S(2)}) collective-permute-start(bf16[512,128]{1,0:T(8,128)(2,1)S(1)} %get-tuple-element.29), channel_id=1, source_target_pairs={{4,0},{5,1},{8,4},{9,5},{12,8},{13,9},{0,12},{1,13},{6,2},{7,3},{1... | collective-permute-start | bytes 393224 | tf_op jit(solution)/shard_map/ppermute | solution.py:28
  36.1 0.5 collective-permute-done.3.first_ref
  36.6 2.2 %collective-permute-done.2.second_ref = bf16[512,256]{1,0:T(8,128)(2,1)S(1)} collective-permute-done((bf16[512,256]{1,0:T(8,128)(2,1)S(1)}, bf16[512,256]{1,0:T(8,128)(2,1)S(1)}, u32[]{:S(2)}, u32[]{:S(2)}) %collective-permute-start.2) | collective-permute-done | bytes 262176 | tf_op jit(solution)/shard_map/ppermute | solution.py:28
  38.8 0.0 copy-done.1
  38.8 0.0 copy-done.5
  38.8 2.4 %next_part.1 = (f32[512,512]{1,0:T(8,128)}, f32[512,512]{1,0:T(8,128)}, f32[512,512]{1,0:T(8,128)}, f32[8,128]{1,0:T(8,128)S(1)}) custom-call(s32[8,8]{1,0:T(8,128)S(1)} %copy-done.4, f32[2]{0:T(128)S(1)} %copy-done.5, bf16[512,1536]{1,0:T(8,128)(2,1)S(1)} %band.1.band_ref, bf16[512,256]{1,0:T(8,128)(2,1)S(1)} %get-tuple-element.24.here_ref, ...), custom_call_target="tpu_custom_call" | custom-call | flops 402653184 | bytes 5505024 | tf_op jit(solution)/shard_map/next_part/pallas_call | solution.py:182
  41.3 6.5 %collective-permute-done.7.first_ref = bf16[512,256]{1,0:T(8,128)(2,1)S(1)} collective-permute-done((bf16[512,256]{1,0:T(8,128)(2,1)S(1)}, bf16[512,256]{1,0:T(8,128)(2,1)S(1)}, u32[]{:S(2)}, u32[]{:S(2)}) %collective-permute-start.7) | collective-permute-done | bytes 262176 | tf_op jit(solution)/shard_map/ppermute | solution.py:28
  47.7 0.4 begun_part.1.sums_ref
  48.2 0.0 collective-permute-done.8.second_ref
  48.2 0.9 %piece_part.1 = (f32[512,128]{1,0:T(8,128)S(1)}, f32[512,128]{1,0:T(8,128)S(1)}) custom-call(s32[8,8]{1,0:T(8,128)S(1)} %copy-done.4, f32[2]{0:T(128)S(1)} %copy-done.5, bf16[512,1536]{1,0:T(8,128)(2,1)S(1)} %band.1.band_ref, bf16[512,128]{1,0:T(8,128)(2,1)S(1)} %collective-permute-done.8.second_ref, f32[512,256]{1,0:T(8,128)S(1)} %begun_part.1.sums_ref, ...), custom_call_target="tpu_custom_call" | custom-call | flops 67108864 | bytes 1966080 | tf_op jit(solution)/shard_map/piece_part/pallas_call | solution.py:223
  49.1 1.4 %collective-permute-done.6.second_ref = bf16[512,128]{1,0:T(8,128)(2,1)S(1)} collective-permute-done((bf16[512,128]{1,0:T(8,128)(2,1)S(1)}, bf16[512,128]{1,0:T(8,128)(2,1)S(1)}, u32[]{:S(2)}, u32[]{:S(2)}) %collective-permute-start.6) | collective-permute-done | bytes 131104 | tf_op jit(solution)/shard_map/ppermute | solution.py:28
  50.5 1.7 %last_part.1 = (f32[512,512]{1,0:T(8,128)}, f32[512,512]{1,0:T(8,128)}) custom-call(s32[8,8]{1,0:T(8,128)S(1)} %copy-done.4, f32[2]{0:T(128)S(1)} %copy-done.5, bf16[512,1536]{1,0:T(8,128)(2,1)S(1)} %band.1.band_ref, bf16[512,128]{1,0:T(8,128)(2,1)S(1)} %collective-permute-done.6.second_ref, ...), custom_call_target="tpu_custom_call", output_to_operand_aliasing={{0}: (8, {}), {1}: (9, {})} | custom-call | flops 67108864 | bytes 1966080 | tf_op jit(solution)/shard_map/last_part/pallas_call | solution.py:264
  (1 shorter events, 0.0 us)
Async XLA Ops:
  0.6 11.4 %copy-start.6 = (s32[8,16]{1,0:T(8,128)S(1)}, s32[8,16]{1,0:T(8,128)}, u32[]{:S(2)}) copy-start(s32[8,16]{1,0:T(8,128)} %slots_ref.1) | copy-start | bytes 1540
  1.7 12.5 %collective-permute-start.1 = (bf16[512,256]{1,0:T(8,128)(2,1)S(1)}, bf16[512,256]{1,0:T(8,128)(2,1)S(1)}, u32[]{:S(2)}, u32[]{:S(2)}) collective-permute-start(bf16[512,256]{1,0:T(8,128)(2,1)S(1)} %slice.7.here_ref), channel_id=1, source_target_pairs={{12,0},{5,1},{0,4},{9,5},{4,8},{13,9},{8,12},{1,13},{14,2},{7,3},{... | collective-permute-start | bytes 786440 | tf_op jit(solution)/shard_map/ppermute | solution.py:28
  4.8 13.8 %collective-permute-start = (bf16[512,256]{1,0:T(8,128)(2,1)S(1)}, bf16[512,256]{1,0:T(8,128)(2,1)S(1)}, u32[]{:S(2)}, u32[]{:S(2)}) collective-permute-start(bf16[512,256]{1,0:T(8,128)(2,1)S(1)} %slice.7.here_ref), channel_id=1, source_target_pairs={{4,0},{13,1},{8,4},{1,5},{12,8},{5,9},{0,12},{9,13},{6,2},{15,3},{... | collective-permute-start | bytes 786440 | tf_op jit(solution)/shard_map/ppermute | solution.py:28
  6.9 1.2 %copy-start = (f32[512,512]{1,0:T(8,128)S(1)}, f32[512,512]{1,0:T(8,128)}, u32[]{:S(2)}) copy-start(f32[512,512]{1,0:T(8,128)} %now_ref.2) | copy-start | bytes 3145732
  8.1 3.9 %copy-start.3 = (bf16[8,64,1024]{2,1,0:T(8,128)(2,1)S(1)}, bf16[8,64,1024]{2,1,0:T(8,128)(2,1)}, u32[]{:S(2)}) copy-start(bf16[8,64,1024]{2,1,0:T(8,128)(2,1)} %strips_ref) | copy-start | bytes 3145732
  8.2 10.4 %copy-start.2 = (f32[512,512]{1,0:T(8,128)S(1)}, f32[512,512]{1,0:T(8,128)}, u32[]{:S(2)}) copy-start(f32[512,512]{1,0:T(8,128)} %prev_ref.1) | copy-start | bytes 3145732
  8.2 10.4 %copy-start.4 = (s32[8,8]{1,0:T(8,128)S(1)}, s32[8,8]{1,0:T(8,128)}, u32[]{:S(2)}) copy-start(s32[8,8]{1,0:T(8,128)} %mask_ref.9) | copy-start | bytes 772
  8.2 17.1 %collective-permute-start.5 = (bf16[512,256]{1,0:T(8,128)(2,1)S(1)}, bf16[512,256]{1,0:T(8,128)(2,1)S(1)}, u32[]{:S(2)}, u32[]{:S(2)}) collective-permute-start(bf16[512,256]{1,0:T(8,128)(2,1)S(1)} %round_part.1.here_ref), channel_id=1, source_target_pairs={{12,0},{5,1},{0,4},{9,5},{4,8},{13,9},{8,12},{1,13},{14,2},{7,3},{... | collective-permute-start | bytes 786440 | tf_op jit(solution)/shard_map/ppermute | solution.py:28
  8.2 20.7 %collective-permute-start.4 = (bf16[512,256]{1,0:T(8,128)(2,1)S(1)}, bf16[512,256]{1,0:T(8,128)(2,1)S(1)}, u32[]{:S(2)}, u32[]{:S(2)}) collective-permute-start(bf16[512,256]{1,0:T(8,128)(2,1)S(1)} %round_part.1.here_ref), channel_id=1, source_target_pairs={{4,0},{13,1},{8,4},{1,5},{12,8},{5,9},{0,12},{9,13},{6,2},{15,3},{... | collective-permute-start | bytes 786440 | tf_op jit(solution)/shard_map/ppermute | solution.py:28
  19.7 16.9 %collective-permute-start.3 = (bf16[512,256]{1,0:T(8,128)(2,1)S(1)}, bf16[512,256]{1,0:T(8,128)(2,1)S(1)}, u32[]{:S(2)}, u32[]{:S(2)}) collective-permute-start(bf16[512,256]{1,0:T(8,128)(2,1)S(1)} %get-tuple-element.24.here_ref), channel_id=1, source_target_pairs={{12,0},{5,1},{0,4},{9,5},{4,8},{13,9},{8,12},{1,13},{14,2},{7,3},{... | collective-permute-start | bytes 786440 | tf_op jit(solution)/shard_map/ppermute | solution.py:28
  22.5 16.3 %collective-permute-start.2 = (bf16[512,256]{1,0:T(8,128)(2,1)S(1)}, bf16[512,256]{1,0:T(8,128)(2,1)S(1)}, u32[]{:S(2)}, u32[]{:S(2)}) collective-permute-start(bf16[512,256]{1,0:T(8,128)(2,1)S(1)} %get-tuple-element.24.here_ref), channel_id=1, source_target_pairs={{4,0},{13,1},{8,4},{1,5},{12,8},{5,9},{0,12},{9,13},{6,2},{15,3},{... | collective-permute-start | bytes 786440 | tf_op jit(solution)/shard_map/ppermute | solution.py:28
  28.9 9.9 %copy-start.1 = (f32[512,512]{1,0:T(8,128)S(1)}, f32[512,512]{1,0:T(8,128)}, u32[]{:S(2)}) copy-start(f32[512,512]{1,0:T(8,128)} %now_ref.2) | copy-start | bytes 3145732
  28.9 9.9 %copy-start.5 = (f32[2]{0:T(128)S(1)}, f32[2]{0:T(128)}, u32[]{:S(2)}) copy-start(f32[2]{0:T(128)} %coeffs_ref.5) | copy-start | bytes 28
  30.1 17.6 %collective-permute-start.7 = (bf16[512,256]{1,0:T(8,128)(2,1)S(1)}, bf16[512,256]{1,0:T(8,128)(2,1)S(1)}, u32[]{:S(2)}, u32[]{:S(2)}) collective-permute-start(bf16[512,256]{1,0:T(8,128)(2,1)S(1)} %get-tuple-element.30.here_ref), channel_id=1, source_target_pairs={{12,0},{13,1},{0,4},{1,5},{4,8},{5,9},{8,12},{9,13},{14,2},{15,3},... | collective-permute-start | bytes 786440 | tf_op jit(solution)/shard_map/ppermute | solution.py:28
  32.7 15.5 %collective-permute-start.8 = (bf16[512,128]{1,0:T(8,128)(2,1)S(1)}, bf16[512,128]{1,0:T(8,128)(2,1)S(1)}, u32[]{:S(2)}, u32[]{:S(2)}) collective-permute-start(bf16[512,128]{1,0:T(8,128)(2,1)S(1)} %get-tuple-element.32), channel_id=1, source_target_pairs={{4,0},{5,1},{8,4},{9,5},{12,8},{13,9},{0,12},{1,13},{6,2},{7,3},{1... | collective-permute-start | bytes 393224 | tf_op jit(solution)/shard_map/ppermute | solution.py:28
  34.2 16.3 %collective-permute-start.6 = (bf16[512,128]{1,0:T(8,128)(2,1)S(1)}, bf16[512,128]{1,0:T(8,128)(2,1)S(1)}, u32[]{:S(2)}, u32[]{:S(2)}) collective-permute-start(bf16[512,128]{1,0:T(8,128)(2,1)S(1)} %get-tuple-element.29), channel_id=1, source_target_pairs={{4,0},{5,1},{8,4},{9,5},{12,8},{13,9},{0,12},{1,13},{6,2},{7,3},{1... | collective-permute-start | bytes 393224 | tf_op jit(solution)/shard_map/ppermute | solution.py:28

commit v5 on v0

--- a/solution.py
+++ b/solution.py
@@ -8,7 +8,7 @@
 from jax.sharding import PartitionSpec as P
 
 LANES = 128
-CHUNKS = 2
+CHUNKS = 4
 MIB = 1024 * 1024
 
 SMEM = pl.BlockSpec(memory_space=pltpu.SMEM)

time: 52.4 us -> 52.4 us (level)
  no operation moved by 1% of the time
where the time goes in v5:
time: 52.4 us; the launch traced here: 52.1 us
  waiting for transfers between devices  19.4 us (37%)
  starting transfers between devices  18.9 us (36%)
  Pallas kernels  10.7 us (20%)
  local copies, waits for them, and re-layouts  2.33 us (4%)
  between operations  0.74 us (1%)
    ppermute x9, waiting for transfers between devices, from_side(): return lax.ppermute(block, ('row', 'rep'), route)  19.4 us
    ppermute x9, starting transfers between devices, from_side(): return lax.ppermute(block, ('row', 'rep'), route)  18.9 us
    pallas_call x2, Pallas kernels, last_part(): pl.pallas_call(functools.partial(last_kernel, begin, column), in_specs=[S...  3.28 us
    pallas_call x1, Pallas kernels, next_part(): pl.pallas_call(next_kernel, in_specs=[SMEM] * 2 + [VMEM] * 7, out_specs=[...  2.44 us
    pallas_call x2, Pallas kernels, mid_part(): pl.pallas_call(functools.partial(mid_kernel, span[0], pieces), in_specs=[...  2.35 us
    pallas_call x1, Pallas kernels, banded(): pl.pallas_call(band_kernel, in_specs=[SMEM, VMEM], out_specs=VMEM, out_sh...  2.17 us
    unnamed x14, local copies, waits for them, and re-layouts  1.25 us
    slice x1, local copies, waits for them, and re-layouts, local(): low = t_now[:, :width].astype(jnp.bfloat16)  1.07 us
  transfers between devices with their start and end apart: 9, of which 7 were waited for; matrix products, arithmetic and copies ran while one was open for 0% of the time, Pallas kernels for 17%

profile of v5, /device:TPU:0, one launch (start us, length us, event | category | flops | bytes accessed | tf_op | source)
XLA Modules:
  0.0 52.1 jit_solution(17493087841239121675)
XLA Ops:
  0.6 0.0 copy-start.6
  0.6 1.1 %slice.7.here_ref = bf16[512,256]{1,0:T(8,128)(2,1)S(1)} slice(f32[512,512]{1,0:T(8,128)} %now_ref.2), slice={[0:512], [0:256]} | slice | bytes 524288 | tf_op jit(solution)/shard_map/slice | solution.py:254
  1.7 3.1 %collective-permute-start.1 = (bf16[512,256]{1,0:T(8,128)(2,1)S(1)}, bf16[512,256]{1,0:T(8,128)(2,1)S(1)}, u32[]{:S(2)}, u32[]{:S(2)}) collective-permute-start(bf16[512,256]{1,0:T(8,128)(2,1)S(1)} %slice.7.here_ref), channel_id=1, source_target_pairs={{12,0},{5,1},{0,4},{9,5},{4,8},{13,9},{8,12},{1,13},{14,2},{7,3},{... | collective-permute-start | bytes 786440 | tf_op jit(solution)/shard_map/ppermute | solution.py:28
  4.8 2.1 %collective-permute-start = (bf16[512,256]{1,0:T(8,128)(2,1)S(1)}, bf16[512,256]{1,0:T(8,128)(2,1)S(1)}, u32[]{:S(2)}, u32[]{:S(2)}) collective-permute-start(bf16[512,256]{1,0:T(8,128)(2,1)S(1)} %slice.7.here_ref), channel_id=1, source_target_pairs={{4,0},{13,1},{8,4},{1,5},{12,8},{5,9},{0,12},{9,13},{6,2},{15,3},{... | collective-permute-start | bytes 786440 | tf_op jit(solution)/shard_map/ppermute | solution.py:28
  6.9 0.0 copy-start
  6.9 1.2 %copy-done = f32[512,512]{1,0:T(8,128)S(1)} copy-done((f32[512,512]{1,0:T(8,128)S(1)}, f32[512,512]{1,0:T(8,128)}, u32[]{:S(2)}) %copy-start) | copy-done | bytes 1048600
  8.1 0.0 copy-start.3
  8.2 0.0 copy-start.2
  8.2 0.0 copy-start.4
  8.2 0.1 collective-permute-start.5
  8.2 3.8 %collective-permute-start.4 = (bf16[512,256]{1,0:T(8,128)(2,1)S(1)}, bf16[512,256]{1,0:T(8,128)(2,1)S(1)}, u32[]{:S(2)}, u32[]{:S(2)}) collective-permute-start(bf16[512,256]{1,0:T(8,128)(2,1)S(1)} %round_part.1.here_ref), channel_id=1, source_target_pairs={{4,0},{13,1},{8,4},{1,5},{12,8},{5,9},{0,12},{9,13},{6,2},{15,3},{... | collective-permute-start | bytes 786440 | tf_op jit(solution)/shard_map/ppermute | solution.py:28
  12.1 0.0 copy-done.6
  12.1 0.0 copy-done.3
  12.1 2.2 %band.1.band_ref = bf16[512,1536]{1,0:T(8,128)(2,1)S(1)} custom-call(s32[8,16]{1,0:T(8,128)S(1)} %copy-done.6, bf16[8,64,1024]{2,1,0:T(8,128)(2,1)S(1)} %copy-done.3), custom_call_target="tpu_custom_call" | custom-call | flops 6291456 | bytes 2621440 | tf_op jit(solution)/shard_map/band/pallas_call | solution.py:92
  14.2 0.0 collective-permute-done.1.first_ref
  14.2 4.3 %collective-permute-done.second_ref = bf16[512,256]{1,0:T(8,128)(2,1)S(1)} collective-permute-done((bf16[512,256]{1,0:T(8,128)(2,1)S(1)}, bf16[512,256]{1,0:T(8,128)(2,1)S(1)}, u32[]{:S(2)}, u32[]{:S(2)}) %collective-permute-start) | collective-permute-done | bytes 262176 | tf_op jit(solution)/shard_map/ppermute | solution.py:28
  18.6 0.0 copy-done.2
  18.6 0.0 copy-done.4
  18.6 1.2 %mid_part.2 = (f32[512,256]{1,0:T(8,128)S(1)}, bf16[512,256]{1,0:T(8,128)(2,1)S(1)}) custom-call(s32[8,8]{1,0:T(8,128)S(1)} %copy-done.4, bf16[512,1536]{1,0:T(8,128)(2,1)S(1)} %band.1.band_ref, bf16[512,256]{1,0:T(8,128)(2,1)S(1)} %slice.7.here_ref, bf16[512,256]{1,0:T(8,128)(2,1)S(1)} %collective-permute-done.second_ref, ...), custom_call_target="tpu_custom_call" | custom-call | flops 402653184 | bytes 3670016 | tf_op jit(solution)/shard_map/mid_part/pallas_call | solution.py:150
  19.7 2.8 %collective-permute-start.3 = (bf16[512,256]{1,0:T(8,128)(2,1)S(1)}, bf16[512,256]{1,0:T(8,128)(2,1)S(1)}, u32[]{:S(2)}, u32[]{:S(2)}) collective-permute-start(bf16[512,256]{1,0:T(8,128)(2,1)S(1)} %get-tuple-element.24.here_ref), channel_id=1, source_target_pairs={{12,0},{5,1},{0,4},{9,5},{4,8},{13,9},{8,12},{1,13},{14,2},{7,3},{... | collective-permute-start | bytes 786440 | tf_op jit(solution)/shard_map/ppermute | solution.py:28
  22.5 1.1 %collective-permute-start.2 = (bf16[512,256]{1,0:T(8,128)(2,1)S(1)}, bf16[512,256]{1,0:T(8,128)(2,1)S(1)}, u32[]{:S(2)}, u32[]{:S(2)}) collective-permute-start(bf16[512,256]{1,0:T(8,128)(2,1)S(1)} %get-tuple-element.24.here_ref), channel_id=1, source_target_pairs={{4,0},{13,1},{8,4},{1,5},{12,8},{5,9},{0,12},{9,13},{6,2},{15,3},{... | collective-permute-start | bytes 786440 | tf_op jit(solution)/shard_map/ppermute | solution.py:28
  23.6 1.7 %collective-permute-done.5.first_ref = bf16[512,256]{1,0:T(8,128)(2,1)S(1)} collective-permute-done((bf16[512,256]{1,0:T(8,128)(2,1)S(1)}, bf16[512,256]{1,0:T(8,128)(2,1)S(1)}, u32[]{:S(2)}, u32[]{:S(2)}) %collective-permute-start.5) | collective-permute-done | bytes 262176 | tf_op jit(solution)/shard_map/ppermute | solution.py:28
  25.3 3.6 %collective-permute-done.4.second_ref = bf16[512,256]{1,0:T(8,128)(2,1)S(1)} collective-permute-done((bf16[512,256]{1,0:T(8,128)(2,1)S(1)}, bf16[512,256]{1,0:T(8,128)(2,1)S(1)}, u32[]{:S(2)}, u32[]{:S(2)}) %collective-permute-start.4) | collective-permute-done | bytes 262176 | tf_op jit(solution)/shard_map/ppermute | solution.py:28
  28.9 0.0 copy-start.1
  28.9 0.0 copy-start.5
  28.9 1.2 %mid_part.3 = (f32[512,256]{1,0:T(8,128)S(1)}, bf16[512,256]{1,0:T(8,128)(2,1)S(1)}, bf16[512,128]{1,0:T(8,128)(2,1)S(1)}, bf16[512,128]{1,0:T(8,128)(2,1)S(1)}) custom-call(s32[8,8]{1,0:T(8,128)S(1)} %copy-done.4, bf16[512,1536]{1,0:T(8,128)(2,1)S(1)} %band.1.band_ref, bf16[512,256]{1,0:T(8,128)(2,1)S(1)} %round_part.1.here_ref, ...), custom_call_target="tpu_custom_call" | custom-call | flops 402653184 | bytes 3670016 | tf_op jit(solution)/shard_map/mid_part/pallas_call | solution.py:150
  30.1 2.6 %collective-permute-start.7 = (bf16[512,256]{1,0:T(8,128)(2,1)S(1)}, bf16[512,256]{1,0:T(8,128)(2,1)S(1)}, u32[]{:S(2)}, u32[]{:S(2)}) collective-permute-start(bf16[512,256]{1,0:T(8,128)(2,1)S(1)} %get-tuple-element.30.here_ref), channel_id=1, source_target_pairs={{12,0},{13,1},{0,4},{1,5},{4,8},{5,9},{8,12},{9,13},{14,2},{15,3},... | collective-permute-start | bytes 786440 | tf_op jit(solution)/shard_map/ppermute | solution.py:28
  32.7 1.5 %collective-permute-start.8 = (bf16[512,128]{1,0:T(8,128)(2,1)S(1)}, bf16[512,128]{1,0:T(8,128)(2,1)S(1)}, u32[]{:S(2)}, u32[]{:S(2)}) collective-permute-start(bf16[512,128]{1,0:T(8,128)(2,1)S(1)} %get-tuple-element.32), channel_id=1, source_target_pairs={{4,0},{5,1},{8,4},{9,5},{12,8},{13,9},{0,12},{1,13},{6,2},{7,3},{1... | collective-permute-start | bytes 393224 | tf_op jit(solution)/shard_map/ppermute | solution.py:28
  34.2 2.0 %collective-permute-start.6 = (bf16[512,128]{1,0:T(8,128)(2,1)S(1)}, bf16[512,128]{1,0:T(8,128)(2,1)S(1)}, u32[]{:S(2)}, u32[]{:S(2)}) collective-permute-start(bf16[512,128]{1,0:T(8,128)(2,1)S(1)} %get-tuple-element.29), channel_id=1, source_target_pairs={{4,0},{5,1},{8,4},{9,5},{12,8},{13,9},{0,12},{1,13},{6,2},{7,3},{1... | collective-permute-start | bytes 393224 | tf_op jit(solution)/shard_map/ppermute | solution.py:28
  36.1 0.5 collective-permute-done.3.first_ref
  36.6 2.2 %collective-permute-done.2.second_ref = bf16[512,256]{1,0:T(8,128)(2,1)S(1)} collective-permute-done((bf16[512,256]{1,0:T(8,128)(2,1)S(1)}, bf16[512,256]{1,0:T(8,128)(2,1)S(1)}, u32[]{:S(2)}, u32[]{:S(2)}) %collective-permute-start.2) | collective-permute-done | bytes 262176 | tf_op jit(solution)/shard_map/ppermute | solution.py:28
  38.8 0.0 copy-done.1
  38.8 0.0 copy-done.5
  38.8 2.4 %next_part.1 = (f32[512,512]{1,0:T(8,128)}, f32[512,512]{1,0:T(8,128)}, f32[512,512]{1,0:T(8,128)}, f32[8,128]{1,0:T(8,128)S(1)}) custom-call(s32[8,8]{1,0:T(8,128)S(1)} %copy-done.4, f32[2]{0:T(128)S(1)} %copy-done.5, bf16[512,1536]{1,0:T(8,128)(2,1)S(1)} %band.1.band_ref, bf16[512,256]{1,0:T(8,128)(2,1)S(1)} %get-tuple-element.24.here_ref, ...), custom_call_target="tpu_custom_call" | custom-call | flops 402653184 | bytes 5505024 | tf_op jit(solution)/shard_map/next_part/pallas_call | solution.py:182
  41.3 6.5 %collective-permute-done.7.first_ref = bf16[512,256]{1,0:T(8,128)(2,1)S(1)} collective-permute-done((bf16[512,256]{1,0:T(8,128)(2,1)S(1)}, bf16[512,256]{1,0:T(8,128)(2,1)S(1)}, u32[]{:S(2)}, u32[]{:S(2)}) %collective-permute-start.7) | collective-permute-done | bytes 262176 | tf_op jit(solution)/shard_map/ppermute | solution.py:28
  47.7 0.4 begun_part.1.sums_ref
  48.2 0.0 collective-permute-done.8.second_ref
  48.2 1.6 %last_part.2 = (f32[512,512]{1,0:T(8,128)}, f32[512,512]{1,0:T(8,128)}) custom-call(s32[8,8]{1,0:T(8,128)S(1)} %copy-done.4, f32[2]{0:T(128)S(1)} %copy-done.5, bf16[512,1536]{1,0:T(8,128)(2,1)S(1)} %band.1.band_ref, bf16[512,128]{1,0:T(8,128)(2,1)S(1)} %collective-permute-done.8.second_ref, ...), custom_call_target="tpu_custom_call", output_to_operand_aliasing={{0}: (6, {}), {1}: (7, {})} | custom-call | flops 67108864 | bytes 1966080 | tf_op jit(solution)/shard_map/last_part/pallas_call | solution.py:239
  49.8 0.6 %collective-permute-done.6.second_ref = bf16[512,128]{1,0:T(8,128)(2,1)S(1)} collective-permute-done((bf16[512,128]{1,0:T(8,128)(2,1)S(1)}, bf16[512,128]{1,0:T(8,128)(2,1)S(1)}, u32[]{:S(2)}, u32[]{:S(2)}) %collective-permute-start.6) | collective-permute-done | bytes 131104 | tf_op jit(solution)/shard_map/ppermute | solution.py:28
  50.5 1.6 %last_part.3 = (f32[512,512]{1,0:T(8,128)}, f32[512,512]{1,0:T(8,128)}) custom-call(s32[8,8]{1,0:T(8,128)S(1)} %copy-done.4, f32[2]{0:T(128)S(1)} %copy-done.5, bf16[512,1536]{1,0:T(8,128)(2,1)S(1)} %band.1.band_ref, bf16[512,128]{1,0:T(8,128)(2,1)S(1)} %collective-permute-done.6.second_ref, ...), custom_call_target="tpu_custom_call", output_to_operand_aliasing={{0}: (6, {}), {1}: (7, {})} | custom-call | flops 67108864 | bytes 1966080 | tf_op jit(solution)/shard_map/last_part/pallas_call | solution.py:239
  (1 shorter events, 0.0 us)
Async XLA Ops:
  0.6 11.4 %copy-start.6 = (s32[8,16]{1,0:T(8,128)S(1)}, s32[8,16]{1,0:T(8,128)}, u32[]{:S(2)}) copy-start(s32[8,16]{1,0:T(8,128)} %slots_ref.1) | copy-start | bytes 1540
  1.7 12.5 %collective-permute-start.1 = (bf16[512,256]{1,0:T(8,128)(2,1)S(1)}, bf16[512,256]{1,0:T(8,128)(2,1)S(1)}, u32[]{:S(2)}, u32[]{:S(2)}) collective-permute-start(bf16[512,256]{1,0:T(8,128)(2,1)S(1)} %slice.7.here_ref), channel_id=1, source_target_pairs={{12,0},{5,1},{0,4},{9,5},{4,8},{13,9},{8,12},{1,13},{14,2},{7,3},{... | collective-permute-start | bytes 786440 | tf_op jit(solution)/shard_map/ppermute | solution.py:28
  4.8 13.8 %collective-permute-start = (bf16[512,256]{1,0:T(8,128)(2,1)S(1)}, bf16[512,256]{1,0:T(8,128)(2,1)S(1)}, u32[]{:S(2)}, u32[]{:S(2)}) collective-permute-start(bf16[512,256]{1,0:T(8,128)(2,1)S(1)} %slice.7.here_ref), channel_id=1, source_target_pairs={{4,0},{13,1},{8,4},{1,5},{12,8},{5,9},{0,12},{9,13},{6,2},{15,3},{... | collective-permute-start | bytes 786440 | tf_op jit(solution)/shard_map/ppermute | solution.py:28
  6.9 1.2 %copy-start = (f32[512,512]{1,0:T(8,128)S(1)}, f32[512,512]{1,0:T(8,128)}, u32[]{:S(2)}) copy-start(f32[512,512]{1,0:T(8,128)} %now_ref.2) | copy-start | bytes 3145732
  8.1 3.9 %copy-start.3 = (bf16[8,64,1024]{2,1,0:T(8,128)(2,1)S(1)}, bf16[8,64,1024]{2,1,0:T(8,128)(2,1)}, u32[]{:S(2)}) copy-start(bf16[8,64,1024]{2,1,0:T(8,128)(2,1)} %strips_ref) | copy-start | bytes 3145732
  8.2 10.4 %copy-start.2 = (f32[512,512]{1,0:T(8,128)S(1)}, f32[512,512]{1,0:T(8,128)}, u32[]{:S(2)}) copy-start(f32[512,512]{1,0:T(8,128)} %prev_ref.1) | copy-start | bytes 3145732
  8.2 10.4 %copy-start.4 = (s32[8,8]{1,0:T(8,128)S(1)}, s32[8,8]{1,0:T(8,128)}, u32[]{:S(2)}) copy-start(s32[8,8]{1,0:T(8,128)} %mask_ref.9) | copy-start | bytes 772
  8.2 17.1 %collective-permute-start.5 = (bf16[512,256]{1,0:T(8,128)(2,1)S(1)}, bf16[512,256]{1,0:T(8,128)(2,1)S(1)}, u32[]{:S(2)}, u32[]{:S(2)}) collective-permute-start(bf16[512,256]{1,0:T(8,128)(2,1)S(1)} %round_part.1.here_ref), channel_id=1, source_target_pairs={{12,0},{5,1},{0,4},{9,5},{4,8},{13,9},{8,12},{1,13},{14,2},{7,3},{... | collective-permute-start | bytes 786440 | tf_op jit(solution)/shard_map/ppermute | solution.py:28
  8.2 20.7 %collective-permute-start.4 = (bf16[512,256]{1,0:T(8,128)(2,1)S(1)}, bf16[512,256]{1,0:T(8,128)(2,1)S(1)}, u32[]{:S(2)}, u32[]{:S(2)}) collective-permute-start(bf16[512,256]{1,0:T(8,128)(2,1)S(1)} %round_part.1.here_ref), channel_id=1, source_target_pairs={{4,0},{13,1},{8,4},{1,5},{12,8},{5,9},{0,12},{9,13},{6,2},{15,3},{... | collective-permute-start | bytes 786440 | tf_op jit(solution)/shard_map/ppermute | solution.py:28
  19.7 16.9 %collective-permute-start.3 = (bf16[512,256]{1,0:T(8,128)(2,1)S(1)}, bf16[512,256]{1,0:T(8,128)(2,1)S(1)}, u32[]{:S(2)}, u32[]{:S(2)}) collective-permute-start(bf16[512,256]{1,0:T(8,128)(2,1)S(1)} %get-tuple-element.24.here_ref), channel_id=1, source_target_pairs={{12,0},{5,1},{0,4},{9,5},{4,8},{13,9},{8,12},{1,13},{14,2},{7,3},{... | collective-permute-start | bytes 786440 | tf_op jit(solution)/shard_map/ppermute | solution.py:28
  22.5 16.3 %collective-permute-start.2 = (bf16[512,256]{1,0:T(8,128)(2,1)S(1)}, bf16[512,256]{1,0:T(8,128)(2,1)S(1)}, u32[]{:S(2)}, u32[]{:S(2)}) collective-permute-start(bf16[512,256]{1,0:T(8,128)(2,1)S(1)} %get-tuple-element.24.here_ref), channel_id=1, source_target_pairs={{4,0},{13,1},{8,4},{1,5},{12,8},{5,9},{0,12},{9,13},{6,2},{15,3},{... | collective-permute-start | bytes 786440 | tf_op jit(solution)/shard_map/ppermute | solution.py:28
  28.9 9.9 %copy-start.1 = (f32[512,512]{1,0:T(8,128)S(1)}, f32[512,512]{1,0:T(8,128)}, u32[]{:S(2)}) copy-start(f32[512,512]{1,0:T(8,128)} %now_ref.2) | copy-start | bytes 3145732
  28.9 9.9 %copy-start.5 = (f32[2]{0:T(128)S(1)}, f32[2]{0:T(128)}, u32[]{:S(2)}) copy-start(f32[2]{0:T(128)} %coeffs_ref.5) | copy-start | bytes 28
  30.1 17.6 %collective-permute-start.7 = (bf16[512,256]{1,0:T(8,128)(2,1)S(1)}, bf16[512,256]{1,0:T(8,128)(2,1)S(1)}, u32[]{:S(2)}, u32[]{:S(2)}) collective-permute-start(bf16[512,256]{1,0:T(8,128)(2,1)S(1)} %get-tuple-element.30.here_ref), channel_id=1, source_target_pairs={{12,0},{13,1},{0,4},{1,5},{4,8},{5,9},{8,12},{9,13},{14,2},{15,3},... | collective-permute-start | bytes 786440 | tf_op jit(solution)/shard_map/ppermute | solution.py:28
  32.7 15.5 %collective-permute-start.8 = (bf16[512,128]{1,0:T(8,128)(2,1)S(1)}, bf16[512,128]{1,0:T(8,128)(2,1)S(1)}, u32[]{:S(2)}, u32[]{:S(2)}) collective-permute-start(bf16[512,128]{1,0:T(8,128)(2,1)S(1)} %get-tuple-element.32), channel_id=1, source_target_pairs={{4,0},{5,1},{8,4},{9,5},{12,8},{13,9},{0,12},{1,13},{6,2},{7,3},{1... | collective-permute-start | bytes 393224 | tf_op jit(solution)/shard_map/ppermute | solution.py:28
  34.2 16.3 %collective-permute-start.6 = (bf16[512,128]{1,0:T(8,128)(2,1)S(1)}, bf16[512,128]{1,0:T(8,128)(2,1)S(1)}, u32[]{:S(2)}, u32[]{:S(2)}) collective-permute-start(bf16[512,128]{1,0:T(8,128)(2,1)S(1)} %get-tuple-element.29), channel_id=1, source_target_pairs={{4,0},{5,1},{8,4},{9,5},{12,8},{13,9},{0,12},{1,13},{6,2},{7,3},{1... | collective-permute-start | bytes 393224 | tf_op jit(solution)/shard_map/ppermute | solution.py:28

commit v6 on v0

--- a/solution.py
+++ b/solution.py
@@ -253,7 +253,7 @@
     width = t_now.shape[1] // 2
     low = t_now[:, :width].astype(jnp.bfloat16)
     low, t_now, t_prev, h_strips = lax.optimization_barrier((low, t_now, t_prev, h_strips))
-    (high,) = rounded(t_now, [(width, width)])
+    high = t_now[:, width:].astype(jnp.bfloat16)
     band = banded(h_slots, h_strips)
     low_sides, high_sides = both_sides(low), both_sides(high)
     mid_low, low_again = mid_part((0, width), [(0, width)], t_mask, band, low, *low_sides, t_prev, [])

time: 52.4 us -> 52.5 us (level)
  local copies, waits for them, and re-layouts: 2.33 us -> 4.07 us
  waiting for transfers between devices: 19.4 us -> 17.7 us
    ppermute x9, waiting for transfers between devices: 19.4 us -> 17.7 us  [from_side(): return lax.ppermute(block, ('row', 'rep'), route)]
    slice x0 -> x1, local copies, waits for them, and re-layouts: none -> 1.07 us  [local(): high = t_now[:, width:].astype(jnp.bfloat16)]
    unnamed x14 -> x12, local copies, waits for them, and re-layouts: 1.25 us -> 1.93 us
  transfers between devices with their start and end apart: 9 -> 9, of which waited for: 7 -> 7; matrix products, arithmetic and copies ran while one was open for 0% -> 2% of each run, Pallas kernels for 17% -> 17%
where the time goes in v6:
time: 52.5 us; the launch traced here: 52.1 us
  starting transfers between devices  18.9 us (36%)
  waiting for transfers between devices  17.7 us (34%)
  Pallas kernels  10.7 us (20%)
  local copies, waits for them, and re-layouts  4.07 us (8%)
  between operations  0.74 us (1%)
    ppermute x9, starting transfers between devices, from_side(): return lax.ppermute(block, ('row', 'rep'), route)  18.9 us
    ppermute x9, waiting for transfers between devices, from_side(): return lax.ppermute(block, ('row', 'rep'), route)  17.7 us
    pallas_call x2, Pallas kernels, last_part(): pl.pallas_call(functools.partial(last_kernel, begin, column), in_specs=[S...  3.28 us
    pallas_call x1, Pallas kernels, next_part(): pl.pallas_call(next_kernel, in_specs=[SMEM] * 2 + [VMEM] * 7, out_specs=[...  2.44 us
    pallas_call x2, Pallas kernels, mid_part(): pl.pallas_call(functools.partial(mid_kernel, span[0], pieces), in_specs=[...  2.35 us
    pallas_call x1, Pallas kernels, banded(): pl.pallas_call(band_kernel, in_specs=[SMEM, VMEM], out_specs=VMEM, out_sh...  2.17 us
    unnamed x12, local copies, waits for them, and re-layouts  1.93 us
    slice x1, local copies, waits for them, and re-layouts, local(): low = t_now[:, :width].astype(jnp.bfloat16)  1.07 us
  transfers between devices with their start and end apart: 9, of which 7 were waited for; matrix products, arithmetic and copies ran while one was open for 2% of the time, Pallas kernels for 17%

profile of v6, /device:TPU:0, one launch (start us, length us, event | category | flops | bytes accessed | tf_op | source)
XLA Modules:
  0.0 52.1 jit_solution(17366578728092149805)
XLA Ops:
  0.6 0.0 copy-start.3
  0.6 1.1 %slice.15.here_ref = bf16[512,256]{1,0:T(8,128)(2,1)S(1)} slice(f32[512,512]{1,0:T(8,128)} %now_ref.1), slice={[0:512], [0:256]} | slice | bytes 524288 | tf_op jit(solution)/shard_map/slice | solution.py:254
  1.7 0.0 copy-start.1
  1.7 3.1 %collective-permute-start.1 = (bf16[512,256]{1,0:T(8,128)(2,1)S(1)}, bf16[512,256]{1,0:T(8,128)(2,1)S(1)}, u32[]{:S(2)}, u32[]{:S(2)}) collective-permute-start(bf16[512,256]{1,0:T(8,128)(2,1)S(1)} %slice.15.here_ref), channel_id=1, source_target_pairs={{12,0},{5,1},{0,4},{9,5},{4,8},{13,9},{8,12},{1,13},{14,2},{7,3},{... | collective-permute-start | bytes 786440 | tf_op jit(solution)/shard_map/ppermute | solution.py:28
  4.8 2.1 %collective-permute-start = (bf16[512,256]{1,0:T(8,128)(2,1)S(1)}, bf16[512,256]{1,0:T(8,128)(2,1)S(1)}, u32[]{:S(2)}, u32[]{:S(2)}) collective-permute-start(bf16[512,256]{1,0:T(8,128)(2,1)S(1)} %slice.15.here_ref), channel_id=1, source_target_pairs={{4,0},{13,1},{8,4},{1,5},{12,8},{5,9},{0,12},{9,13},{6,2},{15,3},{... | collective-permute-start | bytes 786440 | tf_op jit(solution)/shard_map/ppermute | solution.py:28
  6.9 1.1 %slice.14.here_ref = bf16[512,256]{1,0:T(8,128)(2,1)S(1)} slice(f32[512,512]{1,0:T(8,128)} %now_ref.1), slice={[0:512], [256:512]} | slice | bytes 524288 | tf_op jit(solution)/shard_map/slice | solution.py:256
  8.0 0.1 collective-permute-start.5
  8.0 3.8 %collective-permute-start.4 = (bf16[512,256]{1,0:T(8,128)(2,1)S(1)}, bf16[512,256]{1,0:T(8,128)(2,1)S(1)}, u32[]{:S(2)}, u32[]{:S(2)}) collective-permute-start(bf16[512,256]{1,0:T(8,128)(2,1)S(1)} %slice.14.here_ref), channel_id=1, source_target_pairs={{4,0},{13,1},{8,4},{1,5},{12,8},{5,9},{0,12},{9,13},{6,2},{15,3},{... | collective-permute-start | bytes 786440 | tf_op jit(solution)/shard_map/ppermute | solution.py:28
  11.8 0.0 copy-start.2
  11.8 1.2 %copy-done.2 = bf16[8,64,1024]{2,1,0:T(8,128)(2,1)S(1)} copy-done((bf16[8,64,1024]{2,1,0:T(8,128)(2,1)S(1)}, bf16[8,64,1024]{2,1,0:T(8,128)(2,1)}, u32[]{:S(2)}) %copy-start.2) | copy-done | bytes 1048600
  13.1 0.0 copy-start.5
  13.1 0.7 %copy-done.5 = s32[8,16]{1,0:T(8,128)S(1)} copy-done((s32[8,16]{1,0:T(8,128)S(1)}, s32[8,16]{1,0:T(8,128)}, u32[]{:S(2)}) %copy-start.5) | copy-done | bytes 536
  13.8 2.2 %band.1.band_ref = bf16[512,1536]{1,0:T(8,128)(2,1)S(1)} custom-call(s32[8,16]{1,0:T(8,128)S(1)} %copy-done.5, bf16[8,64,1024]{2,1,0:T(8,128)(2,1)S(1)} %copy-done.2), custom_call_target="tpu_custom_call" | custom-call | flops 6291456 | bytes 2621440 | tf_op jit(solution)/shard_map/band/pallas_call | solution.py:92
  15.9 0.0 collective-permute-done.1.first_ref
  15.9 2.7 %collective-permute-done.second_ref = bf16[512,256]{1,0:T(8,128)(2,1)S(1)} collective-permute-done((bf16[512,256]{1,0:T(8,128)(2,1)S(1)}, bf16[512,256]{1,0:T(8,128)(2,1)S(1)}, u32[]{:S(2)}, u32[]{:S(2)}) %collective-permute-start) | collective-permute-done | bytes 262176 | tf_op jit(solution)/shard_map/ppermute | solution.py:28
  18.7 0.0 copy-done.3
  18.7 0.0 copy-done.1
  18.7 1.2 %mid_part.2 = (f32[512,256]{1,0:T(8,128)S(1)}, bf16[512,256]{1,0:T(8,128)(2,1)S(1)}) custom-call(s32[8,8]{1,0:T(8,128)S(1)} %copy-done.3, bf16[512,1536]{1,0:T(8,128)(2,1)S(1)} %band.1.band_ref, bf16[512,256]{1,0:T(8,128)(2,1)S(1)} %slice.15.here_ref, bf16[512,256]{1,0:T(8,128)(2,1)S(1)} %collective-permute-done.second_ref, ...), custom_call_target="tpu_custom_call" | custom-call | flops 402653184 | bytes 3670016 | tf_op jit(solution)/shard_map/mid_part/pallas_call | solution.py:150
  19.9 2.7 %collective-permute-start.3 = (bf16[512,256]{1,0:T(8,128)(2,1)S(1)}, bf16[512,256]{1,0:T(8,128)(2,1)S(1)}, u32[]{:S(2)}, u32[]{:S(2)}) collective-permute-start(bf16[512,256]{1,0:T(8,128)(2,1)S(1)} %get-tuple-element.24.here_ref), channel_id=1, source_target_pairs={{12,0},{5,1},{0,4},{9,5},{4,8},{13,9},{8,12},{1,13},{14,2},{7,3},{... | collective-permute-start | bytes 786440 | tf_op jit(solution)/shard_map/ppermute | solution.py:28
  22.5 1.2 %collective-permute-start.2 = (bf16[512,256]{1,0:T(8,128)(2,1)S(1)}, bf16[512,256]{1,0:T(8,128)(2,1)S(1)}, u32[]{:S(2)}, u32[]{:S(2)}) collective-permute-start(bf16[512,256]{1,0:T(8,128)(2,1)S(1)} %get-tuple-element.24.here_ref), channel_id=1, source_target_pairs={{4,0},{13,1},{8,4},{1,5},{12,8},{5,9},{0,12},{9,13},{6,2},{15,3},{... | collective-permute-start | bytes 786440 | tf_op jit(solution)/shard_map/ppermute | solution.py:28
  23.7 1.6 %collective-permute-done.5.first_ref = bf16[512,256]{1,0:T(8,128)(2,1)S(1)} collective-permute-done((bf16[512,256]{1,0:T(8,128)(2,1)S(1)}, bf16[512,256]{1,0:T(8,128)(2,1)S(1)}, u32[]{:S(2)}, u32[]{:S(2)}) %collective-permute-start.5) | collective-permute-done | bytes 262176 | tf_op jit(solution)/shard_map/ppermute | solution.py:28
  25.3 3.6 %collective-permute-done.4.second_ref = bf16[512,256]{1,0:T(8,128)(2,1)S(1)} collective-permute-done((bf16[512,256]{1,0:T(8,128)(2,1)S(1)}, bf16[512,256]{1,0:T(8,128)(2,1)S(1)}, u32[]{:S(2)}, u32[]{:S(2)}) %collective-permute-start.4) | collective-permute-done | bytes 262176 | tf_op jit(solution)/shard_map/ppermute | solution.py:28
  28.9 0.0 copy-start
  28.9 0.0 copy-start.4
  28.9 1.2 %mid_part.3 = (f32[512,256]{1,0:T(8,128)S(1)}, bf16[512,256]{1,0:T(8,128)(2,1)S(1)}, bf16[512,128]{1,0:T(8,128)(2,1)S(1)}, bf16[512,128]{1,0:T(8,128)(2,1)S(1)}) custom-call(s32[8,8]{1,0:T(8,128)S(1)} %copy-done.3, bf16[512,1536]{1,0:T(8,128)(2,1)S(1)} %band.1.band_ref, bf16[512,256]{1,0:T(8,128)(2,1)S(1)} %slice.14.here_ref, ...), custom_call_target="tpu_custom_call" | custom-call | flops 402653184 | bytes 3670016 | tf_op jit(solution)/shard_map/mid_part/pallas_call | solution.py:150
  30.1 2.6 %collective-permute-start.7 = (bf16[512,256]{1,0:T(8,128)(2,1)S(1)}, bf16[512,256]{1,0:T(8,128)(2,1)S(1)}, u32[]{:S(2)}, u32[]{:S(2)}) collective-permute-start(bf16[512,256]{1,0:T(8,128)(2,1)S(1)} %get-tuple-element.30.here_ref), channel_id=1, source_target_pairs={{12,0},{13,1},{0,4},{1,5},{4,8},{5,9},{8,12},{9,13},{14,2},{15,3},... | collective-permute-start | bytes 786440 | tf_op jit(solution)/shard_map/ppermute | solution.py:28
  32.7 1.5 %collective-permute-start.8 = (bf16[512,128]{1,0:T(8,128)(2,1)S(1)}, bf16[512,128]{1,0:T(8,128)(2,1)S(1)}, u32[]{:S(2)}, u32[]{:S(2)}) collective-permute-start(bf16[512,128]{1,0:T(8,128)(2,1)S(1)} %get-tuple-element.32), channel_id=1, source_target_pairs={{4,0},{5,1},{8,4},{9,5},{12,8},{13,9},{0,12},{1,13},{6,2},{7,3},{1... | collective-permute-start | bytes 393224 | tf_op jit(solution)/shard_map/ppermute | solution.py:28
  34.2 2.0 %collective-permute-start.6 = (bf16[512,128]{1,0:T(8,128)(2,1)S(1)}, bf16[512,128]{1,0:T(8,128)(2,1)S(1)}, u32[]{:S(2)}, u32[]{:S(2)}) collective-permute-start(bf16[512,128]{1,0:T(8,128)(2,1)S(1)} %get-tuple-element.29), channel_id=1, source_target_pairs={{4,0},{5,1},{8,4},{9,5},{12,8},{13,9},{0,12},{1,13},{6,2},{7,3},{1... | collective-permute-start | bytes 393224 | tf_op jit(solution)/shard_map/ppermute | solution.py:28
  36.1 0.5 collective-permute-done.3.first_ref
  36.6 2.2 %collective-permute-done.2.second_ref = bf16[512,256]{1,0:T(8,128)(2,1)S(1)} collective-permute-done((bf16[512,256]{1,0:T(8,128)(2,1)S(1)}, bf16[512,256]{1,0:T(8,128)(2,1)S(1)}, u32[]{:S(2)}, u32[]{:S(2)}) %collective-permute-start.2) | collective-permute-done | bytes 262176 | tf_op jit(solution)/shard_map/ppermute | solution.py:28
  38.8 0.0 copy-done
  38.8 0.0 copy-done.4
  38.8 2.4 %next_part.1 = (f32[512,512]{1,0:T(8,128)}, f32[512,512]{1,0:T(8,128)}, f32[512,512]{1,0:T(8,128)}, f32[8,128]{1,0:T(8,128)S(1)}) custom-call(s32[8,8]{1,0:T(8,128)S(1)} %copy-done.3, f32[2]{0:T(128)S(1)} %copy-done.4, bf16[512,1536]{1,0:T(8,128)(2,1)S(1)} %band.1.band_ref, bf16[512,256]{1,0:T(8,128)(2,1)S(1)} %get-tuple-element.24.here_ref, ...), custom_call_target="tpu_custom_call" | custom-call | flops 402653184 | bytes 5505024 | tf_op jit(solution)/shard_map/next_part/pallas_call | solution.py:182
  41.3 6.5 %collective-permute-done.7.first_ref = bf16[512,256]{1,0:T(8,128)(2,1)S(1)} collective-permute-done((bf16[512,256]{1,0:T(8,128)(2,1)S(1)}, bf16[512,256]{1,0:T(8,128)(2,1)S(1)}, u32[]{:S(2)}, u32[]{:S(2)}) %collective-permute-start.7) | collective-permute-done | bytes 262176 | tf_op jit(solution)/shard_map/ppermute | solution.py:28
  47.7 0.4 begun_part.1.sums_ref
  48.2 0.0 collective-permute-done.8.second_ref
  48.2 1.6 %last_part.2 = (f32[512,512]{1,0:T(8,128)}, f32[512,512]{1,0:T(8,128)}) custom-call(s32[8,8]{1,0:T(8,128)S(1)} %copy-done.3, f32[2]{0:T(128)S(1)} %copy-done.4, bf16[512,1536]{1,0:T(8,128)(2,1)S(1)} %band.1.band_ref, bf16[512,128]{1,0:T(8,128)(2,1)S(1)} %collective-permute-done.8.second_ref, ...), custom_call_target="tpu_custom_call", output_to_operand_aliasing={{0}: (6, {}), {1}: (7, {})} | custom-call | flops 67108864 | bytes 1966080 | tf_op jit(solution)/shard_map/last_part/pallas_call | solution.py:239
  49.9 0.6 %collective-permute-done.6.second_ref = bf16[512,128]{1,0:T(8,128)(2,1)S(1)} collective-permute-done((bf16[512,128]{1,0:T(8,128)(2,1)S(1)}, bf16[512,128]{1,0:T(8,128)(2,1)S(1)}, u32[]{:S(2)}, u32[]{:S(2)}) %collective-permute-start.6) | collective-permute-done | bytes 131104 | tf_op jit(solution)/shard_map/ppermute | solution.py:28
  50.5 1.6 %last_part.3 = (f32[512,512]{1,0:T(8,128)}, f32[512,512]{1,0:T(8,128)}) custom-call(s32[8,8]{1,0:T(8,128)S(1)} %copy-done.3, f32[2]{0:T(128)S(1)} %copy-done.4, bf16[512,1536]{1,0:T(8,128)(2,1)S(1)} %band.1.band_ref, bf16[512,128]{1,0:T(8,128)(2,1)S(1)} %collective-permute-done.6.second_ref, ...), custom_call_target="tpu_custom_call", output_to_operand_aliasing={{0}: (6, {}), {1}: (7, {})} | custom-call | flops 67108864 | bytes 1966080 | tf_op jit(solution)/shard_map/last_part/pallas_call | solution.py:239
Async XLA Ops:
  0.6 18.1 %copy-start.3 = (s32[8,8]{1,0:T(8,128)S(1)}, s32[8,8]{1,0:T(8,128)}, u32[]{:S(2)}) copy-start(s32[8,8]{1,0:T(8,128)} %mask_ref.9) | copy-start | bytes 772
  1.7 17.0 %copy-start.1 = (f32[512,512]{1,0:T(8,128)S(1)}, f32[512,512]{1,0:T(8,128)}, u32[]{:S(2)}) copy-start(f32[512,512]{1,0:T(8,128)} %prev_ref.1) | copy-start | bytes 3145732
  1.7 14.2 %collective-permute-start.1 = (bf16[512,256]{1,0:T(8,128)(2,1)S(1)}, bf16[512,256]{1,0:T(8,128)(2,1)S(1)}, u32[]{:S(2)}, u32[]{:S(2)}) collective-permute-start(bf16[512,256]{1,0:T(8,128)(2,1)S(1)} %slice.15.here_ref), channel_id=1, source_target_pairs={{12,0},{5,1},{0,4},{9,5},{4,8},{13,9},{8,12},{1,13},{14,2},{7,3},{... | collective-permute-start | bytes 786440 | tf_op jit(solution)/shard_map/ppermute | solution.py:28
  4.8 13.9 %collective-permute-start = (bf16[512,256]{1,0:T(8,128)(2,1)S(1)}, bf16[512,256]{1,0:T(8,128)(2,1)S(1)}, u32[]{:S(2)}, u32[]{:S(2)}) collective-permute-start(bf16[512,256]{1,0:T(8,128)(2,1)S(1)} %slice.15.here_ref), channel_id=1, source_target_pairs={{4,0},{13,1},{8,4},{1,5},{12,8},{5,9},{0,12},{9,13},{6,2},{15,3},{... | collective-permute-start | bytes 786440 | tf_op jit(solution)/shard_map/ppermute | solution.py:28
  8.0 17.4 %collective-permute-start.5 = (bf16[512,256]{1,0:T(8,128)(2,1)S(1)}, bf16[512,256]{1,0:T(8,128)(2,1)S(1)}, u32[]{:S(2)}, u32[]{:S(2)}) collective-permute-start(bf16[512,256]{1,0:T(8,128)(2,1)S(1)} %slice.14.here_ref), channel_id=1, source_target_pairs={{12,0},{5,1},{0,4},{9,5},{4,8},{13,9},{8,12},{1,13},{14,2},{7,3},{... | collective-permute-start | bytes 786440 | tf_op jit(solution)/shard_map/ppermute | solution.py:28
  8.0 20.9 %collective-permute-start.4 = (bf16[512,256]{1,0:T(8,128)(2,1)S(1)}, bf16[512,256]{1,0:T(8,128)(2,1)S(1)}, u32[]{:S(2)}, u32[]{:S(2)}) collective-permute-start(bf16[512,256]{1,0:T(8,128)(2,1)S(1)} %slice.14.here_ref), channel_id=1, source_target_pairs={{4,0},{13,1},{8,4},{1,5},{12,8},{5,9},{0,12},{9,13},{6,2},{15,3},{... | collective-permute-start | bytes 786440 | tf_op jit(solution)/shard_map/ppermute | solution.py:28
  11.8 1.2 %copy-start.2 = (bf16[8,64,1024]{2,1,0:T(8,128)(2,1)S(1)}, bf16[8,64,1024]{2,1,0:T(8,128)(2,1)}, u32[]{:S(2)}) copy-start(bf16[8,64,1024]{2,1,0:T(8,128)(2,1)} %strips_ref) | copy-start | bytes 3145732
  13.1 0.7 %copy-start.5 = (s32[8,16]{1,0:T(8,128)S(1)}, s32[8,16]{1,0:T(8,128)}, u32[]{:S(2)}) copy-start(s32[8,16]{1,0:T(8,128)} %slots_ref.1) | copy-start | bytes 1540
  19.9 16.7 %collective-permute-start.3 = (bf16[512,256]{1,0:T(8,128)(2,1)S(1)}, bf16[512,256]{1,0:T(8,128)(2,1)S(1)}, u32[]{:S(2)}, u32[]{:S(2)}) collective-permute-start(bf16[512,256]{1,0:T(8,128)(2,1)S(1)} %get-tuple-element.24.here_ref), channel_id=1, source_target_pairs={{12,0},{5,1},{0,4},{9,5},{4,8},{13,9},{8,12},{1,13},{14,2},{7,3},{... | collective-permute-start | bytes 786440 | tf_op jit(solution)/shard_map/ppermute | solution.py:28
  22.5 16.3 %collective-permute-start.2 = (bf16[512,256]{1,0:T(8,128)(2,1)S(1)}, bf16[512,256]{1,0:T(8,128)(2,1)S(1)}, u32[]{:S(2)}, u32[]{:S(2)}) collective-permute-start(bf16[512,256]{1,0:T(8,128)(2,1)S(1)} %get-tuple-element.24.here_ref), channel_id=1, source_target_pairs={{4,0},{13,1},{8,4},{1,5},{12,8},{5,9},{0,12},{9,13},{6,2},{15,3},{... | collective-permute-start | bytes 786440 | tf_op jit(solution)/shard_map/ppermute | solution.py:28
  28.9 9.9 %copy-start = (f32[512,512]{1,0:T(8,128)S(1)}, f32[512,512]{1,0:T(8,128)}, u32[]{:S(2)}) copy-start(f32[512,512]{1,0:T(8,128)} %now_ref.1) | copy-start | bytes 3145732
  28.9 9.9 %copy-start.4 = (f32[2]{0:T(128)S(1)}, f32[2]{0:T(128)}, u32[]{:S(2)}) copy-start(f32[2]{0:T(128)} %coeffs_ref.5) | copy-start | bytes 28
  30.1 17.6 %collective-permute-start.7 = (bf16[512,256]{1,0:T(8,128)(2,1)S(1)}, bf16[512,256]{1,0:T(8,128)(2,1)S(1)}, u32[]{:S(2)}, u32[]{:S(2)}) collective-permute-start(bf16[512,256]{1,0:T(8,128)(2,1)S(1)} %get-tuple-element.30.here_ref), channel_id=1, source_target_pairs={{12,0},{13,1},{0,4},{1,5},{4,8},{5,9},{8,12},{9,13},{14,2},{15,3},... | collective-permute-start | bytes 786440 | tf_op jit(solution)/shard_map/ppermute | solution.py:28
  32.7 15.5 %collective-permute-start.8 = (bf16[512,128]{1,0:T(8,128)(2,1)S(1)}, bf16[512,128]{1,0:T(8,128)(2,1)S(1)}, u32[]{:S(2)}, u32[]{:S(2)}) collective-permute-start(bf16[512,128]{1,0:T(8,128)(2,1)S(1)} %get-tuple-element.32), channel_id=1, source_target_pairs={{4,0},{5,1},{8,4},{9,5},{12,8},{13,9},{0,12},{1,13},{6,2},{7,3},{1... | collective-permute-start | bytes 393224 | tf_op jit(solution)/shard_map/ppermute | solution.py:28
  34.2 16.3 %collective-permute-start.6 = (bf16[512,128]{1,0:T(8,128)(2,1)S(1)}, bf16[512,128]{1,0:T(8,128)(2,1)S(1)}, u32[]{:S(2)}, u32[]{:S(2)}) collective-permute-start(bf16[512,128]{1,0:T(8,128)(2,1)S(1)} %get-tuple-element.29), channel_id=1, source_target_pairs={{4,0},{5,1},{8,4},{9,5},{12,8},{13,9},{0,12},{1,13},{6,2},{7,3},{1... | collective-permute-start | bytes 393224 | tf_op jit(solution)/shard_map/ppermute | solution.py:28

commit v7 on v5

--- a/solution.py
+++ b/solution.py
@@ -8,7 +8,7 @@
 from jax.sharding import PartitionSpec as P
 
 LANES = 128
-CHUNKS = 4
+CHUNKS = 1
 MIB = 1024 * 1024
 
 SMEM = pl.BlockSpec(memory_space=pltpu.SMEM)

time: 52.4 us -> 52.4 us (level)
  transfers between devices with their start and end apart: 9 -> 9, of which waited for: 7 -> 7; matrix products, arithmetic and copies ran while one was open for 0% -> 0% of each run, Pallas kernels for 17% -> 18%
where the time goes in v7:
time: 52.4 us; the launch traced here: 52.2 us
  waiting for transfers between devices  19.4 us (37%)
  starting transfers between devices  18.9 us (36%)
  Pallas kernels  10.9 us (21%)
  local copies, waits for them, and re-layouts  2.33 us (4%)
  between operations  0.74 us (1%)
    ppermute x9, waiting for transfers between devices, from_side(): return lax.ppermute(block, ('row', 'rep'), route)  19.4 us
    ppermute x9, starting transfers between devices, from_side(): return lax.ppermute(block, ('row', 'rep'), route)  18.9 us
    pallas_call x2, Pallas kernels, last_part(): pl.pallas_call(functools.partial(last_kernel, begin, column), in_specs=[S...  3.42 us
    pallas_call x1, Pallas kernels, next_part(): pl.pallas_call(next_kernel, in_specs=[SMEM] * 2 + [VMEM] * 7, out_specs=[...  2.44 us
    pallas_call x2, Pallas kernels, mid_part(): pl.pallas_call(functools.partial(mid_kernel, span[0], pieces), in_specs=[...  2.35 us
    pallas_call x1, Pallas kernels, banded(): pl.pallas_call(band_kernel, in_specs=[SMEM, VMEM], out_specs=VMEM, out_sh...  2.17 us
    unnamed x14, local copies, waits for them, and re-layouts  1.25 us
    slice x1, local copies, waits for them, and re-layouts, local(): low = t_now[:, :width].astype(jnp.bfloat16)  1.07 us
  transfers between devices with their start and end apart: 9, of which 7 were waited for; matrix products, arithmetic and copies ran while one was open for 0% of the time, Pallas kernels for 18%

profile of v7, /device:TPU:0, one launch (start us, length us, event | category | flops | bytes accessed | tf_op | source)
XLA Modules:
  0.0 52.2 jit_solution(1774026610935889832)
XLA Ops:
  0.6 0.0 copy-start.6
  0.6 1.1 %slice.7.here_ref = bf16[512,256]{1,0:T(8,128)(2,1)S(1)} slice(f32[512,512]{1,0:T(8,128)} %now_ref.2), slice={[0:512], [0:256]} | slice | bytes 524288 | tf_op jit(solution)/shard_map/slice | solution.py:254
  1.7 3.1 %collective-permute-start.1 = (bf16[512,256]{1,0:T(8,128)(2,1)S(1)}, bf16[512,256]{1,0:T(8,128)(2,1)S(1)}, u32[]{:S(2)}, u32[]{:S(2)}) collective-permute-start(bf16[512,256]{1,0:T(8,128)(2,1)S(1)} %slice.7.here_ref), channel_id=1, source_target_pairs={{12,0},{5,1},{0,4},{9,5},{4,8},{13,9},{8,12},{1,13},{14,2},{7,3},{... | collective-permute-start | bytes 786440 | tf_op jit(solution)/shard_map/ppermute | solution.py:28
  4.8 2.1 %collective-permute-start = (bf16[512,256]{1,0:T(8,128)(2,1)S(1)}, bf16[512,256]{1,0:T(8,128)(2,1)S(1)}, u32[]{:S(2)}, u32[]{:S(2)}) collective-permute-start(bf16[512,256]{1,0:T(8,128)(2,1)S(1)} %slice.7.here_ref), channel_id=1, source_target_pairs={{4,0},{13,1},{8,4},{1,5},{12,8},{5,9},{0,12},{9,13},{6,2},{15,3},{... | collective-permute-start | bytes 786440 | tf_op jit(solution)/shard_map/ppermute | solution.py:28
  6.9 0.0 copy-start
  6.9 1.2 %copy-done = f32[512,512]{1,0:T(8,128)S(1)} copy-done((f32[512,512]{1,0:T(8,128)S(1)}, f32[512,512]{1,0:T(8,128)}, u32[]{:S(2)}) %copy-start) | copy-done | bytes 1048600
  8.1 0.0 copy-start.3
  8.2 0.0 copy-start.2
  8.2 0.0 copy-start.4
  8.2 0.1 collective-permute-start.5
  8.2 3.8 %collective-permute-start.4 = (bf16[512,256]{1,0:T(8,128)(2,1)S(1)}, bf16[512,256]{1,0:T(8,128)(2,1)S(1)}, u32[]{:S(2)}, u32[]{:S(2)}) collective-permute-start(bf16[512,256]{1,0:T(8,128)(2,1)S(1)} %round_part.1.here_ref), channel_id=1, source_target_pairs={{4,0},{13,1},{8,4},{1,5},{12,8},{5,9},{0,12},{9,13},{6,2},{15,3},{... | collective-permute-start | bytes 786440 | tf_op jit(solution)/shard_map/ppermute | solution.py:28
  12.1 0.0 copy-done.6
  12.1 0.0 copy-done.3
  12.1 2.2 %band.1.band_ref = bf16[512,1536]{1,0:T(8,128)(2,1)S(1)} custom-call(s32[8,16]{1,0:T(8,128)S(1)} %copy-done.6, bf16[8,64,1024]{2,1,0:T(8,128)(2,1)S(1)} %copy-done.3), custom_call_target="tpu_custom_call" | custom-call | flops 6291456 | bytes 2621440 | tf_op jit(solution)/shard_map/band/pallas_call | solution.py:92
  14.2 0.0 collective-permute-done.1.first_ref
  14.2 4.3 %collective-permute-done.second_ref = bf16[512,256]{1,0:T(8,128)(2,1)S(1)} collective-permute-done((bf16[512,256]{1,0:T(8,128)(2,1)S(1)}, bf16[512,256]{1,0:T(8,128)(2,1)S(1)}, u32[]{:S(2)}, u32[]{:S(2)}) %collective-permute-start) | collective-permute-done | bytes 262176 | tf_op jit(solution)/shard_map/ppermute | solution.py:28
  18.6 0.0 copy-done.2
  18.6 0.0 copy-done.4
  18.6 1.2 %mid_part.2 = (f32[512,256]{1,0:T(8,128)S(1)}, bf16[512,256]{1,0:T(8,128)(2,1)S(1)}) custom-call(s32[8,8]{1,0:T(8,128)S(1)} %copy-done.4, bf16[512,1536]{1,0:T(8,128)(2,1)S(1)} %band.1.band_ref, bf16[512,256]{1,0:T(8,128)(2,1)S(1)} %slice.7.here_ref, bf16[512,256]{1,0:T(8,128)(2,1)S(1)} %collective-permute-done.second_ref, ...), custom_call_target="tpu_custom_call" | custom-call | flops 402653184 | bytes 3670016 | tf_op jit(solution)/shard_map/mid_part/pallas_call | solution.py:150
  19.7 2.8 %collective-permute-start.3 = (bf16[512,256]{1,0:T(8,128)(2,1)S(1)}, bf16[512,256]{1,0:T(8,128)(2,1)S(1)}, u32[]{:S(2)}, u32[]{:S(2)}) collective-permute-start(bf16[512,256]{1,0:T(8,128)(2,1)S(1)} %get-tuple-element.24.here_ref), channel_id=1, source_target_pairs={{12,0},{5,1},{0,4},{9,5},{4,8},{13,9},{8,12},{1,13},{14,2},{7,3},{... | collective-permute-start | bytes 786440 | tf_op jit(solution)/shard_map/ppermute | solution.py:28
  22.5 1.1 %collective-permute-start.2 = (bf16[512,256]{1,0:T(8,128)(2,1)S(1)}, bf16[512,256]{1,0:T(8,128)(2,1)S(1)}, u32[]{:S(2)}, u32[]{:S(2)}) collective-permute-start(bf16[512,256]{1,0:T(8,128)(2,1)S(1)} %get-tuple-element.24.here_ref), channel_id=1, source_target_pairs={{4,0},{13,1},{8,4},{1,5},{12,8},{5,9},{0,12},{9,13},{6,2},{15,3},{... | collective-permute-start | bytes 786440 | tf_op jit(solution)/shard_map/ppermute | solution.py:28
  23.6 1.7 %collective-permute-done.5.first_ref = bf16[512,256]{1,0:T(8,128)(2,1)S(1)} collective-permute-done((bf16[512,256]{1,0:T(8,128)(2,1)S(1)}, bf16[512,256]{1,0:T(8,128)(2,1)S(1)}, u32[]{:S(2)}, u32[]{:S(2)}) %collective-permute-start.5) | collective-permute-done | bytes 262176 | tf_op jit(solution)/shard_map/ppermute | solution.py:28
  25.3 3.6 %collective-permute-done.4.second_ref = bf16[512,256]{1,0:T(8,128)(2,1)S(1)} collective-permute-done((bf16[512,256]{1,0:T(8,128)(2,1)S(1)}, bf16[512,256]{1,0:T(8,128)(2,1)S(1)}, u32[]{:S(2)}, u32[]{:S(2)}) %collective-permute-start.4) | collective-permute-done | bytes 262176 | tf_op jit(solution)/shard_map/ppermute | solution.py:28
  28.9 0.0 copy-start.1
  28.9 0.0 copy-start.5
  28.9 1.2 %mid_part.3 = (f32[512,256]{1,0:T(8,128)S(1)}, bf16[512,256]{1,0:T(8,128)(2,1)S(1)}, bf16[512,128]{1,0:T(8,128)(2,1)S(1)}, bf16[512,128]{1,0:T(8,128)(2,1)S(1)}) custom-call(s32[8,8]{1,0:T(8,128)S(1)} %copy-done.4, bf16[512,1536]{1,0:T(8,128)(2,1)S(1)} %band.1.band_ref, bf16[512,256]{1,0:T(8,128)(2,1)S(1)} %round_part.1.here_ref, ...), custom_call_target="tpu_custom_call" | custom-call | flops 402653184 | bytes 3670016 | tf_op jit(solution)/shard_map/mid_part/pallas_call | solution.py:150
  30.1 2.6 %collective-permute-start.7 = (bf16[512,256]{1,0:T(8,128)(2,1)S(1)}, bf16[512,256]{1,0:T(8,128)(2,1)S(1)}, u32[]{:S(2)}, u32[]{:S(2)}) collective-permute-start(bf16[512,256]{1,0:T(8,128)(2,1)S(1)} %get-tuple-element.30.here_ref), channel_id=1, source_target_pairs={{12,0},{13,1},{0,4},{1,5},{4,8},{5,9},{8,12},{9,13},{14,2},{15,3},... | collective-permute-start | bytes 786440 | tf_op jit(solution)/shard_map/ppermute | solution.py:28
  32.7 1.5 %collective-permute-start.8 = (bf16[512,128]{1,0:T(8,128)(2,1)S(1)}, bf16[512,128]{1,0:T(8,128)(2,1)S(1)}, u32[]{:S(2)}, u32[]{:S(2)}) collective-permute-start(bf16[512,128]{1,0:T(8,128)(2,1)S(1)} %get-tuple-element.32), channel_id=1, source_target_pairs={{4,0},{5,1},{8,4},{9,5},{12,8},{13,9},{0,12},{1,13},{6,2},{7,3},{1... | collective-permute-start | bytes 393224 | tf_op jit(solution)/shard_map/ppermute | solution.py:28
  34.2 2.0 %collective-permute-start.6 = (bf16[512,128]{1,0:T(8,128)(2,1)S(1)}, bf16[512,128]{1,0:T(8,128)(2,1)S(1)}, u32[]{:S(2)}, u32[]{:S(2)}) collective-permute-start(bf16[512,128]{1,0:T(8,128)(2,1)S(1)} %get-tuple-element.29), channel_id=1, source_target_pairs={{4,0},{5,1},{8,4},{9,5},{12,8},{13,9},{0,12},{1,13},{6,2},{7,3},{1... | collective-permute-start | bytes 393224 | tf_op jit(solution)/shard_map/ppermute | solution.py:28
  36.1 0.5 collective-permute-done.3.first_ref
  36.6 2.2 %collective-permute-done.2.second_ref = bf16[512,256]{1,0:T(8,128)(2,1)S(1)} collective-permute-done((bf16[512,256]{1,0:T(8,128)(2,1)S(1)}, bf16[512,256]{1,0:T(8,128)(2,1)S(1)}, u32[]{:S(2)}, u32[]{:S(2)}) %collective-permute-start.2) | collective-permute-done | bytes 262176 | tf_op jit(solution)/shard_map/ppermute | solution.py:28
  38.8 0.0 copy-done.1
  38.8 0.0 copy-done.5
  38.8 2.4 %next_part.1 = (f32[512,512]{1,0:T(8,128)}, f32[512,512]{1,0:T(8,128)}, f32[512,512]{1,0:T(8,128)}, f32[8,128]{1,0:T(8,128)S(1)}) custom-call(s32[8,8]{1,0:T(8,128)S(1)} %copy-done.4, f32[2]{0:T(128)S(1)} %copy-done.5, bf16[512,1536]{1,0:T(8,128)(2,1)S(1)} %band.1.band_ref, bf16[512,256]{1,0:T(8,128)(2,1)S(1)} %get-tuple-element.24.here_ref, ...), custom_call_target="tpu_custom_call" | custom-call | flops 402653184 | bytes 5505024 | tf_op jit(solution)/shard_map/next_part/pallas_call | solution.py:182
  41.3 6.5 %collective-permute-done.7.first_ref = bf16[512,256]{1,0:T(8,128)(2,1)S(1)} collective-permute-done((bf16[512,256]{1,0:T(8,128)(2,1)S(1)}, bf16[512,256]{1,0:T(8,128)(2,1)S(1)}, u32[]{:S(2)}, u32[]{:S(2)}) %collective-permute-start.7) | collective-permute-done | bytes 262176 | tf_op jit(solution)/shard_map/ppermute | solution.py:28
  47.7 0.4 begun_part.1.sums_ref
  48.2 0.0 collective-permute-done.8.second_ref
  48.2 1.7 %last_part.2 = (f32[512,512]{1,0:T(8,128)}, f32[512,512]{1,0:T(8,128)}) custom-call(s32[8,8]{1,0:T(8,128)S(1)} %copy-done.4, f32[2]{0:T(128)S(1)} %copy-done.5, bf16[512,1536]{1,0:T(8,128)(2,1)S(1)} %band.1.band_ref, bf16[512,128]{1,0:T(8,128)(2,1)S(1)} %collective-permute-done.8.second_ref, ...), custom_call_target="tpu_custom_call", output_to_operand_aliasing={{0}: (6, {}), {1}: (7, {})} | custom-call | flops 67108864 | bytes 1966080 | tf_op jit(solution)/shard_map/last_part/pallas_call | solution.py:239
  49.9 0.6 %collective-permute-done.6.second_ref = bf16[512,128]{1,0:T(8,128)(2,1)S(1)} collective-permute-done((bf16[512,128]{1,0:T(8,128)(2,1)S(1)}, bf16[512,128]{1,0:T(8,128)(2,1)S(1)}, u32[]{:S(2)}, u32[]{:S(2)}) %collective-permute-start.6) | collective-permute-done | bytes 131104 | tf_op jit(solution)/shard_map/ppermute | solution.py:28
  50.5 1.7 %last_part.3 = (f32[512,512]{1,0:T(8,128)}, f32[512,512]{1,0:T(8,128)}) custom-call(s32[8,8]{1,0:T(8,128)S(1)} %copy-done.4, f32[2]{0:T(128)S(1)} %copy-done.5, bf16[512,1536]{1,0:T(8,128)(2,1)S(1)} %band.1.band_ref, bf16[512,128]{1,0:T(8,128)(2,1)S(1)} %collective-permute-done.6.second_ref, ...), custom_call_target="tpu_custom_call", output_to_operand_aliasing={{0}: (6, {}), {1}: (7, {})} | custom-call | flops 67108864 | bytes 1966080 | tf_op jit(solution)/shard_map/last_part/pallas_call | solution.py:239
  (1 shorter events, 0.0 us)
Async XLA Ops:
  0.6 11.4 %copy-start.6 = (s32[8,16]{1,0:T(8,128)S(1)}, s32[8,16]{1,0:T(8,128)}, u32[]{:S(2)}) copy-start(s32[8,16]{1,0:T(8,128)} %slots_ref.1) | copy-start | bytes 1540
  1.7 12.5 %collective-permute-start.1 = (bf16[512,256]{1,0:T(8,128)(2,1)S(1)}, bf16[512,256]{1,0:T(8,128)(2,1)S(1)}, u32[]{:S(2)}, u32[]{:S(2)}) collective-permute-start(bf16[512,256]{1,0:T(8,128)(2,1)S(1)} %slice.7.here_ref), channel_id=1, source_target_pairs={{12,0},{5,1},{0,4},{9,5},{4,8},{13,9},{8,12},{1,13},{14,2},{7,3},{... | collective-permute-start | bytes 786440 | tf_op jit(solution)/shard_map/ppermute | solution.py:28
  4.8 13.8 %collective-permute-start = (bf16[512,256]{1,0:T(8,128)(2,1)S(1)}, bf16[512,256]{1,0:T(8,128)(2,1)S(1)}, u32[]{:S(2)}, u32[]{:S(2)}) collective-permute-start(bf16[512,256]{1,0:T(8,128)(2,1)S(1)} %slice.7.here_ref), channel_id=1, source_target_pairs={{4,0},{13,1},{8,4},{1,5},{12,8},{5,9},{0,12},{9,13},{6,2},{15,3},{... | collective-permute-start | bytes 786440 | tf_op jit(solution)/shard_map/ppermute | solution.py:28
  6.9 1.2 %copy-start = (f32[512,512]{1,0:T(8,128)S(1)}, f32[512,512]{1,0:T(8,128)}, u32[]{:S(2)}) copy-start(f32[512,512]{1,0:T(8,128)} %now_ref.2) | copy-start | bytes 3145732
  8.1 3.9 %copy-start.3 = (bf16[8,64,1024]{2,1,0:T(8,128)(2,1)S(1)}, bf16[8,64,1024]{2,1,0:T(8,128)(2,1)}, u32[]{:S(2)}) copy-start(bf16[8,64,1024]{2,1,0:T(8,128)(2,1)} %strips_ref) | copy-start | bytes 3145732
  8.2 10.4 %copy-start.2 = (f32[512,512]{1,0:T(8,128)S(1)}, f32[512,512]{1,0:T(8,128)}, u32[]{:S(2)}) copy-start(f32[512,512]{1,0:T(8,128)} %prev_ref.1) | copy-start | bytes 3145732
  8.2 10.4 %copy-start.4 = (s32[8,8]{1,0:T(8,128)S(1)}, s32[8,8]{1,0:T(8,128)}, u32[]{:S(2)}) copy-start(s32[8,8]{1,0:T(8,128)} %mask_ref.9) | copy-start | bytes 772
  8.2 17.1 %collective-permute-start.5 = (bf16[512,256]{1,0:T(8,128)(2,1)S(1)}, bf16[512,256]{1,0:T(8,128)(2,1)S(1)}, u32[]{:S(2)}, u32[]{:S(2)}) collective-permute-start(bf16[512,256]{1,0:T(8,128)(2,1)S(1)} %round_part.1.here_ref), channel_id=1, source_target_pairs={{12,0},{5,1},{0,4},{9,5},{4,8},{13,9},{8,12},{1,13},{14,2},{7,3},{... | collective-permute-start | bytes 786440 | tf_op jit(solution)/shard_map/ppermute | solution.py:28
  8.2 20.7 %collective-permute-start.4 = (bf16[512,256]{1,0:T(8,128)(2,1)S(1)}, bf16[512,256]{1,0:T(8,128)(2,1)S(1)}, u32[]{:S(2)}, u32[]{:S(2)}) collective-permute-start(bf16[512,256]{1,0:T(8,128)(2,1)S(1)} %round_part.1.here_ref), channel_id=1, source_target_pairs={{4,0},{13,1},{8,4},{1,5},{12,8},{5,9},{0,12},{9,13},{6,2},{15,3},{... | collective-permute-start | bytes 786440 | tf_op jit(solution)/shard_map/ppermute | solution.py:28
  19.7 16.9 %collective-permute-start.3 = (bf16[512,256]{1,0:T(8,128)(2,1)S(1)}, bf16[512,256]{1,0:T(8,128)(2,1)S(1)}, u32[]{:S(2)}, u32[]{:S(2)}) collective-permute-start(bf16[512,256]{1,0:T(8,128)(2,1)S(1)} %get-tuple-element.24.here_ref), channel_id=1, source_target_pairs={{12,0},{5,1},{0,4},{9,5},{4,8},{13,9},{8,12},{1,13},{14,2},{7,3},{... | collective-permute-start | bytes 786440 | tf_op jit(solution)/shard_map/ppermute | solution.py:28
  22.5 16.3 %collective-permute-start.2 = (bf16[512,256]{1,0:T(8,128)(2,1)S(1)}, bf16[512,256]{1,0:T(8,128)(2,1)S(1)}, u32[]{:S(2)}, u32[]{:S(2)}) collective-permute-start(bf16[512,256]{1,0:T(8,128)(2,1)S(1)} %get-tuple-element.24.here_ref), channel_id=1, source_target_pairs={{4,0},{13,1},{8,4},{1,5},{12,8},{5,9},{0,12},{9,13},{6,2},{15,3},{... | collective-permute-start | bytes 786440 | tf_op jit(solution)/shard_map/ppermute | solution.py:28
  28.9 9.9 %copy-start.1 = (f32[512,512]{1,0:T(8,128)S(1)}, f32[512,512]{1,0:T(8,128)}, u32[]{:S(2)}) copy-start(f32[512,512]{1,0:T(8,128)} %now_ref.2) | copy-start | bytes 3145732
  28.9 9.9 %copy-start.5 = (f32[2]{0:T(128)S(1)}, f32[2]{0:T(128)}, u32[]{:S(2)}) copy-start(f32[2]{0:T(128)} %coeffs_ref.5) | copy-start | bytes 28
  30.1 17.6 %collective-permute-start.7 = (bf16[512,256]{1,0:T(8,128)(2,1)S(1)}, bf16[512,256]{1,0:T(8,128)(2,1)S(1)}, u32[]{:S(2)}, u32[]{:S(2)}) collective-permute-start(bf16[512,256]{1,0:T(8,128)(2,1)S(1)} %get-tuple-element.30.here_ref), channel_id=1, source_target_pairs={{12,0},{13,1},{0,4},{1,5},{4,8},{5,9},{8,12},{9,13},{14,2},{15,3},... | collective-permute-start | bytes 786440 | tf_op jit(solution)/shard_map/ppermute | solution.py:28
  32.7 15.5 %collective-permute-start.8 = (bf16[512,128]{1,0:T(8,128)(2,1)S(1)}, bf16[512,128]{1,0:T(8,128)(2,1)S(1)}, u32[]{:S(2)}, u32[]{:S(2)}) collective-permute-start(bf16[512,128]{1,0:T(8,128)(2,1)S(1)} %get-tuple-element.32), channel_id=1, source_target_pairs={{4,0},{5,1},{8,4},{9,5},{12,8},{13,9},{0,12},{1,13},{6,2},{7,3},{1... | collective-permute-start | bytes 393224 | tf_op jit(solution)/shard_map/ppermute | solution.py:28
  34.2 16.3 %collective-permute-start.6 = (bf16[512,128]{1,0:T(8,128)(2,1)S(1)}, bf16[512,128]{1,0:T(8,128)(2,1)S(1)}, u32[]{:S(2)}, u32[]{:S(2)}) collective-permute-start(bf16[512,128]{1,0:T(8,128)(2,1)S(1)} %get-tuple-element.29), channel_id=1, source_target_pairs={{4,0},{5,1},{8,4},{9,5},{12,8},{13,9},{0,12},{1,13},{6,2},{7,3},{1... | collective-permute-start | bytes 393224 | tf_op jit(solution)/shard_map/ppermute | solution.py:28
